TPU v7x, 256 devices: a whole 4x4x8 slice. The times are simulated.
256 devices in a mesh: edp: 16 (over z_lo, x, core), ep: 16 (over z_hi, y).
Axes of the slice: x: 4, y: 4, z: 8 (z_hi: 4, z_lo: 2; z = z_hi * 2 + z_lo), core: 2. Of those that a mesh axis runs over, the one named last changes fastest.
Arguments:
- tokens: bfloat16 [32768, 5120], P(('edp', 'ep')), may hold values from -6 to 6
- cotangent: bfloat16 [32768, 5120], P(('edp', 'ep')), may hold values from -4 to 4
- gate_probs: bfloat16 [32768, 6], P(('edp', 'ep')), may hold values from 0.099609375 to 1
- expert_ids: int32 [32768, 6], P(('edp', 'ep')), may hold values from 0 to 159, all different within a row
- w_gate: bfloat16 [16, 1536, 5120], P('ep', 'edp'), may hold values from -0.078125 to 0.078125
- w_up: bfloat16 [16, 1536, 5120], P('ep', 'edp'), may hold values from -0.078125 to 0.078125
- w_down: bfloat16 [16, 1536, 5120], P('ep', 'edp'), may hold values from -0.15625 to 0.15625
Outputs:
- token_grad: bfloat16 [32768, 5120], P(('edp', 'ep'))
- gate_grad: bfloat16 [32768, 6], P(('edp', 'ep'))
- gate_wgrad: bfloat16 [16, 1536, 5120], P('ep', 'edp')
- up_wgrad: bfloat16 [16, 1536, 5120], P('ep', 'edp')
- down_wgrad: bfloat16 [16, 1536, 5120], P('ep', 'edp')
Inputs may be any that keep to these rules, and one draw needn't show every extreme that they name: `expert_ids`: each row holds 6 different ids, and every id appears in some row.
All inputs are finite; a program needn't handle non-finite values.
Results may differ from a plain program's by a relative error of at most 0.008.
Values may be sent and summed in bfloat16 or wider, within the bound.
No kernel may reach another device: no remote copies, remote signals or barrier semaphores. Data moves between devices by JAX's collectives and lax.ppermute only.
A program may use at most 128 MiB of HBM per device.

v0:
```python
import functools

import jax
import jax.numpy as jnp
from jax import lax
from jax.experimental import pallas as pl
from jax.experimental.pallas import tpu as pltpu
from jax.sharding import PartitionSpec as P

CAP = 3
QN = 8
LANES = 128
F32 = jnp.float32
BF16 = jnp.bfloat16


def x_perm(step):
    pairs = []
    for i in range(16):
        z, x, c = i >> 3, (i >> 1) & 3, i & 1
        pairs.append((i, z * 8 + ((x + step) % 4) * 2 + c))
    return pairs


X_UP = x_perm(1)
X_DOWN = x_perm(-1)
Z_SWAP = [(i, i ^ 8) for i in range(16)]
C_SWAP = [(i, i ^ 1) for i in range(16)]


def hop(a, perm):
    return lax.ppermute(a, "edp", perm)


def iota(shape, dim):
    return lax.broadcasted_iota(jnp.int32, shape, dim)


def dot(a, b):
    return jnp.dot(a, b, preferred_element_type=F32)


def dot_nt(a, b):
    return lax.dot_general(a, b, (((1,), (1,)), ((), ())), preferred_element_type=F32)


def call(kernel, outs, name, scratch=(), specs=None, out_specs=None, cost=None, limit=48):
    one = pl.BlockSpec(memory_space=pltpu.VMEM)
    params = pltpu.CompilerParams(vmem_limit_bytes=limit * 1024 * 1024)

    def run(*args):
        return pl.pallas_call(
            kernel,
            out_shape=outs,
            in_specs=[one] * len(args) if specs is None else specs,
            out_specs=jax.tree.map(lambda _: one, outs) if out_specs is None else out_specs,
            scratch_shapes=scratch,
            compiler_params=params,
            name=name,
            cost_estimate=cost
            and pl.CostEstimate(flops=cost[0], bytes_accessed=cost[1], transcendentals=0),
        )(*args)

    return run


def live_tables(ids_t):
    tokens = ids_t.shape[1]
    expert = iota((LANES, tokens), 0) >> 3
    hits = jnp.zeros((LANES, tokens), F32)
    for r in range(ids_t.shape[0]):
        hits = hits + jnp.where(ids_t[r : r + 1, :] == expert, 1.0, 0.0)
    earlier = jnp.where(iota((tokens, tokens), 0) < iota((tokens, tokens), 1), 1.0, 0.0)
    before = dot(hits.astype(BF16), earlier.astype(BF16))
    return [jnp.where(before == s, hits, 0.0) for s in range(CAP)]


def send_kernel(*refs, with_p):
    if with_p:
        ids_ref, probs_ref, tok_ref, out_ref = refs
    else:
        ids_ref, tok_ref, out_ref = refs
    ids_t = ids_ref[...]
    group = tok_ref.shape[1] // QN
    live = live_tables(ids_t)
    q = iota(live[0].shape, 0) & (QN - 1)
    for s in range(CAP):
        total = jnp.zeros((LANES, group), F32)
        for k in range(QN):
            pick = jnp.where(q == k, live[s], 0.0).astype(BF16)
            total = total + dot(pick, tok_ref[:, k * group : (k + 1) * group])
        out_ref[:, s * group : (s + 1) * group] = total.astype(BF16)
    if with_p:
        expert = iota(live[0].shape, 0) >> 3
        probs = jnp.zeros(live[0].shape, F32)
        for r in range(ids_t.shape[0]):
            probs = probs + jnp.where(
                ids_t[r : r + 1, :] == expert, probs_ref[r : r + 1, :].astype(F32), 0.0
            )
        lane = iota((LANES, LANES), 1)
        tail = jnp.zeros((LANES, LANES), F32)
        for s in range(CAP):
            col = jnp.sum(live[s] * probs, axis=1, keepdims=True)
            tail = tail + jnp.where(lane == s, col, 0.0)
        out_ref[:, CAP * group :] = tail.astype(BF16)


def unpack_kernel(in_ref, out_ref, *, group):
    row, col = iota((LANES, LANES), 0), iota((LANES, LANES), 1)
    swap = jnp.where((row & 15) * QN + (row >> 4) == col, 1.0, 0.0).astype(BF16)
    for s in range(CAP):
        got = dot(swap, in_ref[:, s * group : (s + 1) * group]).astype(BF16)
        for k in range(QN):
            out_ref[s * 16 : (s + 1) * 16, k * group : (k + 1) * group] = got[
                k * 16 : (k + 1) * 16, :
            ]
    if out_ref.shape[1] > QN * group:
        tail = dot(swap, in_ref[:, CAP * group :])
        for s in range(CAP):
            out_ref[s * 16 : (s + 1) * 16, QN * group :] = jnp.broadcast_to(
                tail[0:16, s : s + 1], (16, LANES)
            ).astype(BF16)


def fetch(copies):
    for c in copies:
        c.start()
    for c in copies:
        c.wait()


def pre_kernel(*refs, chunks):
    xs, (g, u, away) = refs[:chunks], refs[chunks : chunks + 3]
    out_ref, x_all, w_all, sems = refs[chunks + 3 :]
    rows, hid = xs[0].shape[0], g.shape[0]
    copies = [
        (xs[k], x_all.at[pl.ds(k * rows, rows)]) for k in range(chunks)
    ] + [
        (g, w_all.at[pl.ds(0, hid)]),
        (away.at[pl.ds(0, hid)], w_all.at[pl.ds(hid, hid)]),
        (u, w_all.at[pl.ds(2 * hid, hid)]),
        (away.at[pl.ds(hid, hid)], w_all.at[pl.ds(3 * hid, hid)]),
    ]
    fetch([pltpu.make_async_copy(a, b, sems.at[i]) for i, (a, b) in enumerate(copies)])
    out_ref[...] = jnp.zeros(out_ref.shape, F32)
    step = 640

    def body(n, carry):
        cols = pl.ds(pl.multiple_of(n * step, step), step)
        out_ref[...] += dot_nt(w_all[:, cols], x_all[:, cols])
        return carry

    lax.fori_loop(0, x_all.shape[1] // step, body, 0)


def main_kernel(*refs, chunks):
    ys, (g, u, d, away, pre_ref) = refs[:chunks], refs[chunks : chunks + 5]
    outs = refs[chunks + 5 : 2 * chunks + 5]
    mine_ref, away_ref, hid_ref, y_all, w_all, d_all, acc, sems = refs[2 * chunks + 5 :]
    rows, hid = ys[0].shape[0], g.shape[0]
    width = g.shape[1]
    total = rows * chunks
    copies = [
        (d, d_all.at[pl.ds(0, hid)]),
        (away.at[pl.ds(2 * hid, hid)], d_all.at[pl.ds(hid, hid)]),
    ] + [
        (ys[k], y_all.at[pl.ds(k * rows, rows)]) for k in range(chunks)
    ]
    late = [
        (g, w_all.at[pl.ds(0, hid)]),
        (away.at[pl.ds(0, hid)], w_all.at[pl.ds(hid, hid)]),
        (u, w_all.at[pl.ds(2 * hid, hid)]),
        (away.at[pl.ds(hid, hid)], w_all.at[pl.ds(3 * hid, hid)]),
    ]
    started = [
        pltpu.make_async_copy(a, b, sems.at[i]) for i, (a, b) in enumerate(copies + late)
    ]
    for c in started:
        c.start()
    for c in started[: len(copies)]:
        c.wait()
    acc[...] = jnp.zeros(acc.shape, F32)
    step = 640

    def body(n, carry):
        cols = pl.ds(pl.multiple_of(n * step, step), step)
        acc[...] += dot_nt(d_all[:, cols], y_all[:, cols])
        return carry

    lax.fori_loop(0, width // step, body, 0)
    back = acc[...]
    prob = jnp.transpose(y_all[:, width:].astype(F32))[0:1, :]
    gate, up = pre_ref[0 : 2 * hid, :], pre_ref[2 * hid :, :]
    sig = jax.nn.sigmoid(gate)
    hidden = gate * sig * up
    part = jnp.sum(hidden * back, axis=0, keepdims=True)
    scaled = prob * back
    d_gate = scaled * up * sig * (1.0 + gate * (1.0 - sig))
    d_up = scaled * gate * sig
    hid_ref[...] = hidden.astype(BF16)
    d_gate_h, d_up_h = d_gate.astype(BF16), d_up.astype(BF16)
    mine_ref[0:hid, :] = d_gate_h[0:hid, :]
    mine_ref[hid:, :] = d_up_h[0:hid, :]
    away_ref[0:hid, :] = d_gate_h[hid:, :]
    away_ref[hid:, :] = d_up_h[hid:, :]
    both = jnp.concatenate([jnp.transpose(d_gate), jnp.transpose(d_up)], axis=1).astype(BF16)
    high = part.astype(BF16).astype(F32)
    low = part - high
    tail = jnp.where(
        iota((LANES, total), 0) < LANES // 2,
        jnp.broadcast_to(high, (LANES, total)),
        jnp.broadcast_to(low, (LANES, total)),
    )
    tail = jnp.transpose(tail).astype(BF16)
    for k in range(chunks):
        outs[k][:, width:] = tail[k * rows : (k + 1) * rows, :]
    for c in started[len(copies) :]:
        c.wait()

    def body2(n, carry):
        cols = pl.ds(pl.multiple_of(n * step, step), step)
        got = dot(both, w_all[:, cols]).astype(BF16)
        for k in range(chunks):
            outs[k][:, cols] = got[k * rows : (k + 1) * rows, :]
        return carry

    lax.fori_loop(0, width // step, body2, 0)


def summed(refs):
    total = refs[0][...].astype(F32)
    for r in refs[1:]:
        total = total + r[...].astype(F32)
    return total


def join_kernel(*refs, width):
    *parts, out_ref = refs
    body = [p.at[:, pl.ds(0, width)] for p in parts]
    out_ref[:, 0:width] = summed(body).astype(BF16)
    tail = summed([p.at[:, pl.ds(width, LANES)] for p in parts])
    value = tail[:, 0:1] + tail[:, LANES // 2 : LANES // 2 + 1]
    high = value.astype(BF16).astype(F32)
    out_ref[:, width:] = jnp.where(
        iota(tail.shape, 1) < LANES // 2, high, value - high
    ).astype(BF16)


def last_kernel(*refs, group):
    *parts, out_ref = refs
    width = QN * group
    row, col = iota((LANES, LANES), 0), iota((LANES, LANES), 1)
    swap = jnp.where((col & 15) * QN + (col >> 4) == row, 1.0, 0.0).astype(BF16)
    total = summed([p.at[:, pl.ds(0, width)] for p in parts]).astype(BF16)
    for s in range(CAP):
        stack = jnp.concatenate(
            [total[s * 16 : (s + 1) * 16, k * group : (k + 1) * group] for k in range(QN)], axis=0
        )
        out_ref[:, s * group : (s + 1) * group] = dot(swap, stack).astype(BF16)
    tail = summed([p.at[:, pl.ds(width, LANES)] for p in parts])
    value = tail[:, 0:1] + tail[:, LANES // 2 : LANES // 2 + 1]
    lane = iota((16, LANES), 1)
    cols = jnp.zeros((16, LANES), F32)
    for s in range(CAP):
        cols = cols + jnp.where(lane == s, value[s * 16 : (s + 1) * 16, :], 0.0)
    stack = jnp.concatenate([cols] * QN, axis=0).astype(BF16)
    out_ref[:, CAP * group :] = dot(swap, stack).astype(BF16)


def wgrad_kernel(*refs, chunks, came):
    xs, ys = refs[:chunks], refs[chunks : 2 * chunks]
    rest = refs[2 * chunks :]
    if came:
        left_ref, hid_ref, came_ref, g_out, u_out, d_out, x_all, y_all, sems = rest
    else:
        left_ref, hid_ref, out_ref, x_all, y_all, sems = rest
    rows, width = xs[0].shape
    hid = left_ref.shape[0] // 2
    copies = [(xs[k], x_all.at[pl.ds(k * rows, rows)]) for k in range(chunks)]
    copies += [(ys[k], y_all.at[pl.ds(k * rows, rows)]) for k in range(chunks)]
    fetch([pltpu.make_async_copy(a, b, sems.at[i]) for i, (a, b) in enumerate(copies)])
    prob = y_all[:, width : width + 1].astype(F32)
    step = 640

    def body(n, carry):
        cols = pl.ds(pl.multiple_of(n * step, step), step)
        both = dot(left_ref[...], x_all[:, cols])
        scaled = (prob * y_all[:, cols].astype(F32)).astype(BF16)
        if came:
            down = dot(hid_ref[0:hid, :], scaled)
            g_out[:, cols] = (both[0:hid] + came_ref[0:hid, cols].astype(F32)).astype(BF16)
            u_out[:, cols] = (
                both[hid:] + came_ref[hid : 2 * hid, cols].astype(F32)
            ).astype(BF16)
            d_out[:, cols] = (down + came_ref[2 * hid :, cols].astype(F32)).astype(BF16)
        else:
            down = dot(hid_ref[hid:, :], scaled)
            out_ref[0 : 2 * hid, cols] = both.astype(BF16)
            out_ref[2 * hid :, cols] = down.astype(BF16)
        return carry

    lax.fori_loop(0, width // step, body, 0)


def final_kernel(ids_ref, in_ref, tok_ref, gate_ref, *, group):
    ids_t = ids_ref[...]
    live = live_tables(ids_t)
    lane = iota(live[0].shape, 1)
    sides = [jnp.transpose(v) for v in live]
    for k in range(QN):
        total = jnp.zeros((live[0].shape[1], group), F32)
        for s in range(CAP):
            pick = jnp.where((lane & (QN - 1)) == k, sides[s], 0.0).astype(BF16)
            total = total + dot(pick, in_ref[:, s * group : (s + 1) * group])
        tok_ref[:, k * group : (k + 1) * group] = total.astype(BF16)
    row = iota(live[0].shape, 0)
    value = jnp.zeros(live[0].shape, F32)
    for s in range(CAP):
        col = in_ref[:, CAP * group + s : CAP * group + s + 1].astype(F32)
        value = value + live[s] * col
    value = jnp.where((row & (QN - 1)) == 0, value, 0.0)
    for r in range(ids_t.shape[0]):
        mine = jnp.where(ids_t[r : r + 1, :] == (row >> 3), value, 0.0)
        gate_ref[r : r + 1, :] = jnp.sum(mine, axis=0, keepdims=True).astype(BF16)


def first_hops(a):
    return hop(a, Z_SWAP), hop(a, X_UP), hop(a, X_DOWN)


def gather_chips(a, other, left, right):
    o_left = hop(other, X_UP)
    o_right = hop(other, X_DOWN)
    far = hop(left, X_UP)
    o_far = hop(o_right, X_DOWN)
    return [a, left, far, right, other, o_left, o_far, o_right]


def per_device(tokens, cotangent, gate_probs, expert_ids, w_gate, w_up, w_down):
    width = tokens.shape[1]
    group = width // QN
    wide = width + LANES
    rows = CAP * 16
    total = 8 * rows
    g, u, d = w_gate[0], w_up[0], w_down[0]
    hid = g.shape[0]
    ids_t, probs_t = expert_ids.T, gate_probs.T
    shape = jax.ShapeDtypeStruct
    any_spec, vmem = pl.BlockSpec(memory_space=pl.ANY), pl.BlockSpec(memory_space=pltpu.VMEM)
    dma = pltpu.SemaphoreType.DMA

    def exchange(a):
        a = a.reshape(16, QN, a.shape[1])
        a = lax.all_to_all(a, "ep", split_axis=0, concat_axis=0, tiled=True)
        return a.reshape(LANES, a.shape[2])

    away_w = hop(jnp.concatenate([g, u, d], axis=0), C_SWAP)
    send_x = call(
        functools.partial(send_kernel, with_p=False),
        shape((LANES, CAP * group), BF16),
        "send_x",
        cost=(6 * 10**8, 2 * 10**6),
    )(ids_t, tokens)
    send_y = call(
        functools.partial(send_kernel, with_p=True),
        shape((LANES, CAP * group + LANES), BF16),
        "send_y",
        cost=(6 * 10**8, 2 * 10**6),
    )(ids_t, probs_t, cotangent)
    got_x = exchange(send_x)
    send_y, away_w, got_x = lax.optimization_barrier((send_y, away_w, got_x))
    x = call(
        functools.partial(unpack_kernel, group=group),
        shape((rows, width), BF16),
        "unpack_x",
        cost=(10**8, 10**6),
    )(got_x)
    first_x = first_hops(x)
    got_y, *first_x = lax.optimization_barrier((exchange(send_y), *first_x))
    xs = gather_chips(x, *first_x)
    y = call(
        functools.partial(unpack_kernel, group=group),
        shape((rows, wide), BF16),
        "unpack_y",
        cost=(10**8, 10**6),
    )(got_y)
    ys = gather_chips(y, *first_hops(y))
    pre = call(
        functools.partial(pre_kernel, chunks=8),
        shape((4 * hid, total), F32),
        "pre",
        scratch=[
            pltpu.VMEM((total, width), BF16),
            pltpu.VMEM((4 * hid, width), BF16),
            dma((12,)),
        ],
        specs=[any_spec] * 11,
        cost=(2 * total * width * 4 * hid, 8 * 10**6),
    )(*xs, g, u, away_w)
    *parts, mine, away, hidden = call(
        functools.partial(main_kernel, chunks=8),
        [shape((rows, wide), BF16)] * 8
        + [shape((2 * hid, total), BF16), shape((2 * hid, total), BF16), shape((2 * hid, total), BF16)],
        "main",
        scratch=[
            pltpu.VMEM((total, wide), BF16),
            pltpu.VMEM((4 * hid, width), BF16),
            pltpu.VMEM((2 * hid, width), BF16),
            pltpu.VMEM((2 * hid, total), F32),
            dma((14,)),
        ],
        specs=[any_spec] * 12 + [vmem],
        cost=(3 * total * width * 4 * hid, 14 * 10**6),
    )(*ys, g, u, d, away_w, pre)

    def join(*a):
        return call(
            functools.partial(join_kernel, width=width),
            shape((rows, wide), BF16),
            "join",
            cost=(10**6, 10**6),
        )(*a)

    own, left, far, right, other, o_left, o_far, o_right = parts
    of, ol = hop(o_far, X_UP), hop(o_left, X_DOWN)
    of, ol, far, away = lax.optimization_barrier((of, ol, far, away))
    o_r, f = hop(join(o_right, of), X_UP), hop(far, X_DOWN)
    scratch = [
        pltpu.VMEM((total, width), BF16),
        pltpu.VMEM((total, wide), BF16),
        dma((16,)),
    ]
    sent = call(
        functools.partial(wgrad_kernel, chunks=8, came=False),
        shape((3 * hid, width), BF16),
        "wgrad_away",
        scratch=scratch,
        specs=[any_spec] * 16 + [vmem] * 2,
        cost=(2 * total * width * 3 * hid, 12 * 10**6),
    )(*xs, *ys, away, hidden)
    o_r, f, sent, right = lax.optimization_barrier((o_r, f, sent, right))
    came = hop(sent, C_SWAP)
    oz = hop(join(other, ol, o_r), Z_SWAP)
    lf, r = hop(join(left, f), X_DOWN), hop(right, X_UP)
    last = call(
        functools.partial(last_kernel, group=group),
        shape((LANES, CAP * group + LANES), BF16),
        "last",
        cost=(10**8, 3 * 10**6),
    )(own, r, lf, oz)
    last, mine = lax.optimization_barrier((last, mine))
    back = exchange(last)
    g_grad, u_grad, d_grad = call(
        functools.partial(wgrad_kernel, chunks=8, came=True),
        [shape((hid, width), BF16)] * 3,
        "wgrad_mine",
        scratch=scratch,
        specs=[any_spec] * 16 + [vmem] * 3,
        cost=(2 * total * width * 3 * hid, 15 * 10**6),
    )(*xs, *ys, mine, hidden, came)
    back, g_grad, u_grad, d_grad = lax.optimization_barrier((back, g_grad, u_grad, d_grad))
    token_grad, gate_t = call(
        functools.partial(final_kernel, group=group),
        [shape(tokens.shape, BF16), shape(ids_t.shape, BF16)],
        "final",
        cost=(6 * 10**8, 2 * 10**6),
    )(ids_t, back)
    return (token_grad, gate_t.T, g_grad[None], u_grad[None], d_grad[None])


def solution(mesh):
    tok = P(("edp", "ep"), None)
    wgt = P("ep", "edp", None)
    return jax.shard_map(
        per_device,
        mesh=mesh,
        in_specs=(tok, tok, tok, tok, wgt, wgt, wgt),
        out_specs=(tok, tok, wgt, wgt, wgt),
        check_vma=False,
    )
```

profile of v0, /device:TPU:32, one launch (start us, length us, event | category | flops | bytes accessed | tf_op | source)
XLA Modules:
  0.0 211.1 jit_solution(18194452645442096556)
XLA Ops:
  0.7 3.7 %pad_maximum_fusion = bf16[288,5120]{1,0:T(8,128)(2,1)} fusion(bf16[96,5120]{1,0:T(8,128)(2,1)} %bitcast.29, bf16[96,5120]{1,0:T(8,128)(2,1)} %bitcast.26, bf16[96,5120]{1,0:T(8,128)(2,1)} %bitcast.15), kind=kLoop, calls=%fused_computation | loop fusion | flops 8847360 | bytes 5898240 | tf_op jit(solution)/shard_map/concatenate | solution.py:357
  4.4 2.1 send_x.1
  6.5 10.4 %all-to-all-start = ((bf16[16,8,1920]{2,1,0:T(8,128)(2,1)}), bf16[16,8,1920]{2,1,0:T(8,128)(2,1)S(1)}, u32[]{:S(2)}, u32[]{:S(2)}) async-start(bf16[16,8,1920]{2,1,0:T(8,128)(2,1)} %bitcast.5), calls=%async_computation | async-start | bytes 983040 | tf_op jit(solution)/shard_map/all_to_all | solution.py:354
  16.9 1.3 copy-done.22
  18.2 1.3 send_y.1
  19.6 0.8 copy-done.18
  20.4 14.4 %all-to-all-done = bf16[16,8,1920]{2,1,0:T(8,128)(2,1)S(1)} async-done(((bf16[16,8,1920]{2,1,0:T(8,128)(2,1)}), bf16[16,8,1920]{2,1,0:T(8,128)(2,1)S(1)}, u32[]{:S(2)}, u32[]{:S(2)}) %all-to-all-start) | async-done | bytes 491552 | tf_op jit(solution)/shard_map/all_to_all | solution.py:354
  34.7 3.7 %all-to-all-start.1 = ((bf16[16,8,2048]{2,1,0:T(8,128)(2,1)}), bf16[16,8,2048]{2,1,0:T(8,128)(2,1)S(1)}, u32[]{:S(2)}, u32[]{:S(2)}) async-start(bf16[16,8,2048]{2,1,0:T(8,128)(2,1)} %bitcast.21), calls=%async_computation.1 | async-start | bytes 1048576 | tf_op jit(solution)/shard_map/all_to_all | solution.py:354
  38.7 2.9 %collective-permute-start.3 = (bf16[48,5120]{1,0:T(8,128)(2,1)S(1)}, bf16[48,5120]{1,0:T(8,128)(2,1)S(1)}, u32[]{:S(2)}, u32[]{:S(2)}) collective-permute-start(bf16[48,5120]{1,0:T(8,128)(2,1)S(1)} %unpack_x.1.refs_0_), channel_id=1, source_target_pairs={{0,96},{16,112},{32,0},{48,16},{64,32},{80,48},{96,64},{112,80},{1... | collective-permute-start | bytes 1474568 | tf_op jit(solution)/shard_map/ppermute | solution.py:32
  41.6 1.7 collective-permute-start.1
  43.4 8.4 %collective-permute-done.3.refs_3_ = bf16[48,5120]{1,0:T(8,128)(2,1)S(1)} collective-permute-done((bf16[48,5120]{1,0:T(8,128)(2,1)S(1)}, bf16[48,5120]{1,0:T(8,128)(2,1)S(1)}, u32[]{:S(2)}, u32[]{:S(2)}) %collective-permute-start.3) | collective-permute-done | bytes 491552 | tf_op jit(solution)/shard_map/ppermute | solution.py:32
  51.8 3.4 %collective-permute-done.2.refs_1_ = bf16[48,5120]{1,0:T(8,128)(2,1)S(1)} collective-permute-done((bf16[48,5120]{1,0:T(8,128)(2,1)S(1)}, bf16[48,5120]{1,0:T(8,128)(2,1)S(1)}, u32[]{:S(2)}, u32[]{:S(2)}) %collective-permute-start.2) | collective-permute-done | bytes 491552 | tf_op jit(solution)/shard_map/ppermute | solution.py:32
  55.2 7.2 %collective-permute-done.1.refs_4_ = bf16[48,5120]{1,0:T(8,128)(2,1)} collective-permute-done((bf16[48,5120]{1,0:T(8,128)(2,1)S(1)}, bf16[48,5120]{1,0:T(8,128)(2,1)}, u32[]{:S(2)}, u32[]{:S(2)}) %collective-permute-start.1) | collective-permute-done | bytes 491552 | tf_op jit(solution)/shard_map/ppermute | solution.py:32
  62.4 0.8 copy-done.14
  63.2 1.0 copy-done.15
  65.1 2.8 %collective-permute-start.13 = (bf16[48,5120]{1,0:T(8,128)(2,1)}, bf16[48,5120]{1,0:T(8,128)(2,1)S(1)}, u32[]{:S(2)}, u32[]{:S(2)}) collective-permute-start(bf16[48,5120]{1,0:T(8,128)(2,1)} %collective-permute-done.1.refs_4_), channel_id=1, source_target_pairs={{0,96},{16,112},{32,0},{48,16},{64,32},{80,48},{96,64},{112,80},{1... | collective-permute-start | bytes 1474568 | tf_op jit(solution)/shard_map/ppermute | solution.py:32
  67.9 8.7 %collective-permute-done.7.refs_4_.refs_12_ = bf16[48,5248]{1,0:T(8,128)(2,1)S(1)} collective-permute-done((bf16[48,5248]{1,0:T(8,128)(2,1)S(1)}, bf16[48,5248]{1,0:T(8,128)(2,1)S(1)}, u32[]{:S(2)}, u32[]{:S(2)}) %collective-permute-start.7) | collective-permute-done | bytes 503840 | tf_op jit(solution)/shard_map/ppermute | solution.py:32
  76.6 2.8 %collective-permute-start.9 = (bf16[48,5248]{1,0:T(8,128)(2,1)S(1)}, bf16[48,5248]{1,0:T(8,128)(2,1)S(1)}, u32[]{:S(2)}, u32[]{:S(2)}) collective-permute-start(bf16[48,5248]{1,0:T(8,128)(2,1)S(1)} %collective-permute-done.7.refs_4_.refs_12_), channel_id=1, source_target_pairs={{0,96},{16,112},{32,0},{48,16},{64,32},{80,48},{96,64},{112,80},{1... | collective-permute-start | bytes 1511432 | tf_op jit(solution)/shard_map/ppermute | solution.py:32
  79.4 0.8 collective-permute-start.12
  80.1 2.6 %collective-permute-start.14 = (bf16[48,5120]{1,0:T(8,128)(2,1)S(1)}, bf16[48,5120]{1,0:T(8,128)(2,1)S(1)}, u32[]{:S(2)}, u32[]{:S(2)}) collective-permute-start(bf16[48,5120]{1,0:T(8,128)(2,1)S(1)} %collective-permute-done.13.refs_7_), channel_id=1, source_target_pairs={{0,96},{16,112},{32,0},{48,16},{64,32},{80,48},{96,64},{112,80},{1... | collective-permute-start | bytes 1474568 | tf_op jit(solution)/shard_map/ppermute | solution.py:32
  82.7 12.0 %collective-permute-done.11.refs_2_ = bf16[48,5120]{1,0:T(8,128)(2,1)S(1)} collective-permute-done((bf16[48,5120]{1,0:T(8,128)(2,1)S(1)}, bf16[48,5120]{1,0:T(8,128)(2,1)S(1)}, u32[]{:S(2)}, u32[]{:S(2)}) %collective-permute-start.11) | collective-permute-done | bytes 491552 | tf_op jit(solution)/shard_map/ppermute | solution.py:32
  94.8 7.2 %collective-permute-done.12.refs_5_ = bf16[48,5120]{1,0:T(8,128)(2,1)S(1)} collective-permute-done((bf16[48,5120]{1,0:T(8,128)(2,1)}, bf16[48,5120]{1,0:T(8,128)(2,1)S(1)}, u32[]{:S(2)}, u32[]{:S(2)}) %collective-permute-start.12) | collective-permute-done | bytes 491552 | tf_op jit(solution)/shard_map/ppermute | solution.py:32
  102.1 3.2 %collective-permute-start.10 = (bf16[48,5248]{1,0:T(8,128)(2,1)S(1)}, bf16[48,5248]{1,0:T(8,128)(2,1)S(1)}, u32[]{:S(2)}, u32[]{:S(2)}) collective-permute-start(bf16[48,5248]{1,0:T(8,128)(2,1)S(1)} %collective-permute-done.9.refs_7_.refs_15_), channel_id=1, source_target_pairs={{0,96},{16,112},{32,0},{48,16},{64,32},{80,48},{96,64},{112,80},{1... | collective-permute-start | bytes 1511432 | tf_op jit(solution)/shard_map/ppermute | solution.py:32
  105.3 1.0 copy-done.2
  106.3 8.1 %pre.1.refs_12_ = f32[384,384]{1,0:T(8,128)S(1)} custom-call(bf16[48,5120]{1,0:T(8,128)(2,1)S(1)} %unpack_x.1.refs_0_, bf16[48,5120]{1,0:T(8,128)(2,1)S(1)} %copy-done.2, bf16[48,5120]{1,0:T(8,128)(2,1)S(1)} %collective-permute-done.11.refs_2_, bf16[48,5120]{1,0:T(8,128)(2,1)S(1)} %collective-permute-done.3.refs_3_, ...), custom_call_target="tpu_custom_call" | custom-call | flops 1509949440 | bytes 8000000 | tf_op jit(solution)/shard_map/pre/pallas_call | solution.py:52
  114.4 0.8 copy-done.12
  115.2 2.3 %collective-permute-done.8.refs_5_.refs_13_ = bf16[48,5248]{1,0:T(8,128)(2,1)S(1)} collective-permute-done((bf16[48,5248]{1,0:T(8,128)(2,1)S(1)}, bf16[48,5248]{1,0:T(8,128)(2,1)S(1)}, u32[]{:S(2)}, u32[]{:S(2)}) %collective-permute-start.8) | collective-permute-done | bytes 503840 | tf_op jit(solution)/shard_map/ppermute | solution.py:32
  117.6 6.5 %collective-permute-done.5.refs_2_.refs_10_ = bf16[48,5248]{1,0:T(8,128)(2,1)S(1)} collective-permute-done((bf16[48,5248]{1,0:T(8,128)(2,1)S(1)}, bf16[48,5248]{1,0:T(8,128)(2,1)S(1)}, u32[]{:S(2)}, u32[]{:S(2)}) %collective-permute-start.5) | collective-permute-done | bytes 503840 | tf_op jit(solution)/shard_map/ppermute | solution.py:32
  124.1 0.8 copy-done.29
  124.9 10.6 %main.1 = (bf16[48,5248]{1,0:T(8,128)(2,1)S(1)}, bf16[48,5248]{1,0:T(8,128)(2,1)S(1)}, bf16[48,5248]{1,0:T(8,128)(2,1)S(1)}, bf16[48,5248]{1,0:T(8,128)(2,1)S(1)...) custom-call(bf16[48,5248]{1,0:T(8,128)(2,1)S(1)} %unpack_y.1.refs_0_, ...), custom_call_target="tpu_custom_call" | custom-call | flops 2264924160 | bytes 14000000 | tf_op jit(solution)/shard_map/main/pallas_call | solution.py:52
  135.6 3.2 %collective-permute-start.16 = (bf16[48,5248]{1,0:T(8,128)(2,1)S(1)}, bf16[48,5248]{1,0:T(8,128)(2,1)S(1)}, u32[]{:S(2)}, u32[]{:S(2)}) collective-permute-start(bf16[48,5248]{1,0:T(8,128)(2,1)S(1)} %get-tuple-element.52), channel_id=1, source_target_pairs={{0,96},{16,112},{32,0},{48,16},{64,32},{80,48},{96,64},{112,80},{1... | collective-permute-start | bytes 1511432 | tf_op jit(solution)/shard_map/ppermute | solution.py:32
  138.8 8.1 %collective-permute-done.15.refs_1_ = bf16[48,5248]{1,0:T(8,128)(2,1)S(1)} collective-permute-done((bf16[48,5248]{1,0:T(8,128)(2,1)S(1)}, bf16[48,5248]{1,0:T(8,128)(2,1)S(1)}, u32[]{:S(2)}, u32[]{:S(2)}) %collective-permute-start.15) | collective-permute-done | bytes 503840 | tf_op jit(solution)/shard_map/ppermute | solution.py:32
  147.3 3.2 %collective-permute-start.18 = (bf16[48,5248]{1,0:T(8,128)(2,1)S(1)}, bf16[48,5248]{1,0:T(8,128)(2,1)S(1)}, u32[]{:S(2)}, u32[]{:S(2)}) collective-permute-start(bf16[48,5248]{1,0:T(8,128)(2,1)S(1)} %get-tuple-element.56), channel_id=1, source_target_pairs={{0,96},{16,112},{32,0},{48,16},{64,32},{80,48},{96,64},{112,80},{1... | collective-permute-start | bytes 1511432 | tf_op jit(solution)/shard_map/ppermute | solution.py:32
  150.5 10.2 %wgrad_away.1 = bf16[288,5120]{1,0:T(8,128)(2,1)} custom-call(bf16[48,5120]{1,0:T(8,128)(2,1)S(1)} %unpack_x.1.refs_0_, bf16[48,5120]{1,0:T(8,128)(2,1)S(1)} %copy-done.3, bf16[48,5120]{1,0:T(8,128)(2,1)S(1)} %collective-permute-done.11.refs_2_, bf16[48,5120]{1,0:T(8,128)(2,1)S(1)} %collective-permute-done.3.refs_3_, ...), custom_call_target="tpu_custom_call" | custom-call | flops 1132462080 | bytes 12000000 | tf_op jit(solution)/shard_map/wgrad_away/pallas_call | solution.py:52
  161.2 1.8 collective-permute-start.20
  163.7 1.6 collective-permute-start.21
  165.4 9.8 %collective-permute-done.20.refs_2_ = bf16[48,5248]{1,0:T(8,128)(2,1)S(1)} collective-permute-done((bf16[48,5248]{1,0:T(8,128)(2,1)S(1)}, bf16[48,5248]{1,0:T(8,128)(2,1)S(1)}, u32[]{:S(2)}, u32[]{:S(2)}) %collective-permute-start.20) | collective-permute-done | bytes 503840 | tf_op jit(solution)/shard_map/ppermute | solution.py:32
  175.1 2.7 %collective-permute-done.19.refs_1_ = bf16[48,5248]{1,0:T(8,128)(2,1)S(1)} collective-permute-done((bf16[48,5248]{1,0:T(8,128)(2,1)S(1)}, bf16[48,5248]{1,0:T(8,128)(2,1)S(1)}, u32[]{:S(2)}, u32[]{:S(2)}) %collective-permute-start.19) | collective-permute-done | bytes 503840 | tf_op jit(solution)/shard_map/ppermute | solution.py:32
  178.3 0.8 copy-done.13
  179.1 10.8 %all-to-all-start.2 = ((bf16[16,8,2048]{2,1,0:T(8,128)(2,1)}), bf16[16,8,2048]{2,1,0:T(8,128)(2,1)}, u32[]{:S(2)}, u32[]{:S(2)}) async-start(bf16[16,8,2048]{2,1,0:T(8,128)(2,1)} %bitcast.18), calls=%async_computation.2 | async-start | bytes 1048576 | tf_op jit(solution)/shard_map/all_to_all | solution.py:354
  189.9 1.0 copy-done.7
  190.9 1.0 copy-done.9
  192.0 1.0 copy-done.11
  193.0 0.9 copy-done.17
  193.9 0.9 copy-done.20
  194.8 12.0 %wgrad_mine.1 = (bf16[96,5120]{1,0:T(8,128)(2,1)}, bf16[96,5120]{1,0:T(8,128)(2,1)}, bf16[96,5120]{1,0:T(8,128)(2,1)}) custom-call(bf16[48,5120]{1,0:T(8,128)(2,1)S(1)} %unpack_x.1.refs_0_, bf16[48,5120]{1,0:T(8,128)(2,1)S(1)} %copy-done.3, bf16[48,5120]{1,0:T(8,128)(2,1)S(1)} %copy-done.7, bf16[48,5120]{1,0:T(8,128)(2,1)S(1)} %collective-permute-done.3.refs_3_, ...), custom_call_target="tpu_custom_call" | custom-call | flops 1132462080 | bytes 15000000 | tf_op jit(solution)/shard_map/wgrad_mine/pallas_call | solution.py:52
  206.8 0.8 all-to-all-done.2
  207.7 3.5 %final.1 = (bf16[128,5120]{1,0:T(8,128)(2,1)}, bf16[6,128]{1,0:T(8,128)(2,1)}) custom-call(s32[6,128]{1,0:T(8,128)S(1)} %bitcast.24, bf16[128,2048]{1,0:T(8,128)(2,1)} %bitcast.10.in_ref), custom_call_target="tpu_custom_call" | custom-call | flops 600000000 | bytes 2000000 | tf_op jit(solution)/shard_map/final/pallas_call | solution.py:52
  (78 shorter events, 3.4 us)
Async XLA Ops:
  0.6 3.7 %copy-start.21 = (bf16[128,5120]{1,0:T(8,128)(2,1)S(1)}, bf16[128,5120]{1,0:T(8,128)(2,1)}, u32[]{:S(2)}) copy-start(bf16[128,5120]{1,0:T(8,128)(2,1)} %refs_1_.1) | copy-start | bytes 3932164
  0.6 3.7 %copy-start.23 = (s32[128,6]{0,1:T(8,128)S(1)}, s32[128,6]{0,1:T(8,128)}, u32[]{:S(2)}) copy-start(s32[128,6]{0,1:T(8,128)} %param.10) | copy-start | bytes 9220
  4.4 12.5 %copy-start.24 = (bf16[128,6]{0,1:T(8,128)(2,1)S(1)}, bf16[128,6]{0,1:T(8,128)(2,1)}, u32[]{:S(2)}) copy-start(bf16[128,6]{0,1:T(8,128)(2,1)} %param.9) | copy-start | bytes 4612
  4.4 30.4 %collective-permute-start = (bf16[288,5120]{1,0:T(8,128)(2,1)}, bf16[288,5120]{1,0:T(8,128)(2,1)}, u32[]{:S(2)}, u32[]{:S(2)}) collective-permute-start(bf16[288,5120]{1,0:T(8,128)(2,1)} %pad_maximum_fusion), channel_id=1, source_target_pairs={{0,16},{16,0},{32,48},{48,32},{64,80},{80,64},{96,112},{112,96},{1... | collective-permute-start | bytes 8847368 | tf_op jit(solution)/shard_map/ppermute | solution.py:32
  6.5 98.8 %copy-start = (bf16[1,96,5120]{2,1,0:T(8,128)(2,1)S(1)}, bf16[1,96,5120]{2,1,0:T(8,128)(2,1)}, u32[]{:S(2)}) copy-start(bf16[1,96,5120]{2,1,0:T(8,128)(2,1)} %param.11) | copy-start | bytes 2949124
  6.5 28.3 %all-to-all-start = ((bf16[16,8,1920]{2,1,0:T(8,128)(2,1)}), bf16[16,8,1920]{2,1,0:T(8,128)(2,1)S(1)}, u32[]{:S(2)}, u32[]{:S(2)}) async-start(bf16[16,8,1920]{2,1,0:T(8,128)(2,1)} %bitcast.5), calls=%async_computation | async-start | bytes 983040 | tf_op jit(solution)/shard_map/all_to_all | solution.py:354
  16.9 1.3 copy-start.22
  34.7 27.6 %all-to-all-start.1 = ((bf16[16,8,2048]{2,1,0:T(8,128)(2,1)}), bf16[16,8,2048]{2,1,0:T(8,128)(2,1)S(1)}, u32[]{:S(2)}, u32[]{:S(2)}) async-start(bf16[16,8,2048]{2,1,0:T(8,128)(2,1)} %bitcast.21), calls=%async_computation.1 | async-start | bytes 1048576 | tf_op jit(solution)/shard_map/all_to_all | solution.py:354
  38.7 13.0 %collective-permute-start.3 = (bf16[48,5120]{1,0:T(8,128)(2,1)S(1)}, bf16[48,5120]{1,0:T(8,128)(2,1)S(1)}, u32[]{:S(2)}, u32[]{:S(2)}) collective-permute-start(bf16[48,5120]{1,0:T(8,128)(2,1)S(1)} %unpack_x.1.refs_0_), channel_id=1, source_target_pairs={{0,96},{16,112},{32,0},{48,16},{64,32},{80,48},{96,64},{112,80},{1... | collective-permute-start | bytes 1474568 | tf_op jit(solution)/shard_map/ppermute | solution.py:32
  41.6 13.6 %collective-permute-start.2 = (bf16[48,5120]{1,0:T(8,128)(2,1)S(1)}, bf16[48,5120]{1,0:T(8,128)(2,1)S(1)}, u32[]{:S(2)}, u32[]{:S(2)}) collective-permute-start(bf16[48,5120]{1,0:T(8,128)(2,1)S(1)} %unpack_x.1.refs_0_), channel_id=1, source_target_pairs={{0,32},{16,48},{32,64},{48,80},{64,96},{80,112},{96,0},{112,16},{1... | collective-permute-start | bytes 1474568 | tf_op jit(solution)/shard_map/ppermute | solution.py:32
  41.6 20.7 %collective-permute-start.1 = (bf16[48,5120]{1,0:T(8,128)(2,1)S(1)}, bf16[48,5120]{1,0:T(8,128)(2,1)}, u32[]{:S(2)}, u32[]{:S(2)}) collective-permute-start(bf16[48,5120]{1,0:T(8,128)(2,1)S(1)} %unpack_x.1.refs_0_), channel_id=1, source_target_pairs={{0,128},{16,144},{32,160},{48,176},{64,192},{80,208},{96,224},{112... | collective-permute-start | bytes 1474568 | tf_op jit(solution)/shard_map/ppermute | solution.py:32
  55.2 46.7 %copy-start.1 = (bf16[48,5120]{1,0:T(8,128)(2,1)}, bf16[48,5120]{1,0:T(8,128)(2,1)S(1)}, u32[]{:S(2)}) copy-start(bf16[48,5120]{1,0:T(8,128)(2,1)S(1)} %collective-permute-done.2.refs_1_) | copy-start | bytes 1474564
  63.2 1.0 copy-start.15
  64.5 12.1 %collective-permute-start.7 = (bf16[48,5248]{1,0:T(8,128)(2,1)S(1)}, bf16[48,5248]{1,0:T(8,128)(2,1)S(1)}, u32[]{:S(2)}, u32[]{:S(2)}) collective-permute-start(bf16[48,5248]{1,0:T(8,128)(2,1)S(1)} %unpack_y.1.refs_0_.refs_8_), channel_id=1, source_target_pairs={{0,128},{16,144},{32,160},{48,176},{64,192},{80,208},{96,224},{112... | collective-permute-start | bytes 1511432 | tf_op jit(solution)/shard_map/ppermute | solution.py:32
  65.1 15.0 %collective-permute-start.13 = (bf16[48,5120]{1,0:T(8,128)(2,1)}, bf16[48,5120]{1,0:T(8,128)(2,1)S(1)}, u32[]{:S(2)}, u32[]{:S(2)}) collective-permute-start(bf16[48,5120]{1,0:T(8,128)(2,1)} %collective-permute-done.1.refs_4_), channel_id=1, source_target_pairs={{0,96},{16,112},{32,0},{48,16},{64,32},{80,48},{96,64},{112,80},{1... | collective-permute-start | bytes 1474568 | tf_op jit(solution)/shard_map/ppermute | solution.py:32
  67.9 34.0 %collective-permute-start.4 = (bf16[48,5248]{1,0:T(8,128)(2,1)S(1)}, bf16[48,5248]{1,0:T(8,128)(2,1)S(1)}, u32[]{:S(2)}, u32[]{:S(2)}) collective-permute-start(bf16[48,5248]{1,0:T(8,128)(2,1)S(1)} %unpack_y.1.refs_0_.refs_8_), channel_id=1, source_target_pairs={{0,32},{16,48},{32,64},{48,80},{64,96},{80,112},{96,0},{112,16},{1... | collective-permute-start | bytes 1511432 | tf_op jit(solution)/shard_map/ppermute | solution.py:32
  76.6 37.8 %copy-start.25 = (bf16[48,5248]{1,0:T(8,128)(2,1)}, bf16[48,5248]{1,0:T(8,128)(2,1)S(1)}, u32[]{:S(2)}) copy-start(bf16[48,5248]{1,0:T(8,128)(2,1)S(1)} %collective-permute-done.7.refs_4_.refs_12_) | copy-start | bytes 1511428
  76.6 25.4 %collective-permute-start.9 = (bf16[48,5248]{1,0:T(8,128)(2,1)S(1)}, bf16[48,5248]{1,0:T(8,128)(2,1)S(1)}, u32[]{:S(2)}, u32[]{:S(2)}) collective-permute-start(bf16[48,5248]{1,0:T(8,128)(2,1)S(1)} %collective-permute-done.7.refs_4_.refs_12_), channel_id=1, source_target_pairs={{0,96},{16,112},{32,0},{48,16},{64,32},{80,48},{96,64},{112,80},{1... | collective-permute-start | bytes 1511432 | tf_op jit(solution)/shard_map/ppermute | solution.py:32
  79.4 15.4 %collective-permute-start.11 = (bf16[48,5120]{1,0:T(8,128)(2,1)S(1)}, bf16[48,5120]{1,0:T(8,128)(2,1)S(1)}, u32[]{:S(2)}, u32[]{:S(2)}) collective-permute-start(bf16[48,5120]{1,0:T(8,128)(2,1)S(1)} %collective-permute-done.2.refs_1_), channel_id=1, source_target_pairs={{0,32},{16,48},{32,64},{48,80},{64,96},{80,112},{96,0},{112,16},{1... | collective-permute-start | bytes 1474568 | tf_op jit(solution)/shard_map/ppermute | solution.py:32
  79.4 22.6 %collective-permute-start.12 = (bf16[48,5120]{1,0:T(8,128)(2,1)}, bf16[48,5120]{1,0:T(8,128)(2,1)S(1)}, u32[]{:S(2)}, u32[]{:S(2)}) collective-permute-start(bf16[48,5120]{1,0:T(8,128)(2,1)} %collective-permute-done.1.refs_4_), channel_id=1, source_target_pairs={{0,32},{16,48},{32,64},{48,80},{64,96},{80,112},{96,0},{112,16},{1... | collective-permute-start | bytes 1474568 | tf_op jit(solution)/shard_map/ppermute | solution.py:32
  80.1 70.4 %copy-start.4 = (bf16[48,5120]{1,0:T(8,128)(2,1)}, bf16[48,5120]{1,0:T(8,128)(2,1)S(1)}, u32[]{:S(2)}) copy-start(bf16[48,5120]{1,0:T(8,128)(2,1)S(1)} %collective-permute-done.13.refs_7_) | copy-start | bytes 1474564
  80.1 25.1 %collective-permute-start.14 = (bf16[48,5120]{1,0:T(8,128)(2,1)S(1)}, bf16[48,5120]{1,0:T(8,128)(2,1)S(1)}, u32[]{:S(2)}, u32[]{:S(2)}) collective-permute-start(bf16[48,5120]{1,0:T(8,128)(2,1)S(1)} %collective-permute-done.13.refs_7_), channel_id=1, source_target_pairs={{0,96},{16,112},{32,0},{48,16},{64,32},{80,48},{96,64},{112,80},{1... | collective-permute-start | bytes 1474568 | tf_op jit(solution)/shard_map/ppermute | solution.py:32
  94.7 55.8 %copy-start.6 = (bf16[48,5120]{1,0:T(8,128)(2,1)}, bf16[48,5120]{1,0:T(8,128)(2,1)S(1)}, u32[]{:S(2)}) copy-start(bf16[48,5120]{1,0:T(8,128)(2,1)S(1)} %collective-permute-done.11.refs_2_) | copy-start | bytes 1474564
  94.7 20.5 %collective-permute-start.6 = (bf16[48,5248]{1,0:T(8,128)(2,1)S(1)}, bf16[48,5248]{1,0:T(8,128)(2,1)S(1)}, u32[]{:S(2)}, u32[]{:S(2)}) collective-permute-start(bf16[48,5248]{1,0:T(8,128)(2,1)S(1)} %unpack_y.1.refs_0_.refs_8_), channel_id=1, source_target_pairs={{0,96},{16,112},{32,0},{48,16},{64,32},{80,48},{96,64},{112,80},{1... | collective-permute-start | bytes 1511432 | tf_op jit(solution)/shard_map/ppermute | solution.py:32
  101.9 48.6 %copy-start.8 = (bf16[48,5120]{1,0:T(8,128)(2,1)}, bf16[48,5120]{1,0:T(8,128)(2,1)S(1)}, u32[]{:S(2)}) copy-start(bf16[48,5120]{1,0:T(8,128)(2,1)S(1)} %collective-permute-done.12.refs_5_) | copy-start | bytes 1474564
  101.9 15.6 %collective-permute-start.8 = (bf16[48,5248]{1,0:T(8,128)(2,1)S(1)}, bf16[48,5248]{1,0:T(8,128)(2,1)S(1)}, u32[]{:S(2)}, u32[]{:S(2)}) collective-permute-start(bf16[48,5248]{1,0:T(8,128)(2,1)S(1)} %collective-permute-done.7.refs_4_.refs_12_), channel_id=1, source_target_pairs={{0,32},{16,48},{32,64},{48,80},{64,96},{80,112},{96,0},{112,16},{1... | collective-permute-start | bytes 1511432 | tf_op jit(solution)/shard_map/ppermute | solution.py:32
  102.0 22.1 %collective-permute-start.5 = (bf16[48,5248]{1,0:T(8,128)(2,1)S(1)}, bf16[48,5248]{1,0:T(8,128)(2,1)S(1)}, u32[]{:S(2)}, u32[]{:S(2)}) collective-permute-start(bf16[48,5248]{1,0:T(8,128)(2,1)S(1)} %collective-permute-done.4.refs_1_.refs_9_), channel_id=1, source_target_pairs={{0,32},{16,48},{32,64},{48,80},{64,96},{80,112},{96,0},{112,16},{1... | collective-permute-start | bytes 1511432 | tf_op jit(solution)/shard_map/ppermute | solution.py:32
  102.1 12.4 %copy-start.26 = (bf16[48,5248]{1,0:T(8,128)(2,1)}, bf16[48,5248]{1,0:T(8,128)(2,1)S(1)}, u32[]{:S(2)}) copy-start(bf16[48,5248]{1,0:T(8,128)(2,1)S(1)} %collective-permute-done.9.refs_7_.refs_15_) | copy-start | bytes 1511428
  102.1 22.0 %collective-permute-start.10 = (bf16[48,5248]{1,0:T(8,128)(2,1)S(1)}, bf16[48,5248]{1,0:T(8,128)(2,1)S(1)}, u32[]{:S(2)}, u32[]{:S(2)}) collective-permute-start(bf16[48,5248]{1,0:T(8,128)(2,1)S(1)} %collective-permute-done.9.refs_7_.refs_15_), channel_id=1, source_target_pairs={{0,96},{16,112},{32,0},{48,16},{64,32},{80,48},{96,64},{112,80},{1... | collective-permute-start | bytes 1511432 | tf_op jit(solution)/shard_map/ppermute | solution.py:32
  105.3 1.0 copy-start.2
  106.3 44.2 %copy-start.10 = (bf16[48,5120]{1,0:T(8,128)(2,1)}, bf16[48,5120]{1,0:T(8,128)(2,1)S(1)}, u32[]{:S(2)}) copy-start(bf16[48,5120]{1,0:T(8,128)(2,1)S(1)} %collective-permute-done.14.refs_6_) | copy-start | bytes 1474564
  115.2 35.3 %copy-start.3 = (bf16[48,5120]{1,0:T(8,128)(2,1)S(1)}, bf16[48,5120]{1,0:T(8,128)(2,1)}, u32[]{:S(2)}) copy-start(bf16[48,5120]{1,0:T(8,128)(2,1)} %copy-done.1) | copy-start | bytes 1474564
  115.2 8.9 %copy-start.27 = (bf16[48,5248]{1,0:T(8,128)(2,1)}, bf16[48,5248]{1,0:T(8,128)(2,1)S(1)}, u32[]{:S(2)}) copy-start(bf16[48,5248]{1,0:T(8,128)(2,1)S(1)} %collective-permute-done.6.refs_3_.refs_11_) | copy-start | bytes 1511428
  117.6 6.5 %copy-start.28 = (bf16[48,5248]{1,0:T(8,128)(2,1)}, bf16[48,5248]{1,0:T(8,128)(2,1)S(1)}, u32[]{:S(2)}) copy-start(bf16[48,5248]{1,0:T(8,128)(2,1)S(1)} %collective-permute-done.8.refs_5_.refs_13_) | copy-start | bytes 1511428
  135.5 25.2 %copy-start.16 = (bf16[192,384]{1,0:T(8,128)(2,1)}, bf16[192,384]{1,0:T(8,128)(2,1)S(1)}, u32[]{:S(2)}) copy-start(bf16[192,384]{1,0:T(8,128)(2,1)S(1)} %get-tuple-element.58.refs_17_) | copy-start | bytes 442372
  135.5 25.2 %copy-start.19 = (bf16[192,384]{1,0:T(8,128)(2,1)}, bf16[192,384]{1,0:T(8,128)(2,1)S(1)}, u32[]{:S(2)}) copy-start(bf16[192,384]{1,0:T(8,128)(2,1)S(1)} %get-tuple-element.68.refs_16_) | copy-start | bytes 442372
  135.5 11.4 %collective-permute-start.15 = (bf16[48,5248]{1,0:T(8,128)(2,1)S(1)}, bf16[48,5248]{1,0:T(8,128)(2,1)S(1)}, u32[]{:S(2)}, u32[]{:S(2)}) collective-permute-start(bf16[48,5248]{1,0:T(8,128)(2,1)S(1)} %get-tuple-element.51), channel_id=1, source_target_pairs={{0,32},{16,48},{32,64},{48,80},{64,96},{80,112},{96,0},{112,16},{1... | collective-permute-start | bytes 1511432 | tf_op jit(solution)/shard_map/ppermute | solution.py:32
  135.6 11.3 %collective-permute-start.16 = (bf16[48,5248]{1,0:T(8,128)(2,1)S(1)}, bf16[48,5248]{1,0:T(8,128)(2,1)S(1)}, u32[]{:S(2)}, u32[]{:S(2)}) collective-permute-start(bf16[48,5248]{1,0:T(8,128)(2,1)S(1)} %get-tuple-element.52), channel_id=1, source_target_pairs={{0,96},{16,112},{32,0},{48,16},{64,32},{80,48},{96,64},{112,80},{1... | collective-permute-start | bytes 1511432 | tf_op jit(solution)/shard_map/ppermute | solution.py:32
  147.2 13.5 %collective-permute-start.17 = (bf16[48,5248]{1,0:T(8,128)(2,1)S(1)}, bf16[48,5248]{1,0:T(8,128)(2,1)S(1)}, u32[]{:S(2)}, u32[]{:S(2)}) collective-permute-start(bf16[48,5248]{1,0:T(8,128)(2,1)S(1)} %join.3), channel_id=1, source_target_pairs={{0,32},{16,48},{32,64},{48,80},{64,96},{80,112},{96,0},{112,16},{1... | collective-permute-start | bytes 1511432 | tf_op jit(solution)/shard_map/ppermute | solution.py:32
  147.3 13.5 %collective-permute-start.18 = (bf16[48,5248]{1,0:T(8,128)(2,1)S(1)}, bf16[48,5248]{1,0:T(8,128)(2,1)S(1)}, u32[]{:S(2)}, u32[]{:S(2)}) collective-permute-start(bf16[48,5248]{1,0:T(8,128)(2,1)S(1)} %get-tuple-element.56), channel_id=1, source_target_pairs={{0,96},{16,112},{32,0},{48,16},{64,32},{80,48},{96,64},{112,80},{1... | collective-permute-start | bytes 1511432 | tf_op jit(solution)/shard_map/ppermute | solution.py:32
  160.8 29.1 %collective-permute-start.22 = (bf16[288,5120]{1,0:T(8,128)(2,1)}, bf16[288,5120]{1,0:T(8,128)(2,1)}, u32[]{:S(2)}, u32[]{:S(2)}) collective-permute-start(bf16[288,5120]{1,0:T(8,128)(2,1)} %wgrad_away.1), channel_id=1, source_target_pairs={{0,16},{16,0},{32,48},{48,32},{64,80},{80,64},{96,112},{112,96},{1... | collective-permute-start | bytes 8847368 | tf_op jit(solution)/shard_map/ppermute | solution.py:32
  161.2 28.7 %copy-start.5 = (bf16[48,5120]{1,0:T(8,128)(2,1)S(1)}, bf16[48,5120]{1,0:T(8,128)(2,1)}, u32[]{:S(2)}) copy-start(bf16[48,5120]{1,0:T(8,128)(2,1)} %copy-done.4) | copy-start | bytes 1474564
  161.2 13.9 %collective-permute-start.20 = (bf16[48,5248]{1,0:T(8,128)(2,1)S(1)}, bf16[48,5248]{1,0:T(8,128)(2,1)S(1)}, u32[]{:S(2)}, u32[]{:S(2)}) collective-permute-start(bf16[48,5248]{1,0:T(8,128)(2,1)S(1)} %join.4), channel_id=1, source_target_pairs={{0,96},{16,112},{32,0},{48,16},{64,32},{80,48},{96,64},{112,80},{1... | collective-permute-start | bytes 1511432 | tf_op jit(solution)/shard_map/ppermute | solution.py:32
  163.0 14.8 %collective-permute-start.19 = (bf16[48,5248]{1,0:T(8,128)(2,1)S(1)}, bf16[48,5248]{1,0:T(8,128)(2,1)S(1)}, u32[]{:S(2)}, u32[]{:S(2)}) collective-permute-start(bf16[48,5248]{1,0:T(8,128)(2,1)S(1)} %get-tuple-element.60), channel_id=1, source_target_pairs={{0,32},{16,48},{32,64},{48,80},{64,96},{80,112},{96,0},{112,16},{1... | collective-permute-start | bytes 1511432 | tf_op jit(solution)/shard_map/ppermute | solution.py:32
  163.7 14.1 %collective-permute-start.21 = (bf16[48,5248]{1,0:T(8,128)(2,1)S(1)}, bf16[48,5248]{1,0:T(8,128)(2,1)S(1)}, u32[]{:S(2)}, u32[]{:S(2)}) collective-permute-start(bf16[48,5248]{1,0:T(8,128)(2,1)S(1)} %join.5), channel_id=1, source_target_pairs={{0,128},{16,144},{32,160},{48,176},{64,192},{80,208},{96,224},{112... | collective-permute-start | bytes 1511432 | tf_op jit(solution)/shard_map/ppermute | solution.py:32
  179.1 28.6 %all-to-all-start.2 = ((bf16[16,8,2048]{2,1,0:T(8,128)(2,1)}), bf16[16,8,2048]{2,1,0:T(8,128)(2,1)}, u32[]{:S(2)}, u32[]{:S(2)}) async-start(bf16[16,8,2048]{2,1,0:T(8,128)(2,1)} %bitcast.18), calls=%async_computation.2 | async-start | bytes 1048576 | tf_op jit(solution)/shard_map/all_to_all | solution.py:354
  189.9 1.0 copy-start.7
  190.9 1.0 copy-start.9
  (8 other events, 6.8 us)
where the time goes:
time: 212 us; the launch traced here: 211 us
  waiting for transfers between devices  91.5 us (43%)
  starting transfers between devices  52.7 us (25%)
  Pallas kernels  50 us (24%)
  local copies, waits for them, and re-layouts  12.3 us (6%)
  other arithmetic  3.72 us (2%)
    ppermute x23, waiting for transfers between devices, hop(): return lax.ppermute(a, 'edp', perm)  76.3 us
    pallas_call x13, Pallas kernels, run(): pl.pallas_call(kernel, out_shape=outs, in_specs=[one] * len(args) if spec...  50 us
    ppermute x23, starting transfers between devices, hop(): return lax.ppermute(a, 'edp', perm)  27.7 us
    all_to_all x3, starting transfers between devices, exchange(): a = lax.all_to_all(a, 'ep', split_axis=0, concat_axis=0, tiled=True)  24.9 us
    all_to_all x3, waiting for transfers between devices, exchange(): a = lax.all_to_all(a, 'ep', split_axis=0, concat_axis=0, tiled=True)  15.2 us
    unnamed x60, local copies, waits for them, and re-layouts  12.3 us
  transfers between devices with their start and end apart: 26, of which 13 were waited for; matrix products, arithmetic and copies ran while one was open for 0% of the time, Pallas kernels for 17%

commit v1 on v0

v1 whole, which is shorter than its diff:
```python
import functools

import jax
import jax.numpy as jnp
from jax import lax
from jax.experimental import pallas as pl
from jax.experimental.pallas import tpu as pltpu
from jax.sharding import PartitionSpec as P

CAP = 3
QN = 8
LANES = 128
F32 = jnp.float32
BF16 = jnp.bfloat16


def chip_perm(move):
    return [(i, (i & 9) | (move((i >> 1) & 3) << 1)) for i in range(16)]


ROW_SWAP = chip_perm(lambda x: 3 - x)
PAIR_SWAP = chip_perm(lambda x: x ^ 1)
Z_SWAP = [(i, i ^ 8) for i in range(16)]
C_SWAP = [(i, i ^ 1) for i in range(16)]


def hop(a, perm):
    return lax.ppermute(a, "edp", perm)


def iota(shape, dim):
    return lax.broadcasted_iota(jnp.int32, shape, dim)


def dot(a, b):
    return jnp.dot(a, b, preferred_element_type=F32)


def dot_nt(a, b):
    return lax.dot_general(a, b, (((1,), (1,)), ((), ())), preferred_element_type=F32)


def call(kernel, outs, name, scratch=(), specs=None, out_specs=None, cost=None, limit=48):
    one = pl.BlockSpec(memory_space=pltpu.VMEM)
    params = pltpu.CompilerParams(vmem_limit_bytes=limit * 1024 * 1024)

    def run(*args):
        return pl.pallas_call(
            kernel,
            out_shape=outs,
            in_specs=[one] * len(args) if specs is None else specs,
            out_specs=jax.tree.map(lambda _: one, outs) if out_specs is None else out_specs,
            scratch_shapes=scratch,
            compiler_params=params,
            name=name,
            cost_estimate=cost
            and pl.CostEstimate(flops=cost[0], bytes_accessed=cost[1], transcendentals=0),
        )(*args)

    return run


def live_tables(ids_t):
    tokens = ids_t.shape[1]
    expert = iota((LANES, tokens), 0) >> 3
    hits = jnp.zeros((LANES, tokens), F32)
    for r in range(ids_t.shape[0]):
        hits = hits + jnp.where(ids_t[r : r + 1, :] == expert, 1.0, 0.0)
    earlier = jnp.where(iota((tokens, tokens), 0) < iota((tokens, tokens), 1), 1.0, 0.0)
    before = dot(hits.astype(BF16), earlier.astype(BF16))
    return [jnp.where(before == s, hits, 0.0) for s in range(CAP)]


def send_kernel(*refs, with_p):
    if with_p:
        ids_ref, probs_ref, tok_ref, out_ref = refs
    else:
        ids_ref, tok_ref, out_ref = refs
    ids_t = ids_ref[...]
    group = tok_ref.shape[1] // QN
    live = live_tables(ids_t)
    q = iota(live[0].shape, 0) & (QN - 1)
    for s in range(CAP):
        total = jnp.zeros((LANES, group), F32)
        for k in range(QN):
            pick = jnp.where(q == k, live[s], 0.0).astype(BF16)
            total = total + dot(pick, tok_ref[:, k * group : (k + 1) * group])
        out_ref[:, s * group : (s + 1) * group] = total.astype(BF16)
    if with_p:
        expert = iota(live[0].shape, 0) >> 3
        probs = jnp.zeros(live[0].shape, F32)
        for r in range(ids_t.shape[0]):
            probs = probs + jnp.where(
                ids_t[r : r + 1, :] == expert, probs_ref[r : r + 1, :].astype(F32), 0.0
            )
        lane = iota((LANES, LANES), 1)
        tail = jnp.zeros((LANES, LANES), F32)
        for s in range(CAP):
            col = jnp.sum(live[s] * probs, axis=1, keepdims=True)
            tail = tail + jnp.where(lane == s, col, 0.0)
        out_ref[:, CAP * group :] = tail.astype(BF16)


def unpack_kernel(in_ref, out_ref, *, group):
    row, col = iota((LANES, LANES), 0), iota((LANES, LANES), 1)
    swap = jnp.where((row & 15) * QN + (row >> 4) == col, 1.0, 0.0).astype(BF16)
    for s in range(CAP):
        got = dot(swap, in_ref[:, s * group : (s + 1) * group]).astype(BF16)
        for k in range(QN):
            out_ref[s * 16 : (s + 1) * 16, k * group : (k + 1) * group] = got[
                k * 16 : (k + 1) * 16, :
            ]
    if out_ref.shape[1] > QN * group:
        tail = dot(swap, in_ref[:, CAP * group :])
        for s in range(CAP):
            out_ref[s * 16 : (s + 1) * 16, QN * group :] = jnp.broadcast_to(
                tail[0:16, s : s + 1], (16, LANES)
            ).astype(BF16)


def fetch(copies):
    for c in copies:
        c.start()
    for c in copies:
        c.wait()


def product(out_ref, left, right, step=640):
    out_ref[...] = jnp.zeros(out_ref.shape, F32)

    def body(n, carry):
        cols = pl.ds(pl.multiple_of(n * step, step), step)
        out_ref[...] += dot_nt(left[:, cols], right[:, cols])
        return carry

    lax.fori_loop(0, left.shape[1] // step, body, 0)


def stacked(sources, target, sems, first):
    rows = sources[0].shape[0]
    return [
        pltpu.make_async_copy(a, target.at[pl.ds(k * rows, rows)], sems.at[first + k])
        for k, a in enumerate(sources)
    ]


def pre_kernel(*refs):
    xs, gs, us = refs[0:4], refs[4:8], refs[8:12]
    gate_ref, up_ref, x_out, g_all, u_all, sems = refs[12:]
    first = stacked(xs, x_out, sems, 0) + stacked(gs, g_all, sems, 4)
    second = stacked(us, u_all, sems, 8)
    for c in first + second:
        c.start()
    for c in first:
        c.wait()
    product(gate_ref, g_all, x_out)
    for c in second:
        c.wait()
    product(up_ref, u_all, x_out)


def main_kernel(*refs):
    ys, ds, (gate_ref, up_ref) = refs[0:4], refs[4:8], refs[8:10]
    dg_ref, du_ref, hid_ref, py_ref, tail_ref, y_all, d_all, acc, sems = refs[10:]
    copies = stacked(ds, d_all, sems, 0) + stacked(ys, y_all, sems, 4)
    fetch(copies)
    width = d_all.shape[1]
    total = y_all.shape[0]
    product(acc, d_all, y_all)
    back = acc[...]
    probs = y_all[:, width:].astype(F32)
    prob = jnp.transpose(probs)[0:1, :]
    gate, up = gate_ref[...], up_ref[...]
    sig = jax.nn.sigmoid(gate)
    hidden = gate * sig * up
    part = jnp.sum(hidden * back, axis=0, keepdims=True)
    scaled = prob * back
    dg_ref[...] = (scaled * up * sig * (1.0 + gate * (1.0 - sig))).astype(BF16)
    du_ref[...] = (scaled * gate * sig).astype(BF16)
    hid_ref[...] = hidden.astype(BF16)
    py_ref[...] = (probs[:, 0:1] * y_all[:, 0:width].astype(F32)).astype(BF16)
    high = part.astype(BF16).astype(F32)
    low = part - high
    tail = jnp.where(
        iota((LANES, total), 0) < LANES // 2,
        jnp.broadcast_to(high, (LANES, total)),
        jnp.broadcast_to(low, (LANES, total)),
    )
    tail_ref[...] = jnp.transpose(tail).astype(BF16)


def back_kernel(*refs):
    dg_ref, du_ref, tail_ref = refs[0:3]
    gs, us, outs = refs[3:7], refs[7:11], refs[11:15]
    g_all, u_all, sems = refs[15:]
    copies = stacked(gs, g_all, sems, 0) + stacked(us, u_all, sems, 4)
    for c in copies:
        c.start()
    rows, width = outs[0].shape[0], g_all.shape[1]
    for k in range(4):
        outs[k][:, width:] = tail_ref[k * rows : (k + 1) * rows, :]
    d_gate = jnp.transpose(dg_ref[...].astype(F32)).astype(BF16)
    d_up = jnp.transpose(du_ref[...].astype(F32)).astype(BF16)
    for c in copies:
        c.wait()
    step = 640

    def body(n, carry):
        cols = pl.ds(pl.multiple_of(n * step, step), step)
        got = (dot(d_gate, g_all[:, cols]) + dot(d_up, u_all[:, cols])).astype(BF16)
        for k in range(4):
            outs[k][:, cols] = got[k * rows : (k + 1) * rows, :]
        return carry

    lax.fori_loop(0, width // step, body, 0)


def wgrad_kernel(left_ref, rows_ref, *rest, first):
    *came, out_ref = rest
    hid = out_ref.shape[0]
    total = dot(left_ref[first : first + hid, :], rows_ref[...])
    for c in came:
        total = total + c[...].astype(F32)
    out_ref[...] = total.astype(BF16)


def summed(refs):
    total = refs[0][...].astype(F32)
    for r in refs[1:]:
        total = total + r[...].astype(F32)
    return total


def join_kernel(*refs, width):
    *parts, out_ref = refs
    body = [p.at[:, pl.ds(0, width)] for p in parts]
    out_ref[:, 0:width] = summed(body).astype(BF16)
    tail = summed([p.at[:, pl.ds(width, LANES)] for p in parts])
    value = tail[:, 0:1] + tail[:, LANES // 2 : LANES // 2 + 1]
    high = value.astype(BF16).astype(F32)
    out_ref[:, width:] = jnp.where(
        iota(tail.shape, 1) < LANES // 2, high, value - high
    ).astype(BF16)


def last_kernel(*refs, group):
    *parts, out_ref = refs
    width = QN * group
    row, col = iota((LANES, LANES), 0), iota((LANES, LANES), 1)
    swap = jnp.where((col & 15) * QN + (col >> 4) == row, 1.0, 0.0).astype(BF16)
    total = summed([p.at[:, pl.ds(0, width)] for p in parts]).astype(BF16)
    for s in range(CAP):
        stack = jnp.concatenate(
            [total[s * 16 : (s + 1) * 16, k * group : (k + 1) * group] for k in range(QN)], axis=0
        )
        out_ref[:, s * group : (s + 1) * group] = dot(swap, stack).astype(BF16)
    tail = summed([p.at[:, pl.ds(width, LANES)] for p in parts])
    value = tail[:, 0:1] + tail[:, LANES // 2 : LANES // 2 + 1]
    lane = iota((16, LANES), 1)
    cols = jnp.zeros((16, LANES), F32)
    for s in range(CAP):
        cols = cols + jnp.where(lane == s, value[s * 16 : (s + 1) * 16, :], 0.0)
    stack = jnp.concatenate([cols] * QN, axis=0).astype(BF16)
    out_ref[:, CAP * group :] = dot(swap, stack).astype(BF16)


def final_kernel(ids_ref, in_ref, tok_ref, gate_ref, *, group):
    ids_t = ids_ref[...]
    live = live_tables(ids_t)
    lane = iota(live[0].shape, 1)
    sides = [jnp.transpose(v) for v in live]
    for k in range(QN):
        total = jnp.zeros((live[0].shape[1], group), F32)
        for s in range(CAP):
            pick = jnp.where((lane & (QN - 1)) == k, sides[s], 0.0).astype(BF16)
            total = total + dot(pick, in_ref[:, s * group : (s + 1) * group])
        tok_ref[:, k * group : (k + 1) * group] = total.astype(BF16)
    row = iota(live[0].shape, 0)
    value = jnp.zeros(live[0].shape, F32)
    for s in range(CAP):
        col = in_ref[:, CAP * group + s : CAP * group + s + 1].astype(F32)
        value = value + live[s] * col
    value = jnp.where((row & (QN - 1)) == 0, value, 0.0)
    for r in range(ids_t.shape[0]):
        mine = jnp.where(ids_t[r : r + 1, :] == (row >> 3), value, 0.0)
        gate_ref[r : r + 1, :] = jnp.sum(mine, axis=0, keepdims=True).astype(BF16)


def per_device(tokens, cotangent, gate_probs, expert_ids, w_gate, w_up, w_down):
    width = tokens.shape[1]
    group = width // QN
    wide = width + LANES
    rows = CAP * 16
    total = 4 * rows
    g, u, d = w_gate[0], w_up[0], w_down[0]
    hid = g.shape[0]
    ids_t, probs_t = expert_ids.T, gate_probs.T
    shape = jax.ShapeDtypeStruct
    any_spec, vmem = pl.BlockSpec(memory_space=pl.ANY), pl.BlockSpec(memory_space=pltpu.VMEM)
    dma = pltpu.SemaphoreType.DMA
    together = lax.optimization_barrier
    work = 2 * total * width * 4 * hid

    def exchange(a):
        a = a.reshape(16, QN, a.shape[1])
        a = lax.all_to_all(a, "ep", split_axis=0, concat_axis=0, tiled=True)
        return a.reshape(LANES, a.shape[2])

    def unpack(a, columns, name):
        return call(
            functools.partial(unpack_kernel, group=group),
            shape((rows, columns), BF16),
            name,
            cost=(10**8, 10**6),
        )(a)

    send_x = call(
        functools.partial(send_kernel, with_p=False),
        shape((LANES, CAP * group), BF16),
        "send_x",
        cost=(6 * 10**8, 2 * 10**6),
    )(ids_t, tokens)
    send_y = call(
        functools.partial(send_kernel, with_p=True),
        shape((LANES, CAP * group + LANES), BF16),
        "send_y",
        cost=(6 * 10**8, 2 * 10**6),
    )(ids_t, probs_t, cotangent)

    core_g, core_u, core_d = hop(g, C_SWAP), hop(u, C_SWAP), hop(d, C_SWAP)
    pair_g = hop(g, PAIR_SWAP)
    got_x, core_g, core_u, core_d, pair_g, send_y, u_next = together(
        (exchange(send_x), core_g, core_u, core_d, pair_g, send_y, u)
    )
    got_y = exchange(send_y)
    x = unpack(got_x, width, "unpack_x")
    x_row, x_oth = hop(x, ROW_SWAP), hop(x, Z_SWAP)
    pair_u = hop(u_next, PAIR_SWAP)
    cross_g = hop(pair_g, C_SWAP)
    got_y, x_row, x_oth, pair_u, cross_g, d_next = together(
        (got_y, x_row, x_oth, pair_u, cross_g, d)
    )
    pair_d = hop(d_next, PAIR_SWAP)
    cross_u = hop(pair_u, C_SWAP)
    y = unpack(got_y, wide, "unpack_y")
    x_oth_row = hop(x_oth, ROW_SWAP)
    y_oth, y_row = hop(y, Z_SWAP), hop(y, ROW_SWAP)
    y_oth_row = hop(y_oth, ROW_SWAP)
    cross_d = hop(pair_d, C_SWAP)
    gs, us = (g, core_g, pair_g, cross_g), (u, core_u, pair_u, cross_u)
    gate, up, x_all = call(
        pre_kernel,
        [shape((4 * hid, total), F32)] * 2 + [shape((total, width), BF16)],
        "pre",
        scratch=[pltpu.VMEM((4 * hid, width), BF16)] * 2 + [dma((12,))],
        specs=[any_spec] * 12,
        cost=(2 * work, 10 * 10**6),
    )(x, x_row, x_oth, x_oth_row, *gs, *us)
    d_gate, d_up, hidden, py, tail = call(
        main_kernel,
        [shape((4 * hid, total), BF16)] * 3
        + [shape((total, width), BF16), shape((total, LANES), BF16)],
        "main",
        scratch=[
            pltpu.VMEM((total, wide), BF16),
            pltpu.VMEM((4 * hid, width), BF16),
            pltpu.VMEM((4 * hid, total), F32),
            dma((8,)),
        ],
        specs=[any_spec] * 8 + [vmem] * 2,
        cost=(work, 8 * 10**6),
    )(y, y_row, y_oth, y_oth_row, d, core_d, pair_d, cross_d, gate, up)

    blocks = 4

    def wgrad(left, right, place, *came):
        cols = width // blocks
        part = pl.BlockSpec((hid, cols), lambda n: (0, n))
        return pl.pallas_call(
            functools.partial(wgrad_kernel, first=place * hid),
            out_shape=shape((hid, width), BF16),
            grid=(blocks,),
            in_specs=[
                pl.BlockSpec(left.shape, lambda n: (0, 0)),
                pl.BlockSpec((total, cols), lambda n: (0, n)),
            ]
            + [part] * len(came),
            out_specs=part,
            compiler_params=pltpu.CompilerParams(vmem_limit_bytes=16 * 1024 * 1024),
            name="wgrad",
            cost_estimate=pl.CostEstimate(
                flops=work // 4, bytes_accessed=3 * 10**6, transcendentals=0
            ),
        )(left, right, *came)

    def join(*a):
        return call(
            functools.partial(join_kernel, width=width),
            shape((rows, wide), BF16),
            "join",
            cost=(10**6, 10**6),
        )(*a)

    cross = [hop(wgrad(hidden, py, 3), C_SWAP)]
    own, row, oth, oth_row = call(
        back_kernel,
        [shape((rows, wide), BF16)] * 4,
        "back",
        scratch=[pltpu.VMEM((4 * hid, width), BF16)] * 2 + [dma((8,))],
        specs=[vmem] * 3 + [any_spec] * 8,
        cost=(2 * work, 10 * 10**6),
    )(d_gate, d_up, tail, *gs, *us)
    cross += [hop(wgrad(d_gate, x_all, 3), C_SWAP), hop(wgrad(d_up, x_all, 3), C_SWAP)]
    far = hop(oth_row, ROW_SWAP)
    pair_dw = hop(wgrad(hidden, py, 2, cross[0]), PAIR_SWAP)
    oth = hop(join(oth, far), Z_SWAP)
    row = hop(row, ROW_SWAP)
    pair_gw = hop(wgrad(d_gate, x_all, 2, cross[1]), PAIR_SWAP)
    pair_uw = hop(wgrad(d_up, x_all, 2, cross[2]), PAIR_SWAP)
    side = [
        hop(wgrad(hidden, py, 1), C_SWAP),
        hop(wgrad(d_gate, x_all, 1), C_SWAP),
        hop(wgrad(d_up, x_all, 1), C_SWAP),
    ]
    last = call(
        functools.partial(last_kernel, group=group),
        shape((LANES, CAP * group + LANES), BF16),
        "last",
        cost=(10**8, 3 * 10**6),
    )(own, row, oth)
    back = exchange(last)
    d_grad = wgrad(hidden, py, 0, side[0], pair_dw)
    g_grad = wgrad(d_gate, x_all, 0, side[1], pair_gw)
    token_grad, gate_t = call(
        functools.partial(final_kernel, group=group),
        [shape(tokens.shape, BF16), shape(ids_t.shape, BF16)],
        "final",
        cost=(6 * 10**8, 2 * 10**6),
    )(ids_t, back)
    u_grad = wgrad(d_up, x_all, 0, side[2], pair_uw)
    return (token_grad, gate_t.T, g_grad[None], u_grad[None], d_grad[None])


def solution(mesh):
    tok = P(("edp", "ep"), None)
    wgt = P("ep", "edp", None)
    return jax.shard_map(
        per_device,
        mesh=mesh,
        in_specs=(tok, tok, tok, tok, wgt, wgt, wgt),
        out_specs=(tok, tok, wgt, wgt, wgt),
        check_vma=False,
    )
```

time: 212 us -> 242 us (1.14)
  waiting for transfers between devices: 91.5 us -> 119 us
  Pallas kernels: 50 us -> 61.4 us
  starting transfers between devices: 52.7 us -> 44.6 us
  other arithmetic: 3.72 us -> 0 us
    ppermute x23 -> x27, waiting for transfers between devices: 76.3 us -> 105 us  [hop(): return lax.ppermute(a, 'edp', perm)]
    pallas_call x0 -> x12, Pallas kernels: none -> 27.7 us  [wgrad(): pl.pallas_call(functools.partial(wgrad_kernel, first=place * hid), out_sh...]
    pallas_call x13 -> x10, Pallas kernels: 50 us -> 33.7 us  [run(): pl.pallas_call(kernel, out_shape=outs, in_specs=[one] * len(args) if spec...]
    ppermute x23 -> x27, starting transfers between devices: 27.7 us -> 21.2 us  [hop(): return lax.ppermute(a, 'edp', perm)]
    concatenate x1 -> x0, other arithmetic: 3.72 us -> none  [per_device(): away_w = hop(jnp.concatenate([g, u, d], axis=0), C_SWAP)]
    unnamed x60 -> x58, local copies, waits for them, and re-layouts: 12.3 us -> 13.2 us
  transfers between devices with their start and end apart: 26 -> 30, of which waited for: 13 -> 10; matrix products, arithmetic and copies ran while one was open for 0% -> 0% of each run, Pallas kernels for 17% -> 21%
where the time goes in v1:
time: 242 us; the launch traced here: 239 us
  waiting for transfers between devices  119 us (49%)
  Pallas kernels  61.4 us (25%)
  starting transfers between devices  44.6 us (18%)
  local copies, waits for them, and re-layouts  13.2 us (5%)
    ppermute x27, waiting for transfers between devices, hop(): return lax.ppermute(a, 'edp', perm)  105 us
    pallas_call x10, Pallas kernels, run(): pl.pallas_call(kernel, out_shape=outs, in_specs=[one] * len(args) if spec...  33.7 us
    pallas_call x12, Pallas kernels, wgrad(): pl.pallas_call(functools.partial(wgrad_kernel, first=place * hid), out_sh...  27.7 us
    all_to_all x3, starting transfers between devices, exchange(): a = lax.all_to_all(a, 'ep', split_axis=0, concat_axis=0, tiled=True)  23.5 us
    ppermute x27, starting transfers between devices, hop(): return lax.ppermute(a, 'edp', perm)  21.2 us
    all_to_all x3, waiting for transfers between devices, exchange(): a = lax.all_to_all(a, 'ep', split_axis=0, concat_axis=0, tiled=True)  14.4 us
    unnamed x58, local copies, waits for them, and re-layouts  13.2 us
  transfers between devices with their start and end apart: 30, of which 10 were waited for; matrix products, arithmetic and copies ran while one was open for 0% of the time, Pallas kernels for 21%

profile of v1, /device:TPU:32, one launch (start us, length us, event | category | flops | bytes accessed | tf_op | source)
XLA Modules:
  0.0 239.3 jit_solution(10338806144436930628)
XLA Ops:
  0.6 1.6 collective-permute-start.3
  2.7 1.3 copy-done.21
  4.7 1.3 send_x.1
  6.8 10.3 %all-to-all-start = ((bf16[16,8,1920]{2,1,0:T(8,128)(2,1)}), bf16[16,8,1920]{2,1,0:T(8,128)(2,1)S(1)}, u32[]{:S(2)}, u32[]{:S(2)}) async-start(bf16[16,8,1920]{2,1,0:T(8,128)(2,1)} %bitcast.24), calls=%async_computation | async-start | bytes 983040 | tf_op jit(solution)/shard_map/all_to_all | solution.py:306
  17.2 1.3 copy-done.22
  18.5 1.3 send_y.1
  20.6 14.4 %all-to-all-done = bf16[16,8,1920]{2,1,0:T(8,128)(2,1)S(1)} async-done(((bf16[16,8,1920]{2,1,0:T(8,128)(2,1)}), bf16[16,8,1920]{2,1,0:T(8,128)(2,1)S(1)}, u32[]{:S(2)}, u32[]{:S(2)}) %all-to-all-start) | async-done | bytes 491552 | tf_op jit(solution)/shard_map/all_to_all | solution.py:306
  35.8 1.0 copy-done.13
  36.8 4.4 %all-to-all-start.1 = ((bf16[16,8,2048]{2,1,0:T(8,128)(2,1)}), bf16[16,8,2048]{2,1,0:T(8,128)(2,1)}, u32[]{:S(2)}, u32[]{:S(2)}) async-start(bf16[16,8,2048]{2,1,0:T(8,128)(2,1)} %bitcast.23), calls=%async_computation.1 | async-start | bytes 1048576 | tf_op jit(solution)/shard_map/all_to_all | solution.py:306
  41.8 1.0 copy-done.11
  43.1 1.4 collective-permute-start.5
  44.5 2.7 %collective-permute-start.4 = (bf16[48,5120]{1,0:T(8,128)(2,1)S(1)}, bf16[48,5120]{1,0:T(8,128)(2,1)S(1)}, u32[]{:S(2)}, u32[]{:S(2)}) collective-permute-start(bf16[48,5120]{1,0:T(8,128)(2,1)S(1)} %unpack_x.1.refs_0_), channel_id=1, source_target_pairs={{0,96},{16,112},{32,64},{48,80},{64,32},{80,48},{96,0},{112,16},{1... | collective-permute-start | bytes 1474568 | tf_op jit(solution)/shard_map/ppermute | solution.py:28
  48.0 16.5 %collective-permute-done.5.refs_2_ = bf16[48,5120]{1,0:T(8,128)(2,1)S(1)} collective-permute-done((bf16[48,5120]{1,0:T(8,128)(2,1)S(1)}, bf16[48,5120]{1,0:T(8,128)(2,1)S(1)}, u32[]{:S(2)}, u32[]{:S(2)}) %collective-permute-start.5) | collective-permute-done | bytes 491552 | tf_op jit(solution)/shard_map/ppermute | solution.py:28
  66.8 1.4 unpack_y.1.refs_0_
  68.9 19.9 %collective-permute-done.11.refs_6_ = bf16[96,5120]{1,0:T(8,128)(2,1)S(1)} collective-permute-done((bf16[96,5120]{1,0:T(8,128)(2,1)}, bf16[96,5120]{1,0:T(8,128)(2,1)S(1)}, u32[]{:S(2)}, u32[]{:S(2)}) %collective-permute-start.11) | collective-permute-done | bytes 983072 | tf_op jit(solution)/shard_map/ppermute | solution.py:28
  88.8 2.0 collective-permute-start.13
  90.8 1.2 collective-permute-start.8
  92.1 2.0 collective-permute-start.10
  94.1 10.2 %collective-permute-done.13.refs_3_ = bf16[48,5120]{1,0:T(8,128)(2,1)S(1)} collective-permute-done((bf16[48,5120]{1,0:T(8,128)(2,1)}, bf16[48,5120]{1,0:T(8,128)(2,1)S(1)}, u32[]{:S(2)}, u32[]{:S(2)}) %collective-permute-start.13) | collective-permute-done | bytes 491552 | tf_op jit(solution)/shard_map/ppermute | solution.py:28
  105.2 1.0 copy-done.19
  106.3 9.9 %pre.1 = (f32[384,192]{1,0:T(8,128)S(1)}, f32[384,192]{1,0:T(8,128)S(1)}, bf16[192,5120]{1,0:T(8,128)(2,1)}) custom-call(bf16[48,5120]{1,0:T(8,128)(2,1)S(1)} %copy-done.9, bf16[48,5120]{1,0:T(8,128)(2,1)S(1)} %copy-done.19, bf16[48,5120]{1,0:T(8,128)(2,1)S(1)} %copy-done.17, bf16[48,5120]{1,0:T(8,128)(2,1)S(1)} %collective-permute-done.13.refs_3_, ...), custom_call_target="tpu_custom_call" | custom-call | flops 1509949440 | bytes 10000000 | tf_op jit(solution)/shard_map/pre/pallas_call | solution.py:48
  116.2 9.3 %collective-permute-done.10.refs_3_ = bf16[48,5248]{1,0:T(8,128)(2,1)S(1)} collective-permute-done((bf16[48,5248]{1,0:T(8,128)(2,1)S(1)}, bf16[48,5248]{1,0:T(8,128)(2,1)S(1)}, u32[]{:S(2)}, u32[]{:S(2)}) %collective-permute-start.10) | collective-permute-done | bytes 503840 | tf_op jit(solution)/shard_map/ppermute | solution.py:28
  125.5 0.9 copy-done.28
  126.4 7.3 %main.1 = (bf16[384,192]{1,0:T(8,128)(2,1)S(1)}, bf16[384,192]{1,0:T(8,128)(2,1)S(1)}, bf16[384,192]{1,0:T(8,128)(2,1)S(1)}, bf16[192,5120]{1,0:T(8,128)(2,1)}, bf16[192,128]{1,0:T(8,128)(2,1)S(1)}) custom-call(bf16[48,5248]{1,0:T(8,128)(2,1)S(1)} %unpack_y.1.refs_0_, bf16[48,5248]{1,0:T(8,128)(2,1)S(1)} %collective-permute-done.8.refs_1_, ...), custom_call_target="tpu_custom_call" | custom-call | flops 754974720 | bytes 8000000 | tf_op jit(solution)/shard_map/main/pallas_call | solution.py:48
  133.8 1.1 wgrad.17
  135.2 7.2 %back.1 = (bf16[48,5248]{1,0:T(8,128)(2,1)S(1)}, bf16[48,5248]{1,0:T(8,128)(2,1)S(1)}, bf16[48,5248]{1,0:T(8,128)(2,1)S(1)}, bf16[48,5248]{1,0:T(8,128)(2,1)S(1)}) custom-call(bf16[384,192]{1,0:T(8,128)(2,1)S(1)} %get-tuple-element.47.refs_0_.left_ref, bf16[384,192]{1,0:T(8,128)(2,1)S(1)} %get-tuple-element.48.refs_1_.left_ref, ...), custom_call_target="tpu_custom_call" | custom-call | flops 1509949440 | bytes 10000000 | tf_op jit(solution)/shard_map/back/pallas_call | solution.py:48
  142.5 2.1 collective-permute-start.16
  144.6 1.1 wgrad.13
  145.8 1.1 wgrad.21
  147.5 1.1 wgrad.16
  148.7 8.7 %collective-permute-done.16.refs_1_ = bf16[48,5248]{1,0:T(8,128)(2,1)S(1)} collective-permute-done((bf16[48,5248]{1,0:T(8,128)(2,1)S(1)}, bf16[48,5248]{1,0:T(8,128)(2,1)S(1)}, u32[]{:S(2)}, u32[]{:S(2)}) %collective-permute-start.16) | collective-permute-done | bytes 503840 | tf_op jit(solution)/shard_map/ppermute | solution.py:28
  157.4 2.0 collective-permute-start.15
  160.1 2.2 wgrad.20
  162.3 2.2 wgrad.12
  164.5 2.2 wgrad.18
  166.8 2.3 wgrad.14
  169.0 2.4 %collective-permute-done.15.refs_1_ = bf16[48,5248]{1,0:T(8,128)(2,1)S(1)} collective-permute-done((bf16[48,5248]{1,0:T(8,128)(2,1)S(1)}, bf16[48,5248]{1,0:T(8,128)(2,1)S(1)}, u32[]{:S(2)}, u32[]{:S(2)}) %collective-permute-start.15) | collective-permute-done | bytes 503840 | tf_op jit(solution)/shard_map/ppermute | solution.py:28
  171.5 2.3 wgrad.22
  174.3 1.8 collective-permute-start.26
  176.1 1.2 last.1
  177.3 8.8 %all-to-all-start.2 = ((bf16[16,8,2048]{2,1,0:T(8,128)(2,1)}), bf16[16,8,2048]{2,1,0:T(8,128)(2,1)}, u32[]{:S(2)}, u32[]{:S(2)}) async-start(bf16[16,8,2048]{2,1,0:T(8,128)(2,1)} %bitcast.9), calls=%async_computation.2 | async-start | bytes 1048576 | tf_op jit(solution)/shard_map/all_to_all | solution.py:306
  186.1 5.6 %collective-permute-done.23.rest_1_ = bf16[96,5120]{1,0:T(8,128)(2,1)} collective-permute-done((bf16[96,5120]{1,0:T(8,128)(2,1)}, bf16[96,5120]{1,0:T(8,128)(2,1)}, u32[]{:S(2)}, u32[]{:S(2)}) %collective-permute-start.23) | collective-permute-done | bytes 983072 | tf_op jit(solution)/shard_map/ppermute | solution.py:28
  191.8 3.9 %wgrad.19 = bf16[96,5120]{1,0:T(8,128)(2,1)} custom-call(bf16[384,192]{1,0:T(8,128)(2,1)S(1)} %get-tuple-element.48.refs_1_.left_ref, bf16[192,5120]{1,0:T(8,128)(2,1)S(1)} %copy-done, bf16[96,5120]{1,0:T(8,128)(2,1)S(1)} %collective-permute-done.21.rest_0_, bf16[96,5120]{1,0:T(8,128)(2,1)} %collective-permute-done.23.rest_1_), custom_call_target="tpu_custom_call" | custom-call | flops 188743680 | bytes 3000000 | tf_op jit(solution)/shard_map/wgrad/pallas_call | solution.py:379
  195.6 17.2 %collective-permute-done.20.rest_1_ = bf16[96,5120]{1,0:T(8,128)(2,1)} collective-permute-done((bf16[96,5120]{1,0:T(8,128)(2,1)}, bf16[96,5120]{1,0:T(8,128)(2,1)}, u32[]{:S(2)}, u32[]{:S(2)}) %collective-permute-start.20) | collective-permute-done | bytes 983072 | tf_op jit(solution)/shard_map/ppermute | solution.py:28
  212.8 4.1 %wgrad.15 = bf16[96,5120]{1,0:T(8,128)(2,1)} custom-call(bf16[384,192]{1,0:T(8,128)(2,1)S(1)} %get-tuple-element.47.refs_0_.left_ref, bf16[192,5120]{1,0:T(8,128)(2,1)S(1)} %copy-done, bf16[96,5120]{1,0:T(8,128)(2,1)} %collective-permute-done.18.rest_0_, bf16[96,5120]{1,0:T(8,128)(2,1)} %collective-permute-done.20.rest_1_), custom_call_target="tpu_custom_call" | custom-call | flops 188743680 | bytes 3000000 | tf_op jit(solution)/shard_map/wgrad/pallas_call | solution.py:379
  216.9 14.8 %collective-permute-done.26.rest_1_ = bf16[96,5120]{1,0:T(8,128)(2,1)} collective-permute-done((bf16[96,5120]{1,0:T(8,128)(2,1)}, bf16[96,5120]{1,0:T(8,128)(2,1)}, u32[]{:S(2)}, u32[]{:S(2)}) %collective-permute-start.26) | collective-permute-done | bytes 983072 | tf_op jit(solution)/shard_map/ppermute | solution.py:28
  231.7 4.1 %wgrad.23 = bf16[96,5120]{1,0:T(8,128)(2,1)} custom-call(bf16[384,192]{1,0:T(8,128)(2,1)S(1)} %get-tuple-element.57.left_ref, bf16[192,5120]{1,0:T(8,128)(2,1)S(1)} %copy-done.2, bf16[96,5120]{1,0:T(8,128)(2,1)} %collective-permute-done.24.rest_0_, bf16[96,5120]{1,0:T(8,128)(2,1)} %collective-permute-done.26.rest_1_), custom_call_target="tpu_custom_call" | custom-call | flops 188743680 | bytes 3000000 | tf_op jit(solution)/shard_map/wgrad/pallas_call | solution.py:379
  235.8 3.5 %final.1 = (bf16[128,5120]{1,0:T(8,128)(2,1)}, bf16[6,128]{1,0:T(8,128)(2,1)}) custom-call(s32[6,128]{1,0:T(8,128)S(1)} %bitcast.27, bf16[128,2048]{1,0:T(8,128)(2,1)} %bitcast.10.in_ref), custom_call_target="tpu_custom_call" | custom-call | flops 600000000 | bytes 2000000 | tf_op jit(solution)/shard_map/final/pallas_call | solution.py:48
  (92 shorter events, 11.5 us)
Async XLA Ops:
  0.6 35.1 %collective-permute-start.3 = (bf16[96,5120]{1,0:T(8,128)(2,1)}, bf16[96,5120]{1,0:T(8,128)(2,1)S(1)}, u32[]{:S(2)}, u32[]{:S(2)}) collective-permute-start(bf16[96,5120]{1,0:T(8,128)(2,1)} %bitcast.15), channel_id=1, source_target_pairs={{0,32},{16,48},{32,0},{48,16},{64,96},{80,112},{96,64},{112,80},{1... | collective-permute-start | bytes 2949128 | tf_op jit(solution)/shard_map/ppermute | solution.py:28
  2.2 33.6 %collective-permute-start = (bf16[96,5120]{1,0:T(8,128)(2,1)}, bf16[96,5120]{1,0:T(8,128)(2,1)S(1)}, u32[]{:S(2)}, u32[]{:S(2)}) collective-permute-start(bf16[96,5120]{1,0:T(8,128)(2,1)} %bitcast.16), channel_id=1, source_target_pairs={{0,16},{16,0},{32,48},{48,32},{64,80},{80,64},{96,112},{112,96},{1... | collective-permute-start | bytes 2949128 | tf_op jit(solution)/shard_map/ppermute | solution.py:28
  2.2 33.6 %collective-permute-start.1 = (bf16[96,5120]{1,0:T(8,128)(2,1)}, bf16[96,5120]{1,0:T(8,128)(2,1)}, u32[]{:S(2)}, u32[]{:S(2)}) collective-permute-start(bf16[96,5120]{1,0:T(8,128)(2,1)} %bitcast.29), channel_id=1, source_target_pairs={{0,16},{16,0},{32,48},{48,32},{64,80},{80,64},{96,112},{112,96},{1... | collective-permute-start | bytes 2949128 | tf_op jit(solution)/shard_map/ppermute | solution.py:28
  2.7 33.1 %collective-permute-start.2 = (bf16[96,5120]{1,0:T(8,128)(2,1)}, bf16[96,5120]{1,0:T(8,128)(2,1)S(1)}, u32[]{:S(2)}, u32[]{:S(2)}) collective-permute-start(bf16[96,5120]{1,0:T(8,128)(2,1)} %bitcast.20), channel_id=1, source_target_pairs={{0,16},{16,0},{32,48},{48,32},{64,80},{80,64},{96,112},{112,96},{1... | collective-permute-start | bytes 2949128 | tf_op jit(solution)/shard_map/ppermute | solution.py:28
  2.7 1.3 copy-start.21
  4.7 12.4 %copy-start.24 = (s32[128,6]{0,1:T(8,128)S(1)}, s32[128,6]{0,1:T(8,128)}, u32[]{:S(2)}) copy-start(s32[128,6]{0,1:T(8,128)} %param.10) | copy-start | bytes 9220
  4.7 12.4 %copy-start.25 = (bf16[128,6]{0,1:T(8,128)(2,1)S(1)}, bf16[128,6]{0,1:T(8,128)(2,1)}, u32[]{:S(2)}) copy-start(bf16[128,6]{0,1:T(8,128)(2,1)} %param.9) | copy-start | bytes 4612
  6.8 28.2 %all-to-all-start = ((bf16[16,8,1920]{2,1,0:T(8,128)(2,1)}), bf16[16,8,1920]{2,1,0:T(8,128)(2,1)S(1)}, u32[]{:S(2)}, u32[]{:S(2)}) async-start(bf16[16,8,1920]{2,1,0:T(8,128)(2,1)} %bitcast.24), calls=%async_computation | async-start | bytes 983040 | tf_op jit(solution)/shard_map/all_to_all | solution.py:306
  17.1 1.3 copy-start.22
  35.8 68.5 %copy-start.4 = (bf16[96,5120]{1,0:T(8,128)(2,1)}, bf16[96,5120]{1,0:T(8,128)(2,1)S(1)}, u32[]{:S(2)}) copy-start(bf16[96,5120]{1,0:T(8,128)(2,1)S(1)} %collective-permute-done.3.refs_6_.refs_5_) | copy-start | bytes 2949124
  35.8 68.5 %copy-start.6 = (bf16[96,5120]{1,0:T(8,128)(2,1)}, bf16[96,5120]{1,0:T(8,128)(2,1)S(1)}, u32[]{:S(2)}) copy-start(bf16[96,5120]{1,0:T(8,128)(2,1)S(1)} %collective-permute-done.refs_5_.refs_4_) | copy-start | bytes 2949124
  36.8 68.4 %copy-start.3 = (bf16[1,96,5120]{2,1,0:T(8,128)(2,1)S(1)}, bf16[1,96,5120]{2,1,0:T(8,128)(2,1)}, u32[]{:S(2)}) copy-start(bf16[1,96,5120]{2,1,0:T(8,128)(2,1)} %param.11) | copy-start | bytes 2949124
  36.8 29.3 %all-to-all-start.1 = ((bf16[16,8,2048]{2,1,0:T(8,128)(2,1)}), bf16[16,8,2048]{2,1,0:T(8,128)(2,1)}, u32[]{:S(2)}, u32[]{:S(2)}) async-start(bf16[16,8,2048]{2,1,0:T(8,128)(2,1)} %bitcast.23), calls=%async_computation.1 | async-start | bytes 1048576 | tf_op jit(solution)/shard_map/all_to_all | solution.py:306
  41.2 24.9 %collective-permute-start.6 = (bf16[96,5120]{1,0:T(8,128)(2,1)}, bf16[96,5120]{1,0:T(8,128)(2,1)}, u32[]{:S(2)}, u32[]{:S(2)}) collective-permute-start(bf16[96,5120]{1,0:T(8,128)(2,1)} %bitcast.30), channel_id=1, source_target_pairs={{0,32},{16,48},{32,0},{48,16},{64,96},{80,112},{96,64},{112,80},{1... | collective-permute-start | bytes 2949128 | tf_op jit(solution)/shard_map/ppermute | solution.py:28
  41.8 24.3 %collective-permute-start.7 = (bf16[96,5120]{1,0:T(8,128)(2,1)S(1)}, bf16[96,5120]{1,0:T(8,128)(2,1)}, u32[]{:S(2)}, u32[]{:S(2)}) collective-permute-start(bf16[96,5120]{1,0:T(8,128)(2,1)S(1)} %collective-permute-done.3.refs_6_.refs_5_), channel_id=1, source_target_pairs={{0,16},{16,0},{32,48},{48,32},{64,80},{80,64},{96,112},{112,96},{1... | collective-permute-start | bytes 2949128 | tf_op jit(solution)/shard_map/ppermute | solution.py:28
  43.1 21.4 %collective-permute-start.5 = (bf16[48,5120]{1,0:T(8,128)(2,1)S(1)}, bf16[48,5120]{1,0:T(8,128)(2,1)S(1)}, u32[]{:S(2)}, u32[]{:S(2)}) collective-permute-start(bf16[48,5120]{1,0:T(8,128)(2,1)S(1)} %unpack_x.1.refs_0_), channel_id=1, source_target_pairs={{0,128},{16,144},{32,160},{48,176},{64,192},{80,208},{96,224},{112... | collective-permute-start | bytes 1474568 | tf_op jit(solution)/shard_map/ppermute | solution.py:28
  44.5 20.8 %collective-permute-start.4 = (bf16[48,5120]{1,0:T(8,128)(2,1)S(1)}, bf16[48,5120]{1,0:T(8,128)(2,1)S(1)}, u32[]{:S(2)}, u32[]{:S(2)}) collective-permute-start(bf16[48,5120]{1,0:T(8,128)(2,1)S(1)} %unpack_x.1.refs_0_), channel_id=1, source_target_pairs={{0,96},{16,112},{32,64},{48,80},{64,32},{80,48},{96,0},{112,16},{1... | collective-permute-start | bytes 1474568 | tf_op jit(solution)/shard_map/ppermute | solution.py:28
  66.1 39.1 %copy-start.9 = (bf16[48,5120]{1,0:T(8,128)(2,1)S(1)}, bf16[48,5120]{1,0:T(8,128)(2,1)}, u32[]{:S(2)}) copy-start(bf16[48,5120]{1,0:T(8,128)(2,1)} %copy-done.8) | copy-start | bytes 1474564
  66.1 39.1 %copy-start.17 = (bf16[48,5120]{1,0:T(8,128)(2,1)S(1)}, bf16[48,5120]{1,0:T(8,128)(2,1)}, u32[]{:S(2)}) copy-start(bf16[48,5120]{1,0:T(8,128)(2,1)} %copy-done.16) | copy-start | bytes 1474564
  66.1 22.7 %collective-permute-start.11 = (bf16[96,5120]{1,0:T(8,128)(2,1)}, bf16[96,5120]{1,0:T(8,128)(2,1)S(1)}, u32[]{:S(2)}, u32[]{:S(2)}) collective-permute-start(bf16[96,5120]{1,0:T(8,128)(2,1)} %bitcast.21), channel_id=1, source_target_pairs={{0,32},{16,48},{32,0},{48,16},{64,96},{80,112},{96,64},{112,80},{1... | collective-permute-start | bytes 2949128 | tf_op jit(solution)/shard_map/ppermute | solution.py:28
  66.8 37.5 %collective-permute-start.14 = (bf16[96,5120]{1,0:T(8,128)(2,1)}, bf16[96,5120]{1,0:T(8,128)(2,1)S(1)}, u32[]{:S(2)}, u32[]{:S(2)}) collective-permute-start(bf16[96,5120]{1,0:T(8,128)(2,1)} %collective-permute-done.6.refs_10_.refs_9_), channel_id=1, source_target_pairs={{0,16},{16,0},{32,48},{48,32},{64,80},{80,64},{96,112},{112,96},{1... | collective-permute-start | bytes 2949128 | tf_op jit(solution)/shard_map/ppermute | solution.py:28
  68.2 58.3 %copy-start.12 = (bf16[1,96,5120]{2,1,0:T(8,128)(2,1)S(1)}, bf16[1,96,5120]{2,1,0:T(8,128)(2,1)}, u32[]{:S(2)}) copy-start(bf16[1,96,5120]{2,1,0:T(8,128)(2,1)} %param.13) | copy-start | bytes 2949124
  68.2 58.3 %copy-start.14 = (bf16[96,5120]{1,0:T(8,128)(2,1)S(1)}, bf16[96,5120]{1,0:T(8,128)(2,1)}, u32[]{:S(2)}) copy-start(bf16[96,5120]{1,0:T(8,128)(2,1)} %copy-done.13) | copy-start | bytes 2949124
  68.2 23.9 %collective-permute-start.9 = (bf16[48,5248]{1,0:T(8,128)(2,1)S(1)}, bf16[48,5248]{1,0:T(8,128)(2,1)S(1)}, u32[]{:S(2)}, u32[]{:S(2)}) collective-permute-start(bf16[48,5248]{1,0:T(8,128)(2,1)S(1)} %unpack_y.1.refs_0_), channel_id=1, source_target_pairs={{0,128},{16,144},{32,160},{48,176},{64,192},{80,208},{96,224},{112... | collective-permute-start | bytes 1511432 | tf_op jit(solution)/shard_map/ppermute | solution.py:28
  88.8 27.3 %copy-start.27 = (bf16[96,5120]{1,0:T(8,128)(2,1)}, bf16[96,5120]{1,0:T(8,128)(2,1)S(1)}, u32[]{:S(2)}) copy-start(bf16[96,5120]{1,0:T(8,128)(2,1)S(1)} %collective-permute-done.11.refs_6_) | copy-start | bytes 2949124
  88.8 36.7 %collective-permute-start.12 = (bf16[96,5120]{1,0:T(8,128)(2,1)S(1)}, bf16[96,5120]{1,0:T(8,128)(2,1)S(1)}, u32[]{:S(2)}, u32[]{:S(2)}) collective-permute-start(bf16[96,5120]{1,0:T(8,128)(2,1)S(1)} %collective-permute-done.11.refs_6_), channel_id=1, source_target_pairs={{0,16},{16,0},{32,48},{48,32},{64,80},{80,64},{96,112},{112,96},{1... | collective-permute-start | bytes 2949128 | tf_op jit(solution)/shard_map/ppermute | solution.py:28
  88.8 15.4 %collective-permute-start.13 = (bf16[48,5120]{1,0:T(8,128)(2,1)}, bf16[48,5120]{1,0:T(8,128)(2,1)S(1)}, u32[]{:S(2)}, u32[]{:S(2)}) collective-permute-start(bf16[48,5120]{1,0:T(8,128)(2,1)} %copy-done.16), channel_id=1, source_target_pairs={{0,96},{16,112},{32,64},{48,80},{64,32},{80,48},{96,0},{112,16},{1... | collective-permute-start | bytes 1474568 | tf_op jit(solution)/shard_map/ppermute | solution.py:28
  90.8 25.3 %collective-permute-start.8 = (bf16[48,5248]{1,0:T(8,128)(2,1)S(1)}, bf16[48,5248]{1,0:T(8,128)(2,1)S(1)}, u32[]{:S(2)}, u32[]{:S(2)}) collective-permute-start(bf16[48,5248]{1,0:T(8,128)(2,1)S(1)} %unpack_y.1.refs_0_), channel_id=1, source_target_pairs={{0,96},{16,112},{32,64},{48,80},{64,32},{80,48},{96,0},{112,16},{1... | collective-permute-start | bytes 1511432 | tf_op jit(solution)/shard_map/ppermute | solution.py:28
  92.1 33.4 %collective-permute-start.10 = (bf16[48,5248]{1,0:T(8,128)(2,1)S(1)}, bf16[48,5248]{1,0:T(8,128)(2,1)S(1)}, u32[]{:S(2)}, u32[]{:S(2)}) collective-permute-start(bf16[48,5248]{1,0:T(8,128)(2,1)S(1)} %collective-permute-done.9.refs_2_), channel_id=1, source_target_pairs={{0,96},{16,112},{32,64},{48,80},{64,32},{80,48},{96,0},{112,16},{1... | collective-permute-start | bytes 1511432 | tf_op jit(solution)/shard_map/ppermute | solution.py:28
  105.2 1.0 copy-start.19
  126.4 7.3 %copy-start = (bf16[192,5120]{1,0:T(8,128)(2,1)S(1)}, bf16[192,5120]{1,0:T(8,128)(2,1)}, u32[]{:S(2)}) copy-start(bf16[192,5120]{1,0:T(8,128)(2,1)} %get-tuple-element.56.rows_ref) | copy-start | bytes 5898244
  133.7 1.3 copy-start.5
  133.8 1.5 copy-start.7
  134.9 24.8 %collective-permute-start.22 = (bf16[96,5120]{1,0:T(8,128)(2,1)S(1)}, bf16[96,5120]{1,0:T(8,128)(2,1)S(1)}, u32[]{:S(2)}, u32[]{:S(2)}) collective-permute-start(bf16[96,5120]{1,0:T(8,128)(2,1)S(1)} %wgrad.17), channel_id=1, source_target_pairs={{0,16},{16,0},{32,48},{48,32},{64,80},{80,64},{96,112},{112,96},{1... | collective-permute-start | bytes 2949128 | tf_op jit(solution)/shard_map/ppermute | solution.py:28
  142.5 3.3 %copy-start.1 = (bf16[192,5120]{1,0:T(8,128)(2,1)S(1)}, bf16[192,5120]{1,0:T(8,128)(2,1)}, u32[]{:S(2)}) copy-start(bf16[192,5120]{1,0:T(8,128)(2,1)} %get-tuple-element.58.rows_ref) | copy-start | bytes 5898244
  142.5 14.9 %collective-permute-start.16 = (bf16[48,5248]{1,0:T(8,128)(2,1)S(1)}, bf16[48,5248]{1,0:T(8,128)(2,1)S(1)}, u32[]{:S(2)}, u32[]{:S(2)}) collective-permute-start(bf16[48,5248]{1,0:T(8,128)(2,1)S(1)} %get-tuple-element.53), channel_id=1, source_target_pairs={{0,96},{16,112},{32,64},{48,80},{64,32},{80,48},{96,0},{112,16},{1... | collective-permute-start | bytes 1511432 | tf_op jit(solution)/shard_map/ppermute | solution.py:28
  145.7 21.1 %collective-permute-start.19 = (bf16[96,5120]{1,0:T(8,128)(2,1)S(1)}, bf16[96,5120]{1,0:T(8,128)(2,1)S(1)}, u32[]{:S(2)}, u32[]{:S(2)}) collective-permute-start(bf16[96,5120]{1,0:T(8,128)(2,1)S(1)} %wgrad.13), channel_id=1, source_target_pairs={{0,16},{16,0},{32,48},{48,32},{64,80},{80,64},{96,112},{112,96},{1... | collective-permute-start | bytes 2949128 | tf_op jit(solution)/shard_map/ppermute | solution.py:28
  146.9 24.5 %collective-permute-start.25 = (bf16[96,5120]{1,0:T(8,128)(2,1)S(1)}, bf16[96,5120]{1,0:T(8,128)(2,1)S(1)}, u32[]{:S(2)}, u32[]{:S(2)}) collective-permute-start(bf16[96,5120]{1,0:T(8,128)(2,1)S(1)} %wgrad.21), channel_id=1, source_target_pairs={{0,16},{16,0},{32,48},{48,32},{64,80},{80,64},{96,112},{112,96},{1... | collective-permute-start | bytes 2949128 | tf_op jit(solution)/shard_map/ppermute | solution.py:28
  148.6 25.2 %collective-permute-start.21 = (bf16[96,5120]{1,0:T(8,128)(2,1)S(1)}, bf16[96,5120]{1,0:T(8,128)(2,1)S(1)}, u32[]{:S(2)}, u32[]{:S(2)}) collective-permute-start(bf16[96,5120]{1,0:T(8,128)(2,1)S(1)} %wgrad.16), channel_id=1, source_target_pairs={{0,16},{16,0},{32,48},{48,32},{64,80},{80,64},{96,112},{112,96},{1... | collective-permute-start | bytes 2949128 | tf_op jit(solution)/shard_map/ppermute | solution.py:28
  157.4 14.0 %collective-permute-start.15 = (bf16[48,5248]{1,0:T(8,128)(2,1)S(1)}, bf16[48,5248]{1,0:T(8,128)(2,1)S(1)}, u32[]{:S(2)}, u32[]{:S(2)}) collective-permute-start(bf16[48,5248]{1,0:T(8,128)(2,1)S(1)} %get-tuple-element.51), channel_id=1, source_target_pairs={{0,96},{16,112},{32,64},{48,80},{64,32},{80,48},{96,0},{112,16},{1... | collective-permute-start | bytes 1511432 | tf_op jit(solution)/shard_map/ppermute | solution.py:28
  159.7 14.5 %collective-permute-start.17 = (bf16[48,5248]{1,0:T(8,128)(2,1)S(1)}, bf16[48,5248]{1,0:T(8,128)(2,1)S(1)}, u32[]{:S(2)}, u32[]{:S(2)}) collective-permute-start(bf16[48,5248]{1,0:T(8,128)(2,1)S(1)} %join.1), channel_id=1, source_target_pairs={{0,128},{16,144},{32,160},{48,176},{64,192},{80,208},{96,224},{112... | collective-permute-start | bytes 1511432 | tf_op jit(solution)/shard_map/ppermute | solution.py:28
  166.7 25.0 %collective-permute-start.23 = (bf16[96,5120]{1,0:T(8,128)(2,1)}, bf16[96,5120]{1,0:T(8,128)(2,1)}, u32[]{:S(2)}, u32[]{:S(2)}) collective-permute-start(bf16[96,5120]{1,0:T(8,128)(2,1)} %wgrad.18), channel_id=1, source_target_pairs={{0,32},{16,48},{32,0},{48,16},{64,96},{80,112},{96,64},{112,80},{1... | collective-permute-start | bytes 2949128 | tf_op jit(solution)/shard_map/ppermute | solution.py:28
  171.5 24.2 %collective-permute-start.18 = (bf16[96,5120]{1,0:T(8,128)(2,1)}, bf16[96,5120]{1,0:T(8,128)(2,1)}, u32[]{:S(2)}, u32[]{:S(2)}) collective-permute-start(bf16[96,5120]{1,0:T(8,128)(2,1)} %wgrad.12), channel_id=1, source_target_pairs={{0,16},{16,0},{32,48},{48,32},{64,80},{80,64},{96,112},{112,96},{1... | collective-permute-start | bytes 2949128 | tf_op jit(solution)/shard_map/ppermute | solution.py:28
  171.5 41.4 %collective-permute-start.20 = (bf16[96,5120]{1,0:T(8,128)(2,1)}, bf16[96,5120]{1,0:T(8,128)(2,1)}, u32[]{:S(2)}, u32[]{:S(2)}) collective-permute-start(bf16[96,5120]{1,0:T(8,128)(2,1)} %wgrad.14), channel_id=1, source_target_pairs={{0,32},{16,48},{32,0},{48,16},{64,96},{80,112},{96,64},{112,80},{1... | collective-permute-start | bytes 2949128 | tf_op jit(solution)/shard_map/ppermute | solution.py:28
  173.8 43.1 %collective-permute-start.24 = (bf16[96,5120]{1,0:T(8,128)(2,1)}, bf16[96,5120]{1,0:T(8,128)(2,1)}, u32[]{:S(2)}, u32[]{:S(2)}) collective-permute-start(bf16[96,5120]{1,0:T(8,128)(2,1)} %wgrad.20), channel_id=1, source_target_pairs={{0,16},{16,0},{32,48},{48,32},{64,80},{80,64},{96,112},{112,96},{1... | collective-permute-start | bytes 2949128 | tf_op jit(solution)/shard_map/ppermute | solution.py:28
  174.3 57.5 %collective-permute-start.26 = (bf16[96,5120]{1,0:T(8,128)(2,1)}, bf16[96,5120]{1,0:T(8,128)(2,1)}, u32[]{:S(2)}, u32[]{:S(2)}) collective-permute-start(bf16[96,5120]{1,0:T(8,128)(2,1)} %wgrad.22), channel_id=1, source_target_pairs={{0,32},{16,48},{32,0},{48,16},{64,96},{80,112},{96,64},{112,80},{1... | collective-permute-start | bytes 2949128 | tf_op jit(solution)/shard_map/ppermute | solution.py:28
  177.3 58.5 %all-to-all-start.2 = ((bf16[16,8,2048]{2,1,0:T(8,128)(2,1)}), bf16[16,8,2048]{2,1,0:T(8,128)(2,1)}, u32[]{:S(2)}, u32[]{:S(2)}) async-start(bf16[16,8,2048]{2,1,0:T(8,128)(2,1)} %bitcast.9), calls=%async_computation.2 | async-start | bytes 1048576 | tf_op jit(solution)/shard_map/all_to_all | solution.py:306
  195.6 36.1 %copy-start.2 = (bf16[192,5120]{1,0:T(8,128)(2,1)S(1)}, bf16[192,5120]{1,0:T(8,128)(2,1)}, u32[]{:S(2)}) copy-start(bf16[192,5120]{1,0:T(8,128)(2,1)} %get-tuple-element.58.rows_ref) | copy-start | bytes 5898244
  (11 other events, 9.3 us)

commit v2 on v1

--- a/solution.py
+++ b/solution.py
@@ -18,8 +18,8 @@
     return [(i, (i & 9) | (move((i >> 1) & 3) << 1)) for i in range(16)]
 
 
-ROW_SWAP = chip_perm(lambda x: 3 - x)
-PAIR_SWAP = chip_perm(lambda x: x ^ 1)
+X_UP = chip_perm(lambda x: (x + 1) % 4)
+X_DOWN = chip_perm(lambda x: (x + 3) % 4)
 Z_SWAP = [(i, i ^ 8) for i in range(16)]
 C_SWAP = [(i, i ^ 1) for i in range(16)]
 
@@ -118,55 +118,75 @@
             ).astype(BF16)
 
 
-def fetch(copies):
-    for c in copies:
-        c.start()
-    for c in copies:
-        c.wait()
-
-
-def product(out_ref, left, right, step=640):
-    out_ref[...] = jnp.zeros(out_ref.shape, F32)
-
-    def body(n, carry):
-        cols = pl.ds(pl.multiple_of(n * step, step), step)
-        out_ref[...] += dot_nt(left[:, cols], right[:, cols])
-        return carry
-
-    lax.fori_loop(0, left.shape[1] // step, body, 0)
-
-
-def stacked(sources, target, sems, first):
-    rows = sources[0].shape[0]
+BLOCKS = 4
+
+
+def stacked(sources, target, sems, n):
+    rows, width = sources[0].shape
+    step = (width // BLOCKS) // LANES * LANES
+    start = n * step
+    size = step if n < BLOCKS - 1 else width - start
     return [
-        pltpu.make_async_copy(a, target.at[pl.ds(k * rows, rows)], sems.at[first + k])
+        pltpu.make_async_copy(
+            a.at[:, pl.ds(start, size)],
+            target.at[pl.ds(k * rows, rows), pl.ds(start, size)],
+            sems.at[k * BLOCKS + n],
+        )
         for k, a in enumerate(sources)
     ]
 
 
+def ready(*copies):
+    for group in copies:
+        for c in group:
+            c.wait()
+
+
 def pre_kernel(*refs):
-    xs, gs, us = refs[0:4], refs[4:8], refs[8:12]
-    gate_ref, up_ref, x_out, g_all, u_all, sems = refs[12:]
-    first = stacked(xs, x_out, sems, 0) + stacked(gs, g_all, sems, 4)
-    second = stacked(us, u_all, sems, 8)
-    for c in first + second:
-        c.start()
-    for c in first:
-        c.wait()
-    product(gate_ref, g_all, x_out)
-    for c in second:
-        c.wait()
-    product(up_ref, u_all, x_out)
+    xs, ws = refs[0:8], refs[8:12]
+    gate_ref, up_ref, x_out, w_all, x_sems, w_sems = refs[12:]
+    x_plan = [stacked(xs, x_out, x_sems, n) for n in range(BLOCKS)]
+    w_plan = [stacked(ws, w_all, w_sems, n) for n in range(BLOCKS)]
+    for n in range(BLOCKS):
+        for c in w_plan[n] + x_plan[n]:
+            c.start()
+    step = x_out.shape[1] // BLOCKS
+    half = w_all.shape[0] // 2
+    for n in range(BLOCKS):
+        ready(w_plan[n], x_plan[n])
+        cols = slice(n * step, (n + 1) * step)
+        for out_ref, first in ((gate_ref, 0), (up_ref, half)):
+            got = dot_nt(w_all[first : first + half, cols], x_out[:, cols])
+            if n == 0:
+                out_ref[...] = got
+            else:
+                out_ref[...] += got
 
 
 def main_kernel(*refs):
-    ys, ds, (gate_ref, up_ref) = refs[0:4], refs[4:8], refs[8:10]
-    dg_ref, du_ref, hid_ref, py_ref, tail_ref, y_all, d_all, acc, sems = refs[10:]
-    copies = stacked(ds, d_all, sems, 0) + stacked(ys, y_all, sems, 4)
-    fetch(copies)
-    width = d_all.shape[1]
-    total = y_all.shape[0]
-    product(acc, d_all, y_all)
+    ys, ds, ws, (gate_ref, up_ref) = refs[0:8], refs[8:10], refs[10:14], refs[14:16]
+    outs, (dg_ref, du_ref, hid_ref, py_ref) = refs[16:24], refs[24:28]
+    y_all, d_all, w_all, acc, y_sems, d_sems, w_sems = refs[28:]
+    y_plan = [stacked(ys, y_all, y_sems, n) for n in range(BLOCKS)]
+    d_plan = [stacked(ds, d_all, d_sems, n) for n in range(BLOCKS)]
+    w_plan = [stacked(ws, w_all, w_sems, n) for n in range(BLOCKS)]
+    for n in range(BLOCKS):
+        for c in d_plan[n] + y_plan[n]:
+            c.start()
+    for n in range(BLOCKS):
+        for c in w_plan[n]:
+            c.start()
+    width, total = d_all.shape[1], y_all.shape[0]
+    rows = total // 8
+    step = width // BLOCKS
+    for n in range(BLOCKS):
+        ready(d_plan[n], y_plan[n])
+        cols = slice(n * step, (n + 1) * step)
+        got = dot_nt(d_all[:, cols], y_all[:, cols])
+        if n == 0:
+            acc[...] = got
+        else:
+            acc[...] += got
     back = acc[...]
     probs = y_all[:, width:].astype(F32)
     prob = jnp.transpose(probs)[0:1, :]
@@ -175,44 +195,30 @@
     hidden = gate * sig * up
     part = jnp.sum(hidden * back, axis=0, keepdims=True)
     scaled = prob * back
-    dg_ref[...] = (scaled * up * sig * (1.0 + gate * (1.0 - sig))).astype(BF16)
-    du_ref[...] = (scaled * gate * sig).astype(BF16)
+    d_gate = scaled * up * sig * (1.0 + gate * (1.0 - sig))
+    d_up = scaled * gate * sig
     hid_ref[...] = hidden.astype(BF16)
-    py_ref[...] = (probs[:, 0:1] * y_all[:, 0:width].astype(F32)).astype(BF16)
+    dg_ref[...] = d_gate.astype(BF16)
+    du_ref[...] = d_up.astype(BF16)
+    both = jnp.transpose(jnp.concatenate([d_gate, d_up], axis=0)).astype(BF16)
     high = part.astype(BF16).astype(F32)
-    low = part - high
     tail = jnp.where(
         iota((LANES, total), 0) < LANES // 2,
         jnp.broadcast_to(high, (LANES, total)),
-        jnp.broadcast_to(low, (LANES, total)),
+        jnp.broadcast_to(part - high, (LANES, total)),
     )
-    tail_ref[...] = jnp.transpose(tail).astype(BF16)
-
-
-def back_kernel(*refs):
-    dg_ref, du_ref, tail_ref = refs[0:3]
-    gs, us, outs = refs[3:7], refs[7:11], refs[11:15]
-    g_all, u_all, sems = refs[15:]
-    copies = stacked(gs, g_all, sems, 0) + stacked(us, u_all, sems, 4)
-    for c in copies:
-        c.start()
-    rows, width = outs[0].shape[0], g_all.shape[1]
-    for k in range(4):
-        outs[k][:, width:] = tail_ref[k * rows : (k + 1) * rows, :]
-    d_gate = jnp.transpose(dg_ref[...].astype(F32)).astype(BF16)
-    d_up = jnp.transpose(du_ref[...].astype(F32)).astype(BF16)
-    for c in copies:
-        c.wait()
-    step = 640
-
-    def body(n, carry):
-        cols = pl.ds(pl.multiple_of(n * step, step), step)
-        got = (dot(d_gate, g_all[:, cols]) + dot(d_up, u_all[:, cols])).astype(BF16)
-        for k in range(4):
-            outs[k][:, cols] = got[k * rows : (k + 1) * rows, :]
-        return carry
-
-    lax.fori_loop(0, width // step, body, 0)
+    tail = jnp.transpose(tail).astype(BF16)
+    for k in range(8):
+        outs[k][:, width:] = tail[k * rows : (k + 1) * rows, :]
+    prob_col = probs[:, 0:1]
+    for n in range(BLOCKS):
+        ready(w_plan[n])
+        for m in range(2):
+            cols = slice(n * step + m * step // 2, n * step + (m + 1) * step // 2)
+            got = dot(both, w_all[:, cols]).astype(BF16)
+            for k in range(8):
+                outs[k][:, cols] = got[k * rows : (k + 1) * rows, :]
+            py_ref[:, cols] = (prob_col * y_all[:, cols].astype(F32)).astype(BF16)
 
 
 def wgrad_kernel(left_ref, rows_ref, *rest, first):
@@ -291,7 +297,7 @@
     group = width // QN
     wide = width + LANES
     rows = CAP * 16
-    total = 4 * rows
+    total = 8 * rows
     g, u, d = w_gate[0], w_up[0], w_down[0]
     hid = g.shape[0]
     ids_t, probs_t = expert_ids.T, gate_probs.T
@@ -299,7 +305,7 @@
     any_spec, vmem = pl.BlockSpec(memory_space=pl.ANY), pl.BlockSpec(memory_space=pltpu.VMEM)
     dma = pltpu.SemaphoreType.DMA
     together = lax.optimization_barrier
-    work = 2 * total * width * 4 * hid
+    work = 2 * total * width * 2 * hid
 
     def exchange(a):
         a = a.reshape(16, QN, a.shape[1])
@@ -320,56 +326,56 @@
         "send_x",
         cost=(6 * 10**8, 2 * 10**6),
     )(ids_t, tokens)
+    core_g, core_u, core_d = hop(g, C_SWAP), hop(u, C_SWAP), hop(d, C_SWAP)
+    got_x, core_g, core_u, core_d = together((exchange(send_x), core_g, core_u, core_d))
+    x = unpack(got_x, width, "unpack_x")
+    left, right, oth = hop(x, X_UP), hop(x, X_DOWN), hop(x, Z_SWAP)
+    x_now, cot_now = together((x, cotangent))
     send_y = call(
         functools.partial(send_kernel, with_p=True),
         shape((LANES, CAP * group + LANES), BF16),
         "send_y",
         cost=(6 * 10**8, 2 * 10**6),
-    )(ids_t, probs_t, cotangent)
-
-    core_g, core_u, core_d = hop(g, C_SWAP), hop(u, C_SWAP), hop(d, C_SWAP)
-    pair_g = hop(g, PAIR_SWAP)
-    got_x, core_g, core_u, core_d, pair_g, send_y, u_next = together(
-        (exchange(send_x), core_g, core_u, core_d, pair_g, send_y, u)
-    )
+    )(ids_t, probs_t, cot_now)
     got_y = exchange(send_y)
-    x = unpack(got_x, width, "unpack_x")
-    x_row, x_oth = hop(x, ROW_SWAP), hop(x, Z_SWAP)
-    pair_u = hop(u_next, PAIR_SWAP)
-    cross_g = hop(pair_g, C_SWAP)
-    got_y, x_row, x_oth, pair_u, cross_g, d_next = together(
-        (got_y, x_row, x_oth, pair_u, cross_g, d)
-    )
-    pair_d = hop(d_next, PAIR_SWAP)
-    cross_u = hop(pair_u, C_SWAP)
+    left, right, oth = together((left, right, oth))
+    far, o_right, o_left = hop(left, X_UP), hop(oth, X_DOWN), hop(oth, X_UP)
+    far, o_right, got_y = together((far, o_right, got_y))
+    o_far = hop(o_right, X_DOWN)
     y = unpack(got_y, wide, "unpack_y")
-    x_oth_row = hop(x_oth, ROW_SWAP)
-    y_oth, y_row = hop(y, Z_SWAP), hop(y, ROW_SWAP)
-    y_oth_row = hop(y_oth, ROW_SWAP)
-    cross_d = hop(pair_d, C_SWAP)
-    gs, us = (g, core_g, pair_g, cross_g), (u, core_u, pair_u, cross_u)
+    y_left, y_right, y_oth = hop(y, X_UP), hop(y, X_DOWN), hop(y, Z_SWAP)
     gate, up, x_all = call(
         pre_kernel,
-        [shape((4 * hid, total), F32)] * 2 + [shape((total, width), BF16)],
+        [shape((2 * hid, total), F32)] * 2 + [shape((total, width), BF16)],
         "pre",
-        scratch=[pltpu.VMEM((4 * hid, width), BF16)] * 2 + [dma((12,))],
+        scratch=[pltpu.VMEM((4 * hid, width), BF16), dma((32,)), dma((16,))],
         specs=[any_spec] * 12,
         cost=(2 * work, 10 * 10**6),
-    )(x, x_row, x_oth, x_oth_row, *gs, *us)
-    d_gate, d_up, hidden, py, tail = call(
+    )(x, left, far, right, oth, o_left, o_far, o_right, g, core_g, u, core_u)
+    y_left, y_right, y_oth, gate = together((y_left, y_right, y_oth, gate))
+    y_far, yo_right, yo_left = hop(y_left, X_UP), hop(y_oth, X_DOWN), hop(y_oth, X_UP)
+    yo_far = hop(yo_right, X_DOWN)
+    *parts, d_gate, d_up, hidden, py = call(
         main_kernel,
-        [shape((4 * hid, total), BF16)] * 3
-        + [shape((total, width), BF16), shape((total, LANES), BF16)],
+        [shape((rows, wide), BF16)] * 8
+        + [shape((2 * hid, total), BF16)] * 3
+        + [shape((total, width), BF16)],
         "main",
         scratch=[
             pltpu.VMEM((total, wide), BF16),
+            pltpu.VMEM((2 * hid, width), BF16),
             pltpu.VMEM((4 * hid, width), BF16),
-            pltpu.VMEM((4 * hid, total), F32),
+            pltpu.VMEM((2 * hid, total), F32),
+            dma((32,)),
             dma((8,)),
+            dma((16,)),
         ],
-        specs=[any_spec] * 8 + [vmem] * 2,
-        cost=(work, 8 * 10**6),
-    )(y, y_row, y_oth, y_oth_row, d, core_d, pair_d, cross_d, gate, up)
+        specs=[any_spec] * 14 + [vmem] * 2,
+        cost=(3 * work, 14 * 10**6),
+    )(
+        *(y, y_left, y_far, y_right, y_oth, yo_left, yo_far, yo_right),
+        *(d, core_d, g, core_g, u, core_u, gate, up),
+    )
 
     blocks = 4
 
@@ -401,43 +407,34 @@
             cost=(10**6, 10**6),
         )(*a)
 
-    cross = [hop(wgrad(hidden, py, 3), C_SWAP)]
-    own, row, oth, oth_row = call(
-        back_kernel,
-        [shape((rows, wide), BF16)] * 4,
-        "back",
-        scratch=[pltpu.VMEM((4 * hid, width), BF16)] * 2 + [dma((8,))],
-        specs=[vmem] * 3 + [any_spec] * 8,
-        cost=(2 * work, 10 * 10**6),
-    )(d_gate, d_up, tail, *gs, *us)
-    cross += [hop(wgrad(d_gate, x_all, 3), C_SWAP), hop(wgrad(d_up, x_all, 3), C_SWAP)]
-    far = hop(oth_row, ROW_SWAP)
-    pair_dw = hop(wgrad(hidden, py, 2, cross[0]), PAIR_SWAP)
-    oth = hop(join(oth, far), Z_SWAP)
-    row = hop(row, ROW_SWAP)
-    pair_gw = hop(wgrad(d_gate, x_all, 2, cross[1]), PAIR_SWAP)
-    pair_uw = hop(wgrad(d_up, x_all, 2, cross[2]), PAIR_SWAP)
-    side = [
-        hop(wgrad(hidden, py, 1), C_SWAP),
-        hop(wgrad(d_gate, x_all, 1), C_SWAP),
-        hop(wgrad(d_up, x_all, 1), C_SWAP),
-    ]
+    own, left, far, right, oth, o_left, o_far, o_right = parts
+    of, ol = hop(o_far, X_UP), hop(o_left, X_DOWN)
+    away = [wgrad(hidden, py, 1), wgrad(d_gate, x_all, 1), wgrad(d_up, x_all, 1)]
+    of, ol, far, *away = together((of, ol, far, *away))
+    o_r, f = hop(join(o_right, of), X_UP), hop(far, X_DOWN)
+    came = [hop(a, C_SWAP) for a in away]
+    o_r, f, right, hidden, d_gate, d_up, *came = together(
+        (o_r, f, right, hidden, d_gate, d_up, *came)
+    )
+    oz = hop(join(oth, ol, o_r), Z_SWAP)
+    lf, r = hop(join(left, f), X_DOWN), hop(right, X_UP)
+    d_grad = wgrad(hidden, py, 0, came[0])
+    g_grad = wgrad(d_gate, x_all, 0, came[1])
+    u_grad = wgrad(d_up, x_all, 0, came[2])
+    oz, lf, r, d_grad, g_grad, u_grad = together((oz, lf, r, d_grad, g_grad, u_grad))
     last = call(
         functools.partial(last_kernel, group=group),
         shape((LANES, CAP * group + LANES), BF16),
         "last",
         cost=(10**8, 3 * 10**6),
-    )(own, row, oth)
+    )(own, r, lf, oz)
     back = exchange(last)
-    d_grad = wgrad(hidden, py, 0, side[0], pair_dw)
-    g_grad = wgrad(d_gate, x_all, 0, side[1], pair_gw)
     token_grad, gate_t = call(
         functools.partial(final_kernel, group=group),
         [shape(tokens.shape, BF16), shape(ids_t.shape, BF16)],
         "final",
         cost=(6 * 10**8, 2 * 10**6),
     )(ids_t, back)
-    u_grad = wgrad(d_up, x_all, 0, side[2], pair_uw)
     return (token_grad, gate_t.T, g_grad[None], u_grad[None], d_grad[None])
 
 

time: 242 us -> 195 us (0.81)
  waiting for transfers between devices: 119 us -> 65.7 us
  blocking collectives: 0 us -> 49.4 us
  Pallas kernels: 61.4 us -> 37.9 us
  starting transfers between devices: 44.6 us -> 33.5 us
  local copies, waits for them, and re-layouts: 13.2 us -> 6.12 us
    all_to_all x0 -> x2, blocking collectives: none -> 49.4 us  [exchange(): a = lax.all_to_all(a, 'ep', split_axis=0, concat_axis=0, tiled=True)]
    ppermute x27, waiting for transfers between devices: 105 us -> 65.7 us  [hop(): return lax.ppermute(a, 'edp', perm)]
    all_to_all x3 -> x1, starting transfers between devices: 23.5 us -> 5.61 us  [exchange(): a = lax.all_to_all(a, 'ep', split_axis=0, concat_axis=0, tiled=True)]
    pallas_call x12 -> x6, Pallas kernels: 27.7 us -> 12.4 us  [wgrad(): pl.pallas_call(functools.partial(wgrad_kernel, first=place * hid), out_sh...]
    all_to_all x3 -> x1, waiting for transfers between devices: 14.4 us -> 0.01 us  [exchange(): a = lax.all_to_all(a, 'ep', split_axis=0, concat_axis=0, tiled=True)]
    pallas_call x10 -> x11, Pallas kernels: 33.7 us -> 25.5 us  [run(): pl.pallas_call(kernel, out_shape=outs, in_specs=[one] * len(args) if spec...]
    unnamed x58 -> x64, local copies, waits for them, and re-layouts: 13.2 us -> 6.12 us
    ppermute x27, starting transfers between devices: 21.2 us -> 27.9 us  [hop(): return lax.ppermute(a, 'edp', perm)]
  transfers between devices with their start and end apart: 30 -> 28, of which waited for: 10 -> 12; matrix products, arithmetic and copies ran while one was open for 0% -> 0% of each run, Pallas kernels for 21% -> 12%
where the time goes in v2:
time: 195 us; the launch traced here: 194 us
  waiting for transfers between devices  65.7 us (34%)
  blocking collectives  49.4 us (25%)
  Pallas kernels  37.9 us (19%)
  starting transfers between devices  33.5 us (17%)
  local copies, waits for them, and re-layouts  6.12 us (3%)
    ppermute x27, waiting for transfers between devices, hop(): return lax.ppermute(a, 'edp', perm)  65.7 us
    all_to_all x2, blocking collectives, exchange(): a = lax.all_to_all(a, 'ep', split_axis=0, concat_axis=0, tiled=True)  49.4 us
    ppermute x27, starting transfers between devices, hop(): return lax.ppermute(a, 'edp', perm)  27.9 us
    pallas_call x11, Pallas kernels, run(): pl.pallas_call(kernel, out_shape=outs, in_specs=[one] * len(args) if spec...  25.5 us
    pallas_call x6, Pallas kernels, wgrad(): pl.pallas_call(functools.partial(wgrad_kernel, first=place * hid), out_sh...  12.4 us
    unnamed x64, local copies, waits for them, and re-layouts  6.12 us
    all_to_all x1, starting transfers between devices, exchange(): a = lax.all_to_all(a, 'ep', split_axis=0, concat_axis=0, tiled=True)  5.61 us
  transfers between devices with their start and end apart: 28, of which 12 were waited for; matrix products, arithmetic and copies ran while one was open for 0% of the time, Pallas kernels for 12%

profile of v2, /device:TPU:32, one launch (start us, length us, event | category | flops | bytes accessed | tf_op | source)
XLA Modules:
  0.0 193.7 jit_solution(12874030373617710371)
XLA Ops:
  0.7 0.5 collective-permute-start.1
  1.3 1.3 copy-done.17
  2.6 0.7 copy-done.20
  3.3 1.3 send_x.1
  4.7 27.9 %all_to_all.15 = bf16[16,8,1920]{2,1,0:T(8,128)(2,1)S(1)} all-to-all(bf16[16,8,1920]{2,1,0:T(8,128)(2,1)S(1)} %bitcast.22), channel_id=1, replica_groups=mesh['edp'=16,'ep'=16] {'ep'}, dimensions={0} | all-to-all | bytes 983040 | tf_op jit(solution)/shard_map/all_to_all | solution.py:312
  33.0 2.8 %collective-permute-start.4 = (bf16[48,5120]{1,0:T(8,128)(2,1)S(1)}, bf16[48,5120]{1,0:T(8,128)(2,1)S(1)}, u32[]{:S(2)}, u32[]{:S(2)}) collective-permute-start(bf16[48,5120]{1,0:T(8,128)(2,1)S(1)} %unpack_x.1.refs_0_), channel_id=1, source_target_pairs={{0,96},{16,112},{32,0},{48,16},{64,32},{80,48},{96,64},{112,80},{1... | collective-permute-start | bytes 1474568 | tf_op jit(solution)/shard_map/ppermute | solution.py:28
  35.9 2.1 %send_y.1 = bf16[128,2048]{1,0:T(8,128)(2,1)} custom-call(s32[6,128]{1,0:T(8,128)S(1)} %bitcast.24, bf16[6,128]{1,0:T(8,128)(2,1)S(1)} %bitcast.26, bf16[128,5120]{1,0:T(8,128)(2,1)S(1)} %copy-done.18), custom_call_target="tpu_custom_call" | custom-call | flops 600000000 | bytes 2000000 | tf_op jit(solution)/shard_map/send_y/pallas_call | solution.py:48
  38.0 5.6 %all-to-all-start.1 = ((bf16[16,8,2048]{2,1,0:T(8,128)(2,1)}), bf16[16,8,2048]{2,1,0:T(8,128)(2,1)S(1)}, u32[]{:S(2)}, u32[]{:S(2)}) async-start(bf16[16,8,2048]{2,1,0:T(8,128)(2,1)} %bitcast.7), calls=%async_computation.1 | async-start | bytes 1048576 | tf_op jit(solution)/shard_map/all_to_all | solution.py:312
  43.6 3.5 %collective-permute-done.5.refs_4_ = bf16[48,5120]{1,0:T(8,128)(2,1)S(1)} collective-permute-done((bf16[48,5120]{1,0:T(8,128)(2,1)S(1)}, bf16[48,5120]{1,0:T(8,128)(2,1)S(1)}, u32[]{:S(2)}, u32[]{:S(2)}) %collective-permute-start.5) | collective-permute-done | bytes 491552 | tf_op jit(solution)/shard_map/ppermute | solution.py:28
  47.1 2.1 %collective-permute-done.3.refs_1_ = bf16[48,5120]{1,0:T(8,128)(2,1)S(1)} collective-permute-done((bf16[48,5120]{1,0:T(8,128)(2,1)S(1)}, bf16[48,5120]{1,0:T(8,128)(2,1)S(1)}, u32[]{:S(2)}, u32[]{:S(2)}) %collective-permute-start.3) | collective-permute-done | bytes 491552 | tf_op jit(solution)/shard_map/ppermute | solution.py:28
  49.3 0.5 collective-permute-start.6
  49.8 2.7 %collective-permute-start.7 = (bf16[48,5120]{1,0:T(8,128)(2,1)S(1)}, bf16[48,5120]{1,0:T(8,128)(2,1)}, u32[]{:S(2)}, u32[]{:S(2)}) collective-permute-start(bf16[48,5120]{1,0:T(8,128)(2,1)S(1)} %collective-permute-done.5.refs_4_), channel_id=1, source_target_pairs={{0,96},{16,112},{32,0},{48,16},{64,32},{80,48},{96,64},{112,80},{1... | collective-permute-start | bytes 1474568 | tf_op jit(solution)/shard_map/ppermute | solution.py:28
  52.5 12.1 %collective-permute-done.6.refs_2_ = bf16[48,5120]{1,0:T(8,128)(2,1)S(1)} collective-permute-done((bf16[48,5120]{1,0:T(8,128)(2,1)S(1)}, bf16[48,5120]{1,0:T(8,128)(2,1)S(1)}, u32[]{:S(2)}, u32[]{:S(2)}) %collective-permute-start.6) | collective-permute-done | bytes 491552 | tf_op jit(solution)/shard_map/ppermute | solution.py:28
  64.6 0.8 copy-done.15
  65.5 0.3 unpack_y.1.refs_0_
  65.9 2.5 %collective-permute-start.10 = (bf16[48,5248]{1,0:T(8,128)(2,1)S(1)}, bf16[48,5248]{1,0:T(8,128)(2,1)S(1)}, u32[]{:S(2)}, u32[]{:S(2)}) collective-permute-start(bf16[48,5248]{1,0:T(8,128)(2,1)S(1)} %unpack_y.1.refs_0_), channel_id=1, source_target_pairs={{0,128},{16,144},{32,160},{48,176},{64,192},{80,208},{96,224},{112... | collective-permute-start | bytes 1511432 | tf_op jit(solution)/shard_map/ppermute | solution.py:28
  68.7 1.7 collective-permute-start.8
  70.4 4.8 %collective-permute-done.11.refs_5_ = bf16[48,5120]{1,0:T(8,128)(2,1)} collective-permute-done((bf16[48,5120]{1,0:T(8,128)(2,1)S(1)}, bf16[48,5120]{1,0:T(8,128)(2,1)}, u32[]{:S(2)}, u32[]{:S(2)}) %collective-permute-start.11) | collective-permute-done | bytes 491552 | tf_op jit(solution)/shard_map/ppermute | solution.py:28
  75.3 4.2 %collective-permute-done.12.refs_6_ = bf16[48,5120]{1,0:T(8,128)(2,1)S(1)} collective-permute-done((bf16[48,5120]{1,0:T(8,128)(2,1)}, bf16[48,5120]{1,0:T(8,128)(2,1)S(1)}, u32[]{:S(2)}, u32[]{:S(2)}) %collective-permute-start.12) | collective-permute-done | bytes 491552 | tf_op jit(solution)/shard_map/ppermute | solution.py:28
  79.5 6.5 %pre.1 = (f32[192,384]{1,0:T(8,128)S(1)}, f32[192,384]{1,0:T(8,128)S(1)}, bf16[384,5120]{1,0:T(8,128)(2,1)}) custom-call(bf16[48,5120]{1,0:T(8,128)(2,1)S(1)} %unpack_x.1.refs_0_, bf16[48,5120]{1,0:T(8,128)(2,1)S(1)} %collective-permute-done.3.refs_1_, bf16[48,5120]{1,0:T(8,128)(2,1)S(1)} %copy-done.16, bf16[48,5120]{1,0:T(8,128)(2,1)S(1)} %collective-permute-done.4.refs_3_, ...), custom_call_target="tpu_custom_call" | custom-call | flops 1509949440 | bytes 10000000 | tf_op jit(solution)/shard_map/pre/pallas_call | solution.py:48
  86.0 3.0 %collective-permute-start.15 = (bf16[48,5248]{1,0:T(8,128)(2,1)S(1)}, bf16[48,5248]{1,0:T(8,128)(2,1)S(1)}, u32[]{:S(2)}, u32[]{:S(2)}) collective-permute-start(bf16[48,5248]{1,0:T(8,128)(2,1)S(1)} %collective-permute-done.10.refs_4_), channel_id=1, source_target_pairs={{0,96},{16,112},{32,0},{48,16},{64,32},{80,48},{96,64},{112,80},{1... | collective-permute-start | bytes 1511432 | tf_op jit(solution)/shard_map/ppermute | solution.py:28
  89.0 8.1 %collective-permute-done.15.refs_7_ = bf16[48,5248]{1,0:T(8,128)(2,1)S(1)} collective-permute-done((bf16[48,5248]{1,0:T(8,128)(2,1)S(1)}, bf16[48,5248]{1,0:T(8,128)(2,1)S(1)}, u32[]{:S(2)}, u32[]{:S(2)}) %collective-permute-start.15) | collective-permute-done | bytes 503840 | tf_op jit(solution)/shard_map/ppermute | solution.py:28
  97.1 3.7 %collective-permute-start.16 = (bf16[48,5248]{1,0:T(8,128)(2,1)S(1)}, bf16[48,5248]{1,0:T(8,128)(2,1)S(1)}, u32[]{:S(2)}, u32[]{:S(2)}) collective-permute-start(bf16[48,5248]{1,0:T(8,128)(2,1)S(1)} %collective-permute-done.15.refs_7_), channel_id=1, source_target_pairs={{0,96},{16,112},{32,0},{48,16},{64,32},{80,48},{96,64},{112,80},{1... | collective-permute-start | bytes 1511432 | tf_op jit(solution)/shard_map/ppermute | solution.py:28
  100.8 10.5 %collective-permute-done.13.refs_2_ = bf16[48,5248]{1,0:T(8,128)(2,1)S(1)} collective-permute-done((bf16[48,5248]{1,0:T(8,128)(2,1)S(1)}, bf16[48,5248]{1,0:T(8,128)(2,1)S(1)}, u32[]{:S(2)}, u32[]{:S(2)}) %collective-permute-start.13) | collective-permute-done | bytes 503840 | tf_op jit(solution)/shard_map/ppermute | solution.py:28
  111.4 0.7 copy-done.30
  112.5 11.0 %main.1 = (bf16[48,5248]{1,0:T(8,128)(2,1)S(1)}, bf16[48,5248]{1,0:T(8,128)(2,1)S(1)}, bf16[48,5248]{1,0:T(8,128)(2,1)S(1)}, bf16[48,5248]{1,0:T(8,128)(2,1)}, b...) custom-call(bf16[48,5248]{1,0:T(8,128)(2,1)S(1)} %unpack_y.1.refs_0_, ...), custom_call_target="tpu_custom_call" | custom-call | flops 2264924160 | bytes 14000000 | tf_op jit(solution)/shard_map/main/pallas_call | solution.py:48
  123.6 3.2 %collective-permute-start.18 = (bf16[48,5248]{1,0:T(8,128)(2,1)S(1)}, bf16[48,5248]{1,0:T(8,128)(2,1)S(1)}, u32[]{:S(2)}, u32[]{:S(2)}) collective-permute-start(bf16[48,5248]{1,0:T(8,128)(2,1)S(1)} %get-tuple-element.78), channel_id=1, source_target_pairs={{0,96},{16,112},{32,0},{48,16},{64,32},{80,48},{96,64},{112,80},{1... | collective-permute-start | bytes 1511432 | tf_op jit(solution)/shard_map/ppermute | solution.py:28
  126.8 1.6 wgrad.7
  128.5 1.6 wgrad.8
  130.0 0.5 copy-done.1
  130.6 1.6 wgrad.6
  132.2 2.1 %collective-permute-done.17.refs_1_ = bf16[48,5248]{1,0:T(8,128)(2,1)S(1)} collective-permute-done((bf16[48,5248]{1,0:T(8,128)(2,1)S(1)}, bf16[48,5248]{1,0:T(8,128)(2,1)S(1)}, u32[]{:S(2)}, u32[]{:S(2)}) %collective-permute-start.17) | collective-permute-done | bytes 503840 | tf_op jit(solution)/shard_map/ppermute | solution.py:28
  134.2 0.8 copy-done.11
  135.0 0.5 collective-permute-start.22
  135.9 3.2 %collective-permute-start.20 = (bf16[48,5248]{1,0:T(8,128)(2,1)}, bf16[48,5248]{1,0:T(8,128)(2,1)S(1)}, u32[]{:S(2)}, u32[]{:S(2)}) collective-permute-start(bf16[48,5248]{1,0:T(8,128)(2,1)} %copy-done.19), channel_id=1, source_target_pairs={{0,96},{16,112},{32,0},{48,16},{64,32},{80,48},{96,64},{112,80},{1... | collective-permute-start | bytes 1511432 | tf_op jit(solution)/shard_map/ppermute | solution.py:28
  139.1 11.9 %collective-permute-done.19.refs_2_ = bf16[48,5248]{1,0:T(8,128)(2,1)S(1)} collective-permute-done((bf16[48,5248]{1,0:T(8,128)(2,1)S(1)}, bf16[48,5248]{1,0:T(8,128)(2,1)S(1)}, u32[]{:S(2)}, u32[]{:S(2)}) %collective-permute-start.19) | collective-permute-done | bytes 503840 | tf_op jit(solution)/shard_map/ppermute | solution.py:28
  151.0 0.8 copy-done.13
  152.2 2.5 %collective-permute-start.25 = (bf16[48,5248]{1,0:T(8,128)(2,1)S(1)}, bf16[48,5248]{1,0:T(8,128)(2,1)S(1)}, u32[]{:S(2)}, u32[]{:S(2)}) collective-permute-start(bf16[48,5248]{1,0:T(8,128)(2,1)S(1)} %join.5), channel_id=1, source_target_pairs={{0,96},{16,112},{32,0},{48,16},{64,32},{80,48},{96,64},{112,80},{1... | collective-permute-start | bytes 1511432 | tf_op jit(solution)/shard_map/ppermute | solution.py:28
  154.6 0.5 join.4
  155.3 2.6 %wgrad.9 = bf16[96,5120]{1,0:T(8,128)(2,1)} custom-call(bf16[192,384]{1,0:T(8,128)(2,1)S(1)} %get-tuple-element.97.left_ref, bf16[384,5120]{1,0:T(8,128)(2,1)S(1)} %copy-done.1, bf16[96,5120]{1,0:T(8,128)(2,1)S(1)} %collective-permute-done.21.rest_0_), custom_call_target="tpu_custom_call" | custom-call | flops 188743680 | bytes 3000000 | tf_op jit(solution)/shard_map/wgrad/pallas_call | solution.py:385
  157.9 2.6 %wgrad.10 = bf16[96,5120]{1,0:T(8,128)(2,1)} custom-call(bf16[192,384]{1,0:T(8,128)(2,1)S(1)} %get-tuple-element.99.left_ref, bf16[384,5120]{1,0:T(8,128)(2,1)S(1)} %copy-done, bf16[96,5120]{1,0:T(8,128)(2,1)S(1)} %collective-permute-done.22.rest_0_), custom_call_target="tpu_custom_call" | custom-call | flops 188743680 | bytes 3000000 | tf_op jit(solution)/shard_map/wgrad/pallas_call | solution.py:385
  160.4 2.6 %wgrad.11 = bf16[96,5120]{1,0:T(8,128)(2,1)} custom-call(bf16[192,384]{1,0:T(8,128)(2,1)S(1)} %get-tuple-element.101.left_ref, bf16[384,5120]{1,0:T(8,128)(2,1)S(1)} %copy-done, bf16[96,5120]{1,0:T(8,128)(2,1)S(1)} %collective-permute-done.23.rest_0_), custom_call_target="tpu_custom_call" | custom-call | flops 188743680 | bytes 3000000 | tf_op jit(solution)/shard_map/wgrad/pallas_call | solution.py:385
  163.0 2.3 %collective-permute-done.25.refs_2_ = bf16[48,5248]{1,0:T(8,128)(2,1)S(1)} collective-permute-done((bf16[48,5248]{1,0:T(8,128)(2,1)S(1)}, bf16[48,5248]{1,0:T(8,128)(2,1)S(1)}, u32[]{:S(2)}, u32[]{:S(2)}) %collective-permute-start.25) | collective-permute-done | bytes 503840 | tf_op jit(solution)/shard_map/ppermute | solution.py:28
  165.3 2.5 %collective-permute-done.24.refs_3_ = bf16[48,5248]{1,0:T(8,128)(2,1)S(1)} collective-permute-done((bf16[48,5248]{1,0:T(8,128)(2,1)S(1)}, bf16[48,5248]{1,0:T(8,128)(2,1)S(1)}, u32[]{:S(2)}, u32[]{:S(2)}) %collective-permute-start.24) | collective-permute-done | bytes 503840 | tf_op jit(solution)/shard_map/ppermute | solution.py:28
  167.8 1.5 collective-permute-done.26.refs_1_
  169.3 0.5 last.1
  169.8 21.5 %all_to_all.16 = bf16[16,8,2048]{2,1,0:T(8,128)(2,1)S(1)} all-to-all(bf16[16,8,2048]{2,1,0:T(8,128)(2,1)S(1)} %bitcast.18), channel_id=1, replica_groups=mesh['edp'=16,'ep'=16] {'ep'}, dimensions={0} | all-to-all | bytes 1048576 | tf_op jit(solution)/shard_map/all_to_all | solution.py:312
  191.3 2.4 %final.1 = (bf16[128,5120]{1,0:T(8,128)(2,1)}, bf16[6,128]{1,0:T(8,128)(2,1)}) custom-call(s32[6,128]{1,0:T(8,128)S(1)} %bitcast.25, bf16[128,2048]{1,0:T(8,128)(2,1)S(1)} %bitcast.21), custom_call_target="tpu_custom_call" | custom-call | flops 600000000 | bytes 2000000 | tf_op jit(solution)/shard_map/final/pallas_call | solution.py:48
  (91 shorter events, 2.4 us)
Async XLA Ops:
  0.6 32.0 %collective-permute-start = (bf16[96,5120]{1,0:T(8,128)(2,1)}, bf16[96,5120]{1,0:T(8,128)(2,1)S(1)}, u32[]{:S(2)}, u32[]{:S(2)}) collective-permute-start(bf16[96,5120]{1,0:T(8,128)(2,1)} %bitcast.15), channel_id=1, source_target_pairs={{0,16},{16,0},{32,48},{48,32},{64,80},{80,64},{96,112},{112,96},{1... | collective-permute-start | bytes 2949128 | tf_op jit(solution)/shard_map/ppermute | solution.py:28
  0.7 31.9 %collective-permute-start.1 = (bf16[96,5120]{1,0:T(8,128)(2,1)}, bf16[96,5120]{1,0:T(8,128)(2,1)S(1)}, u32[]{:S(2)}, u32[]{:S(2)}) collective-permute-start(bf16[96,5120]{1,0:T(8,128)(2,1)} %bitcast.27), channel_id=1, source_target_pairs={{0,16},{16,0},{32,48},{48,32},{64,80},{80,64},{96,112},{112,96},{1... | collective-permute-start | bytes 2949128 | tf_op jit(solution)/shard_map/ppermute | solution.py:28
  1.2 31.4 %collective-permute-start.2 = (bf16[96,5120]{1,0:T(8,128)(2,1)}, bf16[96,5120]{1,0:T(8,128)(2,1)S(1)}, u32[]{:S(2)}, u32[]{:S(2)}) collective-permute-start(bf16[96,5120]{1,0:T(8,128)(2,1)} %bitcast.30), channel_id=1, source_target_pairs={{0,16},{16,0},{32,48},{48,32},{64,80},{80,64},{96,112},{112,96},{1... | collective-permute-start | bytes 2949128 | tf_op jit(solution)/shard_map/ppermute | solution.py:28
  4.6 31.2 %copy-start.18 = (bf16[128,5120]{1,0:T(8,128)(2,1)S(1)}, bf16[128,5120]{1,0:T(8,128)(2,1)}, u32[]{:S(2)}) copy-start(bf16[128,5120]{1,0:T(8,128)(2,1)} %refs_2_) | copy-start | bytes 3932164
  4.6 31.2 %copy-start.21 = (s32[128,6]{0,1:T(8,128)S(1)}, s32[128,6]{0,1:T(8,128)}, u32[]{:S(2)}) copy-start(s32[128,6]{0,1:T(8,128)} %param.10) | copy-start | bytes 9220
  4.7 31.2 %copy-start.22 = (bf16[128,6]{0,1:T(8,128)(2,1)S(1)}, bf16[128,6]{0,1:T(8,128)(2,1)}, u32[]{:S(2)}) copy-start(bf16[128,6]{0,1:T(8,128)(2,1)} %param.9) | copy-start | bytes 4612
  32.6 5.4 %copy-start.24 = (bf16[96,5120]{1,0:T(8,128)(2,1)}, bf16[96,5120]{1,0:T(8,128)(2,1)S(1)}, u32[]{:S(2)}) copy-start(bf16[96,5120]{1,0:T(8,128)(2,1)S(1)} %collective-permute-done.1.refs_11_.refs_13_) | copy-start | bytes 2949124
  32.6 5.4 %copy-start.25 = (bf16[96,5120]{1,0:T(8,128)(2,1)}, bf16[96,5120]{1,0:T(8,128)(2,1)S(1)}, u32[]{:S(2)}) copy-start(bf16[96,5120]{1,0:T(8,128)(2,1)S(1)} %collective-permute-done.2.refs_9_) | copy-start | bytes 2949124
  32.9 14.2 %collective-permute-start.5 = (bf16[48,5120]{1,0:T(8,128)(2,1)S(1)}, bf16[48,5120]{1,0:T(8,128)(2,1)S(1)}, u32[]{:S(2)}, u32[]{:S(2)}) collective-permute-start(bf16[48,5120]{1,0:T(8,128)(2,1)S(1)} %unpack_x.1.refs_0_), channel_id=1, source_target_pairs={{0,128},{16,144},{32,160},{48,176},{64,192},{80,208},{96,224},{112... | collective-permute-start | bytes 1474568 | tf_op jit(solution)/shard_map/ppermute | solution.py:28
  33.0 14.1 %collective-permute-start.4 = (bf16[48,5120]{1,0:T(8,128)(2,1)S(1)}, bf16[48,5120]{1,0:T(8,128)(2,1)S(1)}, u32[]{:S(2)}, u32[]{:S(2)}) collective-permute-start(bf16[48,5120]{1,0:T(8,128)(2,1)S(1)} %unpack_x.1.refs_0_), channel_id=1, source_target_pairs={{0,96},{16,112},{32,0},{48,16},{64,32},{80,48},{96,64},{112,80},{1... | collective-permute-start | bytes 1474568 | tf_op jit(solution)/shard_map/ppermute | solution.py:28
  35.9 13.4 %collective-permute-start.3 = (bf16[48,5120]{1,0:T(8,128)(2,1)S(1)}, bf16[48,5120]{1,0:T(8,128)(2,1)S(1)}, u32[]{:S(2)}, u32[]{:S(2)}) collective-permute-start(bf16[48,5120]{1,0:T(8,128)(2,1)S(1)} %unpack_x.1.refs_0_), channel_id=1, source_target_pairs={{0,32},{16,48},{32,64},{48,80},{64,96},{80,112},{96,0},{112,16},{1... | collective-permute-start | bytes 1474568 | tf_op jit(solution)/shard_map/ppermute | solution.py:28
  38.0 41.4 %copy-start.2 = (bf16[1,96,5120]{2,1,0:T(8,128)(2,1)S(1)}, bf16[1,96,5120]{2,1,0:T(8,128)(2,1)}, u32[]{:S(2)}) copy-start(bf16[1,96,5120]{2,1,0:T(8,128)(2,1)} %param.11) | copy-start | bytes 2949124
  38.0 27.4 %all-to-all-start.1 = ((bf16[16,8,2048]{2,1,0:T(8,128)(2,1)}), bf16[16,8,2048]{2,1,0:T(8,128)(2,1)S(1)}, u32[]{:S(2)}, u32[]{:S(2)}) async-start(bf16[16,8,2048]{2,1,0:T(8,128)(2,1)} %bitcast.7), calls=%async_computation.1 | async-start | bytes 1048576 | tf_op jit(solution)/shard_map/all_to_all | solution.py:312
  49.3 15.4 %collective-permute-start.6 = (bf16[48,5120]{1,0:T(8,128)(2,1)S(1)}, bf16[48,5120]{1,0:T(8,128)(2,1)S(1)}, u32[]{:S(2)}, u32[]{:S(2)}) collective-permute-start(bf16[48,5120]{1,0:T(8,128)(2,1)S(1)} %collective-permute-done.3.refs_1_), channel_id=1, source_target_pairs={{0,32},{16,48},{32,64},{48,80},{64,96},{80,112},{96,0},{112,16},{1... | collective-permute-start | bytes 1474568 | tf_op jit(solution)/shard_map/ppermute | solution.py:28
  49.8 15.7 %collective-permute-start.7 = (bf16[48,5120]{1,0:T(8,128)(2,1)S(1)}, bf16[48,5120]{1,0:T(8,128)(2,1)}, u32[]{:S(2)}, u32[]{:S(2)}) collective-permute-start(bf16[48,5120]{1,0:T(8,128)(2,1)S(1)} %collective-permute-done.5.refs_4_), channel_id=1, source_target_pairs={{0,96},{16,112},{32,0},{48,16},{64,32},{80,48},{96,64},{112,80},{1... | collective-permute-start | bytes 1474568 | tf_op jit(solution)/shard_map/ppermute | solution.py:28
  52.5 22.8 %collective-permute-start.11 = (bf16[48,5120]{1,0:T(8,128)(2,1)S(1)}, bf16[48,5120]{1,0:T(8,128)(2,1)}, u32[]{:S(2)}, u32[]{:S(2)}) collective-permute-start(bf16[48,5120]{1,0:T(8,128)(2,1)S(1)} %collective-permute-done.5.refs_4_), channel_id=1, source_target_pairs={{0,32},{16,48},{32,64},{48,80},{64,96},{80,112},{96,0},{112,16},{1... | collective-permute-start | bytes 1474568 | tf_op jit(solution)/shard_map/ppermute | solution.py:28
  65.4 14.0 %copy-start.16 = (bf16[48,5120]{1,0:T(8,128)(2,1)S(1)}, bf16[48,5120]{1,0:T(8,128)(2,1)}, u32[]{:S(2)}) copy-start(bf16[48,5120]{1,0:T(8,128)(2,1)} %copy-done.15) | copy-start | bytes 1474564
  65.4 14.0 %collective-permute-start.12 = (bf16[48,5120]{1,0:T(8,128)(2,1)}, bf16[48,5120]{1,0:T(8,128)(2,1)S(1)}, u32[]{:S(2)}, u32[]{:S(2)}) collective-permute-start(bf16[48,5120]{1,0:T(8,128)(2,1)} %collective-permute-done.7.refs_7_), channel_id=1, source_target_pairs={{0,96},{16,112},{32,0},{48,16},{64,32},{80,48},{96,64},{112,80},{1... | collective-permute-start | bytes 1474568 | tf_op jit(solution)/shard_map/ppermute | solution.py:28
  65.9 20.1 %collective-permute-start.10 = (bf16[48,5248]{1,0:T(8,128)(2,1)S(1)}, bf16[48,5248]{1,0:T(8,128)(2,1)S(1)}, u32[]{:S(2)}, u32[]{:S(2)}) collective-permute-start(bf16[48,5248]{1,0:T(8,128)(2,1)S(1)} %unpack_y.1.refs_0_), channel_id=1, source_target_pairs={{0,128},{16,144},{32,160},{48,176},{64,192},{80,208},{96,224},{112... | collective-permute-start | bytes 1511432 | tf_op jit(solution)/shard_map/ppermute | solution.py:28
  68.4 17.6 %collective-permute-start.9 = (bf16[48,5248]{1,0:T(8,128)(2,1)S(1)}, bf16[48,5248]{1,0:T(8,128)(2,1)S(1)}, u32[]{:S(2)}, u32[]{:S(2)}) collective-permute-start(bf16[48,5248]{1,0:T(8,128)(2,1)S(1)} %unpack_y.1.refs_0_), channel_id=1, source_target_pairs={{0,96},{16,112},{32,0},{48,16},{64,32},{80,48},{96,64},{112,80},{1... | collective-permute-start | bytes 1511432 | tf_op jit(solution)/shard_map/ppermute | solution.py:28
  68.7 17.3 %collective-permute-start.8 = (bf16[48,5248]{1,0:T(8,128)(2,1)S(1)}, bf16[48,5248]{1,0:T(8,128)(2,1)S(1)}, u32[]{:S(2)}, u32[]{:S(2)}) collective-permute-start(bf16[48,5248]{1,0:T(8,128)(2,1)S(1)} %unpack_y.1.refs_0_), channel_id=1, source_target_pairs={{0,32},{16,48},{32,64},{48,80},{64,96},{80,112},{96,0},{112,16},{1... | collective-permute-start | bytes 1511432 | tf_op jit(solution)/shard_map/ppermute | solution.py:28
  86.0 25.4 %copy-start.26 = (bf16[48,5248]{1,0:T(8,128)(2,1)}, bf16[48,5248]{1,0:T(8,128)(2,1)S(1)}, u32[]{:S(2)}) copy-start(bf16[48,5248]{1,0:T(8,128)(2,1)S(1)} %collective-permute-done.10.refs_4_) | copy-start | bytes 1511428
  86.0 25.4 %copy-start.27 = (bf16[48,5248]{1,0:T(8,128)(2,1)}, bf16[48,5248]{1,0:T(8,128)(2,1)S(1)}, u32[]{:S(2)}) copy-start(bf16[48,5248]{1,0:T(8,128)(2,1)S(1)} %collective-permute-done.9.refs_3_) | copy-start | bytes 1511428
  86.0 11.1 %collective-permute-start.15 = (bf16[48,5248]{1,0:T(8,128)(2,1)S(1)}, bf16[48,5248]{1,0:T(8,128)(2,1)S(1)}, u32[]{:S(2)}, u32[]{:S(2)}) collective-permute-start(bf16[48,5248]{1,0:T(8,128)(2,1)S(1)} %collective-permute-done.10.refs_4_), channel_id=1, source_target_pairs={{0,96},{16,112},{32,0},{48,16},{64,32},{80,48},{96,64},{112,80},{1... | collective-permute-start | bytes 1511432 | tf_op jit(solution)/shard_map/ppermute | solution.py:28
  89.0 22.3 %collective-permute-start.14 = (bf16[48,5248]{1,0:T(8,128)(2,1)S(1)}, bf16[48,5248]{1,0:T(8,128)(2,1)S(1)}, u32[]{:S(2)}, u32[]{:S(2)}) collective-permute-start(bf16[48,5248]{1,0:T(8,128)(2,1)S(1)} %collective-permute-done.10.refs_4_), channel_id=1, source_target_pairs={{0,32},{16,48},{32,64},{48,80},{64,96},{80,112},{96,0},{112,16},{1... | collective-permute-start | bytes 1511432 | tf_op jit(solution)/shard_map/ppermute | solution.py:28
  89.0 22.3 %collective-permute-start.13 = (bf16[48,5248]{1,0:T(8,128)(2,1)S(1)}, bf16[48,5248]{1,0:T(8,128)(2,1)S(1)}, u32[]{:S(2)}, u32[]{:S(2)}) collective-permute-start(bf16[48,5248]{1,0:T(8,128)(2,1)S(1)} %collective-permute-done.8.refs_1_), channel_id=1, source_target_pairs={{0,32},{16,48},{32,64},{48,80},{64,96},{80,112},{96,0},{112,16},{1... | collective-permute-start | bytes 1511432 | tf_op jit(solution)/shard_map/ppermute | solution.py:28
  97.1 14.3 %copy-start.28 = (bf16[48,5248]{1,0:T(8,128)(2,1)}, bf16[48,5248]{1,0:T(8,128)(2,1)S(1)}, u32[]{:S(2)}) copy-start(bf16[48,5248]{1,0:T(8,128)(2,1)S(1)} %collective-permute-done.15.refs_7_) | copy-start | bytes 1511428
  97.1 14.2 %collective-permute-start.16 = (bf16[48,5248]{1,0:T(8,128)(2,1)S(1)}, bf16[48,5248]{1,0:T(8,128)(2,1)S(1)}, u32[]{:S(2)}, u32[]{:S(2)}) collective-permute-start(bf16[48,5248]{1,0:T(8,128)(2,1)S(1)} %collective-permute-done.15.refs_7_), channel_id=1, source_target_pairs={{0,96},{16,112},{32,0},{48,16},{64,32},{80,48},{96,64},{112,80},{1... | collective-permute-start | bytes 1511432 | tf_op jit(solution)/shard_map/ppermute | solution.py:28
  112.5 14.4 %copy-start = (bf16[384,5120]{1,0:T(8,128)(2,1)S(1)}, bf16[384,5120]{1,0:T(8,128)(2,1)}, u32[]{:S(2)}) copy-start(bf16[384,5120]{1,0:T(8,128)(2,1)} %get-tuple-element.83.rows_ref) | copy-start | bytes 11796484
  123.5 4.9 %copy-start.3 = (bf16[48,5248]{1,0:T(8,128)(2,1)}, bf16[48,5248]{1,0:T(8,128)(2,1)S(1)}, u32[]{:S(2)}) copy-start(bf16[48,5248]{1,0:T(8,128)(2,1)S(1)} %get-tuple-element.75.refs_0_) | copy-start | bytes 1511428
  123.5 4.9 %copy-start.5 = (bf16[48,5248]{1,0:T(8,128)(2,1)}, bf16[48,5248]{1,0:T(8,128)(2,1)S(1)}, u32[]{:S(2)}) copy-start(bf16[48,5248]{1,0:T(8,128)(2,1)S(1)} %get-tuple-element.94.refs_0_) | copy-start | bytes 1511428
  123.5 4.9 %copy-start.7 = (bf16[48,5248]{1,0:T(8,128)(2,1)}, bf16[48,5248]{1,0:T(8,128)(2,1)S(1)}, u32[]{:S(2)}) copy-start(bf16[48,5248]{1,0:T(8,128)(2,1)S(1)} %get-tuple-element.86.refs_0_) | copy-start | bytes 1511428
  123.5 4.9 %copy-start.9 = (bf16[48,5248]{1,0:T(8,128)(2,1)}, bf16[48,5248]{1,0:T(8,128)(2,1)S(1)}, u32[]{:S(2)}) copy-start(bf16[48,5248]{1,0:T(8,128)(2,1)S(1)} %get-tuple-element.76.refs_0_) | copy-start | bytes 1511428
  123.5 4.9 %copy-start.19 = (bf16[48,5248]{1,0:T(8,128)(2,1)}, bf16[48,5248]{1,0:T(8,128)(2,1)S(1)}, u32[]{:S(2)}) copy-start(bf16[48,5248]{1,0:T(8,128)(2,1)S(1)} %get-tuple-element.88) | copy-start | bytes 1511428
  123.5 10.7 %collective-permute-start.17 = (bf16[48,5248]{1,0:T(8,128)(2,1)S(1)}, bf16[48,5248]{1,0:T(8,128)(2,1)S(1)}, u32[]{:S(2)}, u32[]{:S(2)}) collective-permute-start(bf16[48,5248]{1,0:T(8,128)(2,1)S(1)} %get-tuple-element.77), channel_id=1, source_target_pairs={{0,32},{16,48},{32,64},{48,80},{64,96},{80,112},{96,0},{112,16},{1... | collective-permute-start | bytes 1511432 | tf_op jit(solution)/shard_map/ppermute | solution.py:28
  123.6 10.6 %collective-permute-start.18 = (bf16[48,5248]{1,0:T(8,128)(2,1)S(1)}, bf16[48,5248]{1,0:T(8,128)(2,1)S(1)}, u32[]{:S(2)}, u32[]{:S(2)}) collective-permute-start(bf16[48,5248]{1,0:T(8,128)(2,1)S(1)} %get-tuple-element.78), channel_id=1, source_target_pairs={{0,96},{16,112},{32,0},{48,16},{64,32},{80,48},{96,64},{112,80},{1... | collective-permute-start | bytes 1511432 | tf_op jit(solution)/shard_map/ppermute | solution.py:28
  130.6 5.0 %copy-start.8 = (bf16[48,5248]{1,0:T(8,128)(2,1)S(1)}, bf16[48,5248]{1,0:T(8,128)(2,1)}, u32[]{:S(2)}) copy-start(bf16[48,5248]{1,0:T(8,128)(2,1)} %copy-done.7) | copy-start | bytes 1511428
  132.1 19.7 %copy-start.6 = (bf16[48,5248]{1,0:T(8,128)(2,1)S(1)}, bf16[48,5248]{1,0:T(8,128)(2,1)}, u32[]{:S(2)}) copy-start(bf16[48,5248]{1,0:T(8,128)(2,1)} %copy-done.5) | copy-start | bytes 1511428
  135.0 16.8 %collective-permute-start.21 = (bf16[96,5120]{1,0:T(8,128)(2,1)S(1)}, bf16[96,5120]{1,0:T(8,128)(2,1)S(1)}, u32[]{:S(2)}, u32[]{:S(2)}) collective-permute-start(bf16[96,5120]{1,0:T(8,128)(2,1)S(1)} %wgrad.6), channel_id=1, source_target_pairs={{0,16},{16,0},{32,48},{48,32},{64,80},{80,64},{96,112},{112,96},{1... | collective-permute-start | bytes 2949128 | tf_op jit(solution)/shard_map/ppermute | solution.py:28
  135.0 16.8 %collective-permute-start.22 = (bf16[96,5120]{1,0:T(8,128)(2,1)S(1)}, bf16[96,5120]{1,0:T(8,128)(2,1)S(1)}, u32[]{:S(2)}, u32[]{:S(2)}) collective-permute-start(bf16[96,5120]{1,0:T(8,128)(2,1)S(1)} %wgrad.7), channel_id=1, source_target_pairs={{0,16},{16,0},{32,48},{48,32},{64,80},{80,64},{96,112},{112,96},{1... | collective-permute-start | bytes 2949128 | tf_op jit(solution)/shard_map/ppermute | solution.py:28
  135.5 16.3 %collective-permute-start.23 = (bf16[96,5120]{1,0:T(8,128)(2,1)S(1)}, bf16[96,5120]{1,0:T(8,128)(2,1)S(1)}, u32[]{:S(2)}, u32[]{:S(2)}) collective-permute-start(bf16[96,5120]{1,0:T(8,128)(2,1)S(1)} %wgrad.8), channel_id=1, source_target_pairs={{0,16},{16,0},{32,48},{48,32},{64,80},{80,64},{96,112},{112,96},{1... | collective-permute-start | bytes 2949128 | tf_op jit(solution)/shard_map/ppermute | solution.py:28
  135.9 18.8 %copy-start.12 = (bf16[48,5248]{1,0:T(8,128)(2,1)S(1)}, bf16[48,5248]{1,0:T(8,128)(2,1)}, u32[]{:S(2)}) copy-start(bf16[48,5248]{1,0:T(8,128)(2,1)} %copy-done.11) | copy-start | bytes 1511428
  135.9 15.1 %collective-permute-start.19 = (bf16[48,5248]{1,0:T(8,128)(2,1)S(1)}, bf16[48,5248]{1,0:T(8,128)(2,1)S(1)}, u32[]{:S(2)}, u32[]{:S(2)}) collective-permute-start(bf16[48,5248]{1,0:T(8,128)(2,1)S(1)} %join.3), channel_id=1, source_target_pairs={{0,32},{16,48},{32,64},{48,80},{64,96},{80,112},{96,0},{112,16},{1... | collective-permute-start | bytes 1511432 | tf_op jit(solution)/shard_map/ppermute | solution.py:28
  135.9 15.9 %collective-permute-start.20 = (bf16[48,5248]{1,0:T(8,128)(2,1)}, bf16[48,5248]{1,0:T(8,128)(2,1)S(1)}, u32[]{:S(2)}, u32[]{:S(2)}) collective-permute-start(bf16[48,5248]{1,0:T(8,128)(2,1)} %copy-done.19), channel_id=1, source_target_pairs={{0,96},{16,112},{32,0},{48,16},{64,32},{80,48},{96,64},{112,80},{1... | collective-permute-start | bytes 1511432 | tf_op jit(solution)/shard_map/ppermute | solution.py:28
  152.2 13.1 %collective-permute-start.25 = (bf16[48,5248]{1,0:T(8,128)(2,1)S(1)}, bf16[48,5248]{1,0:T(8,128)(2,1)S(1)}, u32[]{:S(2)}, u32[]{:S(2)}) collective-permute-start(bf16[48,5248]{1,0:T(8,128)(2,1)S(1)} %join.5), channel_id=1, source_target_pairs={{0,96},{16,112},{32,0},{48,16},{64,32},{80,48},{96,64},{112,80},{1... | collective-permute-start | bytes 1511432 | tf_op jit(solution)/shard_map/ppermute | solution.py:28
  155.1 12.7 %collective-permute-start.24 = (bf16[48,5248]{1,0:T(8,128)(2,1)S(1)}, bf16[48,5248]{1,0:T(8,128)(2,1)S(1)}, u32[]{:S(2)}, u32[]{:S(2)}) collective-permute-start(bf16[48,5248]{1,0:T(8,128)(2,1)S(1)} %join.4), channel_id=1, source_target_pairs={{0,128},{16,144},{32,160},{48,176},{64,192},{80,208},{96,224},{112... | collective-permute-start | bytes 1511432 | tf_op jit(solution)/shard_map/ppermute | solution.py:28
  155.2 14.1 %collective-permute-start.26 = (bf16[48,5248]{1,0:T(8,128)(2,1)}, bf16[48,5248]{1,0:T(8,128)(2,1)S(1)}, u32[]{:S(2)}, u32[]{:S(2)}) collective-permute-start(bf16[48,5248]{1,0:T(8,128)(2,1)} %get-tuple-element.96), channel_id=1, source_target_pairs={{0,32},{16,48},{32,64},{48,80},{64,96},{80,112},{96,0},{112,16},{1... | collective-permute-start | bytes 1511432 | tf_op jit(solution)/shard_map/ppermute | solution.py:28
  160.4 8.9 %copy-start.4 = (bf16[48,5248]{1,0:T(8,128)(2,1)S(1)}, bf16[48,5248]{1,0:T(8,128)(2,1)}, u32[]{:S(2)}) copy-start(bf16[48,5248]{1,0:T(8,128)(2,1)} %copy-done.3) | copy-start | bytes 1511428
  (12 other events, 18.3 us)

commit v3 on v2

--- a/solution.py
+++ b/solution.py
@@ -14,12 +14,15 @@
 BF16 = jnp.bfloat16
 
 
-def chip_perm(move):
-    return [(i, (i & 9) | (move((i >> 1) & 3) << 1)) for i in range(16)]
-
-
-X_UP = chip_perm(lambda x: (x + 1) % 4)
-X_DOWN = chip_perm(lambda x: (x + 3) % 4)
+def x_perm(step):
+    pairs = []
+    for i in range(16):
+        x = ((i >> 1) + (step if i % 2 == 0 else -step)) & 3
+        pairs.append((i, (i & 9) | (x << 1)))
+    return pairs
+
+
+X_A, X_B = x_perm(1), x_perm(-1)
 Z_SWAP = [(i, i ^ 8) for i in range(16)]
 C_SWAP = [(i, i ^ 1) for i in range(16)]
 
@@ -221,13 +224,17 @@
             py_ref[:, cols] = (prob_col * y_all[:, cols].astype(F32)).astype(BF16)
 
 
-def wgrad_kernel(left_ref, rows_ref, *rest, first):
-    *came, out_ref = rest
-    hid = out_ref.shape[0]
-    total = dot(left_ref[first : first + hid, :], rows_ref[...])
-    for c in came:
-        total = total + c[...].astype(F32)
-    out_ref[...] = total.astype(BF16)
+def wgrad_kernel(hid_ref, dg_ref, du_ref, py_ref, x_ref, *rest, away):
+    hid = hid_ref.shape[0] // 2
+    first = hid if away else 0
+    sides = ((dg_ref, x_ref), (du_ref, x_ref), (hid_ref, py_ref))
+    for i, (left, right) in enumerate(sides):
+        total = dot(left[first : first + hid, :], right[...])
+        if away:
+            rest[0][i * hid : (i + 1) * hid, :] = total.astype(BF16)
+        else:
+            came = rest[0][i * hid : (i + 1) * hid, :].astype(F32)
+            rest[1 + i][...] = (total + came).astype(BF16)
 
 
 def summed(refs):
@@ -329,7 +336,7 @@
     core_g, core_u, core_d = hop(g, C_SWAP), hop(u, C_SWAP), hop(d, C_SWAP)
     got_x, core_g, core_u, core_d = together((exchange(send_x), core_g, core_u, core_d))
     x = unpack(got_x, width, "unpack_x")
-    left, right, oth = hop(x, X_UP), hop(x, X_DOWN), hop(x, Z_SWAP)
+    xa, xb, oth = hop(x, X_A), hop(x, X_B), hop(x, Z_SWAP)
     x_now, cot_now = together((x, cotangent))
     send_y = call(
         functools.partial(send_kernel, with_p=True),
@@ -338,12 +345,16 @@
         cost=(6 * 10**8, 2 * 10**6),
     )(ids_t, probs_t, cot_now)
     got_y = exchange(send_y)
-    left, right, oth = together((left, right, oth))
-    far, o_right, o_left = hop(left, X_UP), hop(oth, X_DOWN), hop(oth, X_UP)
-    far, o_right, got_y = together((far, o_right, got_y))
-    o_far = hop(o_right, X_DOWN)
+    xa, xb, oth = together((xa, xb, oth))
+    far, oa, ob = hop(xa, X_A), hop(oth, X_A), hop(oth, X_B)
+    far, oa, ob, got_y = together((far, oa, ob, got_y))
     y = unpack(got_y, wide, "unpack_y")
-    y_left, y_right, y_oth = hop(y, X_UP), hop(y, X_DOWN), hop(y, Z_SWAP)
+    ya, yb, y_oth = hop(y, X_A), hop(y, X_B), hop(y, Z_SWAP)
+    ya, yb, y_oth, far = together((ya, yb, y_oth, far))
+    y_far, yoa, yob = hop(ya, X_A), hop(y_oth, X_A), hop(y_oth, X_B)
+    o_far = hop(far, Z_SWAP)
+    y_far, o_far = together((y_far, o_far))
+    yo_far = hop(y_far, Z_SWAP)
     gate, up, x_all = call(
         pre_kernel,
         [shape((2 * hid, total), F32)] * 2 + [shape((total, width), BF16)],
@@ -351,10 +362,7 @@
         scratch=[pltpu.VMEM((4 * hid, width), BF16), dma((32,)), dma((16,))],
         specs=[any_spec] * 12,
         cost=(2 * work, 10 * 10**6),
-    )(x, left, far, right, oth, o_left, o_far, o_right, g, core_g, u, core_u)
-    y_left, y_right, y_oth, gate = together((y_left, y_right, y_oth, gate))
-    y_far, yo_right, yo_left = hop(y_left, X_UP), hop(y_oth, X_DOWN), hop(y_oth, X_UP)
-    yo_far = hop(yo_right, X_DOWN)
+    )(x, xa, far, xb, oth, oa, o_far, ob, g, core_g, u, core_u)
     *parts, d_gate, d_up, hidden, py = call(
         main_kernel,
         [shape((rows, wide), BF16)] * 8
@@ -373,31 +381,32 @@
         specs=[any_spec] * 14 + [vmem] * 2,
         cost=(3 * work, 14 * 10**6),
     )(
-        *(y, y_left, y_far, y_right, y_oth, yo_left, yo_far, yo_right),
+        *(y, ya, y_far, yb, y_oth, yoa, yo_far, yob),
         *(d, core_d, g, core_g, u, core_u, gate, up),
     )
 
     blocks = 4
 
-    def wgrad(left, right, place, *came):
+    def wgrad(*came):
         cols = width // blocks
-        part = pl.BlockSpec((hid, cols), lambda n: (0, n))
+
+        def part(height):
+            return pl.BlockSpec((height, cols), lambda n: (0, n))
+
+        left = pl.BlockSpec((2 * hid, total), lambda n: (0, 0))
+        out = [shape((hid, width), BF16)] * 3 if came else shape((3 * hid, width), BF16)
         return pl.pallas_call(
-            functools.partial(wgrad_kernel, first=place * hid),
-            out_shape=shape((hid, width), BF16),
+            functools.partial(wgrad_kernel, away=not came),
+            out_shape=out,
             grid=(blocks,),
-            in_specs=[
-                pl.BlockSpec(left.shape, lambda n: (0, 0)),
-                pl.BlockSpec((total, cols), lambda n: (0, n)),
-            ]
-            + [part] * len(came),
-            out_specs=part,
-            compiler_params=pltpu.CompilerParams(vmem_limit_bytes=16 * 1024 * 1024),
-            name="wgrad",
+            in_specs=[left] * 3 + [part(total)] * 2 + [part(3 * hid)] * len(came),
+            out_specs=[part(hid)] * 3 if came else part(3 * hid),
+            compiler_params=pltpu.CompilerParams(vmem_limit_bytes=32 * 1024 * 1024),
+            name="wgrad_mine" if came else "wgrad_away",
             cost_estimate=pl.CostEstimate(
-                flops=work // 4, bytes_accessed=3 * 10**6, transcendentals=0
+                flops=work * 3 // 2, bytes_accessed=12 * 10**6, transcendentals=0
             ),
-        )(left, right, *came)
+        )(hidden, d_gate, d_up, py, x_all, *came)
 
     def join(*a):
         return call(
@@ -407,28 +416,25 @@
             cost=(10**6, 10**6),
         )(*a)
 
-    own, left, far, right, oth, o_left, o_far, o_right = parts
-    of, ol = hop(o_far, X_UP), hop(o_left, X_DOWN)
-    away = [wgrad(hidden, py, 1), wgrad(d_gate, x_all, 1), wgrad(d_up, x_all, 1)]
-    of, ol, far, *away = together((of, ol, far, *away))
-    o_r, f = hop(join(o_right, of), X_UP), hop(far, X_DOWN)
-    came = [hop(a, C_SWAP) for a in away]
-    o_r, f, right, hidden, d_gate, d_up, *came = together(
-        (o_r, f, right, hidden, d_gate, d_up, *came)
-    )
-    oz = hop(join(oth, ol, o_r), Z_SWAP)
-    lf, r = hop(join(left, f), X_DOWN), hop(right, X_UP)
-    d_grad = wgrad(hidden, py, 0, came[0])
-    g_grad = wgrad(d_gate, x_all, 0, came[1])
-    u_grad = wgrad(d_up, x_all, 0, came[2])
-    oz, lf, r, d_grad, g_grad, u_grad = together((oz, lf, r, d_grad, g_grad, u_grad))
+    own, pa, far, pb, oth, oa, o_far, ob = parts
+    of, oa, ob = hop(o_far, Z_SWAP), hop(oa, X_B), hop(ob, X_A)
+    away = wgrad()
+    of, oa, ob, pb, away = together((of, oa, ob, pb, away))
+    f, oz = hop(join(far, of), X_B), hop(join(oth, oa, ob), Z_SWAP)
+    pb = hop(pb, X_A)
+    came = hop(away, C_SWAP)
+    f, oz, pb = together((f, oz, pb))
+    pa = hop(join(pa, f), X_B)
     last = call(
         functools.partial(last_kernel, group=group),
         shape((LANES, CAP * group + LANES), BF16),
         "last",
         cost=(10**8, 3 * 10**6),
-    )(own, r, lf, oz)
+    )(own, pa, pb, oz)
+    last, came = together((last, came))
     back = exchange(last)
+    g_grad, u_grad, d_grad = wgrad(came)
+    back, g_grad, u_grad, d_grad = together((back, g_grad, u_grad, d_grad))
     token_grad, gate_t = call(
         functools.partial(final_kernel, group=group),
         [shape(tokens.shape, BF16), shape(ids_t.shape, BF16)],

time: 195 us -> 194 us (level)
  blocking collectives: 49.4 us -> 27.9 us
  local copies, waits for them, and re-layouts: 6.12 us -> 16.9 us
  starting transfers between devices: 33.5 us -> 43.7 us
  Pallas kernels: 37.9 us -> 34.2 us
  waiting for transfers between devices: 65.7 us -> 67.9 us
    all_to_all x2 -> x1, blocking collectives: 49.4 us -> 27.9 us  [exchange(): a = lax.all_to_all(a, 'ep', split_axis=0, concat_axis=0, tiled=True)]
    unnamed x64 -> x62, local copies, waits for them, and re-layouts: 6.12 us -> 16.9 us
    all_to_all x1 -> x2, starting transfers between devices: 5.61 us -> 14.7 us  [exchange(): a = lax.all_to_all(a, 'ep', split_axis=0, concat_axis=0, tiled=True)]
    all_to_all x1 -> x2, waiting for transfers between devices: 0.01 us -> 7.75 us  [exchange(): a = lax.all_to_all(a, 'ep', split_axis=0, concat_axis=0, tiled=True)]
    ppermute x27 -> x25, waiting for transfers between devices: 65.7 us -> 60.1 us  [hop(): return lax.ppermute(a, 'edp', perm)]
    pallas_call x6 -> x2, Pallas kernels: 12.4 us -> 6.99 us  [wgrad(): pl.pallas_call(functools.partial(wgrad_kernel, away=not came), out_shape=...]
    ppermute x27 -> x25, starting transfers between devices: 27.9 us -> 29 us  [hop(): return lax.ppermute(a, 'edp', perm)]
  transfers between devices with their start and end apart: 28 -> 27, of which waited for: 12 -> 17; matrix products, arithmetic and copies ran while one was open for 0% -> 0% of each run, Pallas kernels for 12% -> 10%
where the time goes in v3:
time: 194 us; the launch traced here: 192 us
  waiting for transfers between devices  67.9 us (35%)
  starting transfers between devices  43.7 us (23%)
  Pallas kernels  34.2 us (18%)
  blocking collectives  27.9 us (14%)
  local copies, waits for them, and re-layouts  16.9 us (9%)
    ppermute x25, waiting for transfers between devices, hop(): return lax.ppermute(a, 'edp', perm)  60.1 us
    ppermute x25, starting transfers between devices, hop(): return lax.ppermute(a, 'edp', perm)  29 us
    all_to_all x1, blocking collectives, exchange(): a = lax.all_to_all(a, 'ep', split_axis=0, concat_axis=0, tiled=True)  27.9 us
    pallas_call x11, Pallas kernels, run(): pl.pallas_call(kernel, out_shape=outs, in_specs=[one] * len(args) if spec...  27.2 us
    unnamed x62, local copies, waits for them, and re-layouts  16.9 us
    all_to_all x2, starting transfers between devices, exchange(): a = lax.all_to_all(a, 'ep', split_axis=0, concat_axis=0, tiled=True)  14.7 us
    all_to_all x2, waiting for transfers between devices, exchange(): a = lax.all_to_all(a, 'ep', split_axis=0, concat_axis=0, tiled=True)  7.75 us
    pallas_call x2, Pallas kernels, wgrad(): pl.pallas_call(functools.partial(wgrad_kernel, away=not came), out_shape=...  6.99 us
  transfers between devices with their start and end apart: 27, of which 17 were waited for; matrix products, arithmetic and copies ran while one was open for 0% of the time, Pallas kernels for 10%

profile of v3, /device:TPU:32, one launch (start us, length us, event | category | flops | bytes accessed | tf_op | source)
XLA Modules:
  0.0 191.5 jit_solution(9595996825952466170)
XLA Ops:
  1.4 1.3 copy-done.17
  3.4 1.3 send_x.1
  4.7 27.9 %all_to_all.15 = bf16[16,8,1920]{2,1,0:T(8,128)(2,1)S(1)} all-to-all(bf16[16,8,1920]{2,1,0:T(8,128)(2,1)S(1)} %bitcast.20), channel_id=1, replica_groups=mesh['edp'=16,'ep'=16] {'ep'}, dimensions={0} | all-to-all | bytes 983040 | tf_op jit(solution)/shard_map/all_to_all | solution.py:319
  32.6 0.9 copy-done.22
  34.5 2.8 %collective-permute-start.4 = (bf16[48,5120]{1,0:T(8,128)(2,1)S(1)}, bf16[48,5120]{1,0:T(8,128)(2,1)S(1)}, u32[]{:S(2)}, u32[]{:S(2)}) collective-permute-start(bf16[48,5120]{1,0:T(8,128)(2,1)S(1)} %unpack_x.1.refs_0_), channel_id=1, source_target_pairs={{0,96},{16,48},{32,0},{48,80},{64,32},{80,112},{96,64},{112,16},{1... | collective-permute-start | bytes 1474568 | tf_op jit(solution)/shard_map/ppermute | solution.py:31
  37.3 2.1 %send_y.1 = bf16[128,2048]{1,0:T(8,128)(2,1)} custom-call(s32[6,128]{1,0:T(8,128)S(1)} %bitcast.22, bf16[6,128]{1,0:T(8,128)(2,1)S(1)} %bitcast.24, bf16[128,5120]{1,0:T(8,128)(2,1)S(1)} %copy-done.18), custom_call_target="tpu_custom_call" | custom-call | flops 600000000 | bytes 2000000 | tf_op jit(solution)/shard_map/send_y/pallas_call | solution.py:51
  39.4 5.0 %all-to-all-start.1 = ((bf16[16,8,2048]{2,1,0:T(8,128)(2,1)}), bf16[16,8,2048]{2,1,0:T(8,128)(2,1)S(1)}, u32[]{:S(2)}, u32[]{:S(2)}) async-start(bf16[16,8,2048]{2,1,0:T(8,128)(2,1)} %bitcast.7), calls=%async_computation.1 | async-start | bytes 1048576 | tf_op jit(solution)/shard_map/all_to_all | solution.py:319
  44.4 3.6 %collective-permute-done.5.refs_4_ = bf16[48,5120]{1,0:T(8,128)(2,1)S(1)} collective-permute-done((bf16[48,5120]{1,0:T(8,128)(2,1)S(1)}, bf16[48,5120]{1,0:T(8,128)(2,1)S(1)}, u32[]{:S(2)}, u32[]{:S(2)}) %collective-permute-start.5) | collective-permute-done | bytes 491552 | tf_op jit(solution)/shard_map/ppermute | solution.py:31
  48.0 4.0 %collective-permute-start.6 = (bf16[48,5120]{1,0:T(8,128)(2,1)S(1)}, bf16[48,5120]{1,0:T(8,128)(2,1)S(1)}, u32[]{:S(2)}, u32[]{:S(2)}) collective-permute-start(bf16[48,5120]{1,0:T(8,128)(2,1)S(1)} %collective-permute-done.3.refs_1_), channel_id=1, source_target_pairs={{0,32},{16,112},{32,64},{48,16},{64,96},{80,48},{96,0},{112,80},{1... | collective-permute-start | bytes 1474568 | tf_op jit(solution)/shard_map/ppermute | solution.py:31
  52.0 1.1 collective-permute-start.8
  53.0 0.9 collective-permute-start.7
  54.0 8.9 %collective-permute-done.6.refs_2_ = bf16[48,5120]{1,0:T(8,128)(2,1)S(1)} collective-permute-done((bf16[48,5120]{1,0:T(8,128)(2,1)S(1)}, bf16[48,5120]{1,0:T(8,128)(2,1)S(1)}, u32[]{:S(2)}, u32[]{:S(2)}) %collective-permute-start.6) | collective-permute-done | bytes 491552 | tf_op jit(solution)/shard_map/ppermute | solution.py:31
  62.9 2.8 %collective-permute-done.8.refs_7_ = bf16[48,5120]{1,0:T(8,128)(2,1)S(1)} collective-permute-done((bf16[48,5120]{1,0:T(8,128)(2,1)S(1)}, bf16[48,5120]{1,0:T(8,128)(2,1)S(1)}, u32[]{:S(2)}, u32[]{:S(2)}) %collective-permute-start.8) | collective-permute-done | bytes 491552 | tf_op jit(solution)/shard_map/ppermute | solution.py:31
  66.4 1.7 collective-permute-done.7.refs_5_
  69.3 1.9 collective-permute-start.11
  71.1 1.1 collective-permute-start.10
  72.2 1.0 collective-permute-start.9
  73.2 6.7 %collective-permute-done.11.refs_4_ = bf16[48,5248]{1,0:T(8,128)(2,1)S(1)} collective-permute-done((bf16[48,5248]{1,0:T(8,128)(2,1)S(1)}, bf16[48,5248]{1,0:T(8,128)(2,1)S(1)}, u32[]{:S(2)}, u32[]{:S(2)}) %collective-permute-start.11) | collective-permute-done | bytes 503840 | tf_op jit(solution)/shard_map/ppermute | solution.py:31
  79.8 1.9 %collective-permute-done.10.refs_3_ = bf16[48,5248]{1,0:T(8,128)(2,1)S(1)} collective-permute-done((bf16[48,5248]{1,0:T(8,128)(2,1)S(1)}, bf16[48,5248]{1,0:T(8,128)(2,1)S(1)}, u32[]{:S(2)}, u32[]{:S(2)}) %collective-permute-start.10) | collective-permute-done | bytes 503840 | tf_op jit(solution)/shard_map/ppermute | solution.py:31
  82.4 1.1 collective-permute-start.12
  84.2 2.3 %collective-permute-start.16 = (bf16[48,5248]{1,0:T(8,128)(2,1)S(1)}, bf16[48,5248]{1,0:T(8,128)(2,1)S(1)}, u32[]{:S(2)}, u32[]{:S(2)}) collective-permute-start(bf16[48,5248]{1,0:T(8,128)(2,1)S(1)} %collective-permute-done.11.refs_4_), channel_id=1, source_target_pairs={{0,96},{16,48},{32,0},{48,80},{64,32},{80,112},{96,64},{112,16},{1... | collective-permute-start | bytes 1511432 | tf_op jit(solution)/shard_map/ppermute | solution.py:31
  86.5 9.3 %collective-permute-done.13.refs_6_ = bf16[48,5120]{1,0:T(8,128)(2,1)S(1)} collective-permute-done((bf16[48,5120]{1,0:T(8,128)(2,1)}, bf16[48,5120]{1,0:T(8,128)(2,1)S(1)}, u32[]{:S(2)}, u32[]{:S(2)}) %collective-permute-start.13) | collective-permute-done | bytes 491552 | tf_op jit(solution)/shard_map/ppermute | solution.py:31
  95.8 1.9 collective-permute-done.12.refs_2_
  97.7 1.1 collective-permute-start.15
  98.9 1.0 copy-done.12
  99.9 1.0 copy-done.14
  100.9 1.0 copy-done.16
  101.9 6.3 %pre.1 = (f32[192,384]{1,0:T(8,128)S(1)}, f32[192,384]{1,0:T(8,128)S(1)}, bf16[384,5120]{1,0:T(8,128)(2,1)}) custom-call(bf16[48,5120]{1,0:T(8,128)(2,1)S(1)} %unpack_x.1.refs_0_, bf16[48,5120]{1,0:T(8,128)(2,1)S(1)} %collective-permute-done.3.refs_1_, bf16[48,5120]{1,0:T(8,128)(2,1)S(1)} %copy-done.12, bf16[48,5120]{1,0:T(8,128)(2,1)S(1)} %collective-permute-done.4.refs_3_, ...), custom_call_target="tpu_custom_call" | custom-call | flops 1509949440 | bytes 10000000 | tf_op jit(solution)/shard_map/pre/pallas_call | solution.py:51
  109.4 11.0 %main.1 = (bf16[48,5248]{1,0:T(8,128)(2,1)S(1)}, bf16[48,5248]{1,0:T(8,128)(2,1)S(1)}, bf16[48,5248]{1,0:T(8,128)(2,1)S(1)}, bf16[48,5248]{1,0:T(8,128)(2,1)S(1)...) custom-call(bf16[48,5248]{1,0:T(8,128)(2,1)S(1)} %unpack_y.1.refs_0_, ...), custom_call_target="tpu_custom_call" | custom-call | flops 2264924160 | bytes 14000000 | tf_op jit(solution)/shard_map/main/pallas_call | solution.py:51
  122.1 1.2 collective-permute-start.18
  124.2 2.1 %copy-done.2 = bf16[384,5120]{1,0:T(8,128)(2,1)S(1)} copy-done((bf16[384,5120]{1,0:T(8,128)(2,1)S(1)}, bf16[384,5120]{1,0:T(8,128)(2,1)}, u32[]{:S(2)}) %copy-start.2) | copy-done | bytes 3932184
  126.3 3.1 %wgrad_away.1 = bf16[288,5120]{1,0:T(8,128)(2,1)S(1)} custom-call(bf16[192,384]{1,0:T(8,128)(2,1)S(1)} %get-tuple-element.84.hid_ref, bf16[192,384]{1,0:T(8,128)(2,1)S(1)} %get-tuple-element.85.dg_ref, bf16[192,384]{1,0:T(8,128)(2,1)S(1)} %get-tuple-element.86.du_ref, bf16[384,5120]{1,0:T(8,128)(2,1)S(1)} %copy-done.2, bf16[384,5120]{1,0:T(8,128)(2,1)S(1)} %copy-done), custom_call_target="tpu_custom_call" | custom-call | flops 1132462080 | bytes 12000000 | tf_op jit(solution)/shard_map/wgrad_away/pallas_call | solution.py:398
  129.4 2.1 %collective-permute-done.17.refs_1_ = bf16[48,5248]{1,0:T(8,128)(2,1)S(1)} collective-permute-done((bf16[48,5248]{1,0:T(8,128)(2,1)S(1)}, bf16[48,5248]{1,0:T(8,128)(2,1)S(1)}, u32[]{:S(2)}, u32[]{:S(2)}) %collective-permute-start.17) | collective-permute-done | bytes 503840 | tf_op jit(solution)/shard_map/ppermute | solution.py:31
  132.1 1.4 collective-permute-done.19.refs_2_
  134.0 1.2 collective-permute-start.21
  135.2 1.0 copy-done.8
  136.6 2.7 %collective-permute-start.20 = (bf16[48,5248]{1,0:T(8,128)(2,1)S(1)}, bf16[48,5248]{1,0:T(8,128)(2,1)S(1)}, u32[]{:S(2)}, u32[]{:S(2)}) collective-permute-start(bf16[48,5248]{1,0:T(8,128)(2,1)S(1)} %join.3), channel_id=1, source_target_pairs={{0,96},{16,48},{32,0},{48,80},{64,32},{80,112},{96,64},{112,16},{1... | collective-permute-start | bytes 1511432 | tf_op jit(solution)/shard_map/ppermute | solution.py:31
  139.3 8.7 %collective-permute-done.21.refs_3_ = bf16[48,5248]{1,0:T(8,128)(2,1)S(1)} collective-permute-done((bf16[48,5248]{1,0:T(8,128)(2,1)S(1)}, bf16[48,5248]{1,0:T(8,128)(2,1)S(1)}, u32[]{:S(2)}, u32[]{:S(2)}) %collective-permute-start.21) | collective-permute-done | bytes 503840 | tf_op jit(solution)/shard_map/ppermute | solution.py:31
  148.0 2.7 %collective-permute-done.20.refs_1_ = bf16[48,5248]{1,0:T(8,128)(2,1)S(1)} collective-permute-done((bf16[48,5248]{1,0:T(8,128)(2,1)S(1)}, bf16[48,5248]{1,0:T(8,128)(2,1)S(1)}, u32[]{:S(2)}, u32[]{:S(2)}) %collective-permute-start.20) | collective-permute-done | bytes 503840 | tf_op jit(solution)/shard_map/ppermute | solution.py:31
  151.7 3.0 %collective-permute-start.23 = (bf16[48,5248]{1,0:T(8,128)(2,1)S(1)}, bf16[48,5248]{1,0:T(8,128)(2,1)S(1)}, u32[]{:S(2)}, u32[]{:S(2)}) collective-permute-start(bf16[48,5248]{1,0:T(8,128)(2,1)S(1)} %join.5), channel_id=1, source_target_pairs={{0,96},{16,48},{32,0},{48,80},{64,32},{80,112},{96,64},{112,16},{1... | collective-permute-start | bytes 1511432 | tf_op jit(solution)/shard_map/ppermute | solution.py:31
  154.7 6.5 %collective-permute-done.23.refs_1_ = bf16[48,5248]{1,0:T(8,128)(2,1)S(1)} collective-permute-done((bf16[48,5248]{1,0:T(8,128)(2,1)S(1)}, bf16[48,5248]{1,0:T(8,128)(2,1)S(1)}, u32[]{:S(2)}, u32[]{:S(2)}) %collective-permute-start.23) | collective-permute-done | bytes 503840 | tf_op jit(solution)/shard_map/ppermute | solution.py:31
  161.2 1.3 last.1
  162.5 9.7 %all-to-all-start.2 = ((bf16[16,8,2048]{2,1,0:T(8,128)(2,1)}), bf16[16,8,2048]{2,1,0:T(8,128)(2,1)}, u32[]{:S(2)}, u32[]{:S(2)}) async-start(bf16[16,8,2048]{2,1,0:T(8,128)(2,1)} %bitcast.9), calls=%async_computation.2 | async-start | bytes 1048576 | tf_op jit(solution)/shard_map/all_to_all | solution.py:319
  172.2 2.1 %copy-done.1 = bf16[384,5120]{1,0:T(8,128)(2,1)S(1)} copy-done((bf16[384,5120]{1,0:T(8,128)(2,1)S(1)}, bf16[384,5120]{1,0:T(8,128)(2,1)}, u32[]{:S(2)}) %copy-start.1) | copy-done | bytes 3932184
  174.3 2.1 %copy-done.3 = bf16[384,5120]{1,0:T(8,128)(2,1)S(1)} copy-done((bf16[384,5120]{1,0:T(8,128)(2,1)S(1)}, bf16[384,5120]{1,0:T(8,128)(2,1)}, u32[]{:S(2)}) %copy-start.3) | copy-done | bytes 3932184
  176.4 3.9 %wgrad_mine.1 = (bf16[96,5120]{1,0:T(8,128)(2,1)}, bf16[96,5120]{1,0:T(8,128)(2,1)}, bf16[96,5120]{1,0:T(8,128)(2,1)}) custom-call(bf16[192,384]{1,0:T(8,128)(2,1)S(1)} %get-tuple-element.84.hid_ref, bf16[192,384]{1,0:T(8,128)(2,1)S(1)} %get-tuple-element.85.dg_ref, bf16[192,384]{1,0:T(8,128)(2,1)S(1)} %get-tuple-element.86.du_ref, ...), custom_call_target="tpu_custom_call" | custom-call | flops 1132462080 | bytes 12000000 | tf_op jit(solution)/shard_map/wgrad_mine/pallas_call | solution.py:398
  180.3 7.7 %all-to-all-done.2 = bf16[16,8,2048]{2,1,0:T(8,128)(2,1)} async-done(((bf16[16,8,2048]{2,1,0:T(8,128)(2,1)}), bf16[16,8,2048]{2,1,0:T(8,128)(2,1)}, u32[]{:S(2)}, u32[]{:S(2)}) %all-to-all-start.2) | async-done | bytes 524320 | tf_op jit(solution)/shard_map/all_to_all | solution.py:319
  188.0 3.5 %final.1 = (bf16[128,5120]{1,0:T(8,128)(2,1)}, bf16[6,128]{1,0:T(8,128)(2,1)}) custom-call(s32[6,128]{1,0:T(8,128)S(1)} %bitcast.23, bf16[128,2048]{1,0:T(8,128)(2,1)} %bitcast.10.in_ref), custom_call_target="tpu_custom_call" | custom-call | flops 600000000 | bytes 2000000 | tf_op jit(solution)/shard_map/final/pallas_call | solution.py:51
  (82 shorter events, 11.8 us)
Async XLA Ops:
  0.6 36.6 %copy-start.20 = (s32[128,6]{0,1:T(8,128)S(1)}, s32[128,6]{0,1:T(8,128)}, u32[]{:S(2)}) copy-start(s32[128,6]{0,1:T(8,128)} %param.10) | copy-start | bytes 9220
  0.6 36.6 %copy-start.21 = (bf16[128,6]{0,1:T(8,128)(2,1)S(1)}, bf16[128,6]{0,1:T(8,128)(2,1)}, u32[]{:S(2)}) copy-start(bf16[128,6]{0,1:T(8,128)(2,1)} %param.9) | copy-start | bytes 4612
  0.7 31.9 %collective-permute-start = (bf16[96,5120]{1,0:T(8,128)(2,1)}, bf16[96,5120]{1,0:T(8,128)(2,1)S(1)}, u32[]{:S(2)}, u32[]{:S(2)}) collective-permute-start(bf16[96,5120]{1,0:T(8,128)(2,1)} %bitcast.15), channel_id=1, source_target_pairs={{0,16},{16,0},{32,48},{48,32},{64,80},{80,64},{96,112},{112,96},{1... | collective-permute-start | bytes 2949128 | tf_op jit(solution)/shard_map/ppermute | solution.py:31
  0.8 31.8 %collective-permute-start.1 = (bf16[96,5120]{1,0:T(8,128)(2,1)}, bf16[96,5120]{1,0:T(8,128)(2,1)S(1)}, u32[]{:S(2)}, u32[]{:S(2)}) collective-permute-start(bf16[96,5120]{1,0:T(8,128)(2,1)} %bitcast.25), channel_id=1, source_target_pairs={{0,16},{16,0},{32,48},{48,32},{64,80},{80,64},{96,112},{112,96},{1... | collective-permute-start | bytes 2949128 | tf_op jit(solution)/shard_map/ppermute | solution.py:31
  1.2 31.4 %collective-permute-start.2 = (bf16[96,5120]{1,0:T(8,128)(2,1)}, bf16[96,5120]{1,0:T(8,128)(2,1)S(1)}, u32[]{:S(2)}, u32[]{:S(2)}) collective-permute-start(bf16[96,5120]{1,0:T(8,128)(2,1)} %bitcast.28), channel_id=1, source_target_pairs={{0,16},{16,0},{32,48},{48,32},{64,80},{80,64},{96,112},{112,96},{1... | collective-permute-start | bytes 2949128 | tf_op jit(solution)/shard_map/ppermute | solution.py:31
  1.4 1.3 copy-start.17
  3.4 33.9 %copy-start.18 = (bf16[128,5120]{1,0:T(8,128)(2,1)S(1)}, bf16[128,5120]{1,0:T(8,128)(2,1)}, u32[]{:S(2)}) copy-start(bf16[128,5120]{1,0:T(8,128)(2,1)} %refs_2_) | copy-start | bytes 3932164
  4.7 94.2 %copy-start.4 = (bf16[1,96,5120]{2,1,0:T(8,128)(2,1)S(1)}, bf16[1,96,5120]{2,1,0:T(8,128)(2,1)}, u32[]{:S(2)}) copy-start(bf16[1,96,5120]{2,1,0:T(8,128)(2,1)} %param.11) | copy-start | bytes 2949124
  32.6 1.3 copy-start.23
  33.5 5.8 %copy-start.24 = (bf16[96,5120]{1,0:T(8,128)(2,1)}, bf16[96,5120]{1,0:T(8,128)(2,1)S(1)}, u32[]{:S(2)}) copy-start(bf16[96,5120]{1,0:T(8,128)(2,1)S(1)} %collective-permute-done.2.refs_9_) | copy-start | bytes 2949124
  33.9 14.1 %collective-permute-start.5 = (bf16[48,5120]{1,0:T(8,128)(2,1)S(1)}, bf16[48,5120]{1,0:T(8,128)(2,1)S(1)}, u32[]{:S(2)}, u32[]{:S(2)}) collective-permute-start(bf16[48,5120]{1,0:T(8,128)(2,1)S(1)} %unpack_x.1.refs_0_), channel_id=1, source_target_pairs={{0,128},{16,144},{32,160},{48,176},{64,192},{80,208},{96,224},{112... | collective-permute-start | bytes 1474568 | tf_op jit(solution)/shard_map/ppermute | solution.py:31
  34.5 13.5 %collective-permute-start.4 = (bf16[48,5120]{1,0:T(8,128)(2,1)S(1)}, bf16[48,5120]{1,0:T(8,128)(2,1)S(1)}, u32[]{:S(2)}, u32[]{:S(2)}) collective-permute-start(bf16[48,5120]{1,0:T(8,128)(2,1)S(1)} %unpack_x.1.refs_0_), channel_id=1, source_target_pairs={{0,96},{16,48},{32,0},{48,80},{64,32},{80,112},{96,64},{112,16},{1... | collective-permute-start | bytes 1474568 | tf_op jit(solution)/shard_map/ppermute | solution.py:31
  37.2 10.8 %collective-permute-start.3 = (bf16[48,5120]{1,0:T(8,128)(2,1)S(1)}, bf16[48,5120]{1,0:T(8,128)(2,1)S(1)}, u32[]{:S(2)}, u32[]{:S(2)}) collective-permute-start(bf16[48,5120]{1,0:T(8,128)(2,1)S(1)} %unpack_x.1.refs_0_), channel_id=1, source_target_pairs={{0,32},{16,112},{32,64},{48,16},{64,96},{80,48},{96,0},{112,80},{1... | collective-permute-start | bytes 1474568 | tf_op jit(solution)/shard_map/ppermute | solution.py:31
  39.4 29.5 %all-to-all-start.1 = ((bf16[16,8,2048]{2,1,0:T(8,128)(2,1)}), bf16[16,8,2048]{2,1,0:T(8,128)(2,1)S(1)}, u32[]{:S(2)}, u32[]{:S(2)}) async-start(bf16[16,8,2048]{2,1,0:T(8,128)(2,1)} %bitcast.7), calls=%async_computation.1 | async-start | bytes 1048576 | tf_op jit(solution)/shard_map/all_to_all | solution.py:319
  48.0 14.9 %collective-permute-start.6 = (bf16[48,5120]{1,0:T(8,128)(2,1)S(1)}, bf16[48,5120]{1,0:T(8,128)(2,1)S(1)}, u32[]{:S(2)}, u32[]{:S(2)}) collective-permute-start(bf16[48,5120]{1,0:T(8,128)(2,1)S(1)} %collective-permute-done.3.refs_1_), channel_id=1, source_target_pairs={{0,32},{16,112},{32,64},{48,16},{64,96},{80,48},{96,0},{112,80},{1... | collective-permute-start | bytes 1474568 | tf_op jit(solution)/shard_map/ppermute | solution.py:31
  52.0 13.7 %collective-permute-start.8 = (bf16[48,5120]{1,0:T(8,128)(2,1)S(1)}, bf16[48,5120]{1,0:T(8,128)(2,1)S(1)}, u32[]{:S(2)}, u32[]{:S(2)}) collective-permute-start(bf16[48,5120]{1,0:T(8,128)(2,1)S(1)} %collective-permute-done.5.refs_4_), channel_id=1, source_target_pairs={{0,96},{16,48},{32,0},{48,80},{64,32},{80,112},{96,64},{112,16},{1... | collective-permute-start | bytes 1474568 | tf_op jit(solution)/shard_map/ppermute | solution.py:31
  53.0 15.1 %collective-permute-start.7 = (bf16[48,5120]{1,0:T(8,128)(2,1)S(1)}, bf16[48,5120]{1,0:T(8,128)(2,1)S(1)}, u32[]{:S(2)}, u32[]{:S(2)}) collective-permute-start(bf16[48,5120]{1,0:T(8,128)(2,1)S(1)} %collective-permute-done.5.refs_4_), channel_id=1, source_target_pairs={{0,32},{16,112},{32,64},{48,16},{64,96},{80,48},{96,0},{112,80},{1... | collective-permute-start | bytes 1474568 | tf_op jit(solution)/shard_map/ppermute | solution.py:31
  62.9 2.8 %copy-start.11 = (bf16[48,5120]{1,0:T(8,128)(2,1)}, bf16[48,5120]{1,0:T(8,128)(2,1)S(1)}, u32[]{:S(2)}) copy-start(bf16[48,5120]{1,0:T(8,128)(2,1)S(1)} %collective-permute-done.6.refs_2_) | copy-start | bytes 1474564
  69.3 10.6 %collective-permute-start.11 = (bf16[48,5248]{1,0:T(8,128)(2,1)S(1)}, bf16[48,5248]{1,0:T(8,128)(2,1)S(1)}, u32[]{:S(2)}, u32[]{:S(2)}) collective-permute-start(bf16[48,5248]{1,0:T(8,128)(2,1)S(1)} %unpack_y.1.refs_0_), channel_id=1, source_target_pairs={{0,128},{16,144},{32,160},{48,176},{64,192},{80,208},{96,224},{112... | collective-permute-start | bytes 1511432 | tf_op jit(solution)/shard_map/ppermute | solution.py:31
  71.1 10.6 %collective-permute-start.10 = (bf16[48,5248]{1,0:T(8,128)(2,1)S(1)}, bf16[48,5248]{1,0:T(8,128)(2,1)S(1)}, u32[]{:S(2)}, u32[]{:S(2)}) collective-permute-start(bf16[48,5248]{1,0:T(8,128)(2,1)S(1)} %unpack_y.1.refs_0_), channel_id=1, source_target_pairs={{0,96},{16,48},{32,0},{48,80},{64,32},{80,112},{96,64},{112,16},{1... | collective-permute-start | bytes 1511432 | tf_op jit(solution)/shard_map/ppermute | solution.py:31
  72.2 10.2 %collective-permute-start.9 = (bf16[48,5248]{1,0:T(8,128)(2,1)S(1)}, bf16[48,5248]{1,0:T(8,128)(2,1)S(1)}, u32[]{:S(2)}, u32[]{:S(2)}) collective-permute-start(bf16[48,5248]{1,0:T(8,128)(2,1)S(1)} %unpack_y.1.refs_0_), channel_id=1, source_target_pairs={{0,32},{16,112},{32,64},{48,16},{64,96},{80,48},{96,0},{112,80},{1... | collective-permute-start | bytes 1511432 | tf_op jit(solution)/shard_map/ppermute | solution.py:31
  79.8 28.5 %copy-start.25 = (bf16[48,5248]{1,0:T(8,128)(2,1)}, bf16[48,5248]{1,0:T(8,128)(2,1)S(1)}, u32[]{:S(2)}) copy-start(bf16[48,5248]{1,0:T(8,128)(2,1)S(1)} %collective-permute-done.11.refs_4_) | copy-start | bytes 1511428
  81.8 26.5 %copy-start.26 = (bf16[48,5248]{1,0:T(8,128)(2,1)}, bf16[48,5248]{1,0:T(8,128)(2,1)S(1)}, u32[]{:S(2)}) copy-start(bf16[48,5248]{1,0:T(8,128)(2,1)S(1)} %collective-permute-done.10.refs_3_) | copy-start | bytes 1511428
  82.4 15.3 %collective-permute-start.12 = (bf16[48,5248]{1,0:T(8,128)(2,1)S(1)}, bf16[48,5248]{1,0:T(8,128)(2,1)S(1)}, u32[]{:S(2)}, u32[]{:S(2)}) collective-permute-start(bf16[48,5248]{1,0:T(8,128)(2,1)S(1)} %collective-permute-done.9.refs_1_), channel_id=1, source_target_pairs={{0,32},{16,112},{32,64},{48,16},{64,96},{80,48},{96,0},{112,80},{1... | collective-permute-start | bytes 1511432 | tf_op jit(solution)/shard_map/ppermute | solution.py:31
  83.4 12.4 %collective-permute-start.13 = (bf16[48,5120]{1,0:T(8,128)(2,1)}, bf16[48,5120]{1,0:T(8,128)(2,1)S(1)}, u32[]{:S(2)}, u32[]{:S(2)}) collective-permute-start(bf16[48,5120]{1,0:T(8,128)(2,1)} %copy-done.11), channel_id=1, source_target_pairs={{0,128},{16,144},{32,160},{48,176},{64,192},{80,208},{96,224},{112... | collective-permute-start | bytes 1474568 | tf_op jit(solution)/shard_map/ppermute | solution.py:31
  84.2 24.1 %collective-permute-start.16 = (bf16[48,5248]{1,0:T(8,128)(2,1)S(1)}, bf16[48,5248]{1,0:T(8,128)(2,1)S(1)}, u32[]{:S(2)}, u32[]{:S(2)}) collective-permute-start(bf16[48,5248]{1,0:T(8,128)(2,1)S(1)} %collective-permute-done.11.refs_4_), channel_id=1, source_target_pairs={{0,96},{16,48},{32,0},{48,80},{64,32},{80,112},{96,64},{112,16},{1... | collective-permute-start | bytes 1511432 | tf_op jit(solution)/shard_map/ppermute | solution.py:31
  86.5 21.8 %collective-permute-start.14 = (bf16[48,5248]{1,0:T(8,128)(2,1)S(1)}, bf16[48,5248]{1,0:T(8,128)(2,1)S(1)}, u32[]{:S(2)}, u32[]{:S(2)}) collective-permute-start(bf16[48,5248]{1,0:T(8,128)(2,1)S(1)} %collective-permute-done.11.refs_4_), channel_id=1, source_target_pairs={{0,32},{16,112},{32,64},{48,16},{64,96},{80,48},{96,0},{112,80},{1... | collective-permute-start | bytes 1511432 | tf_op jit(solution)/shard_map/ppermute | solution.py:31
  97.7 10.6 %copy-start.27 = (bf16[48,5248]{1,0:T(8,128)(2,1)}, bf16[48,5248]{1,0:T(8,128)(2,1)S(1)}, u32[]{:S(2)}) copy-start(bf16[48,5248]{1,0:T(8,128)(2,1)S(1)} %collective-permute-done.12.refs_2_) | copy-start | bytes 1511428
  97.7 10.6 %collective-permute-start.15 = (bf16[48,5248]{1,0:T(8,128)(2,1)S(1)}, bf16[48,5248]{1,0:T(8,128)(2,1)S(1)}, u32[]{:S(2)}, u32[]{:S(2)}) collective-permute-start(bf16[48,5248]{1,0:T(8,128)(2,1)S(1)} %collective-permute-done.12.refs_2_), channel_id=1, source_target_pairs={{0,128},{16,144},{32,160},{48,176},{64,192},{80,208},{96,224},{112... | collective-permute-start | bytes 1511432 | tf_op jit(solution)/shard_map/ppermute | solution.py:31
  108.3 1.1 copy-start.28
  109.4 14.7 %copy-start = (bf16[384,5120]{1,0:T(8,128)(2,1)S(1)}, bf16[384,5120]{1,0:T(8,128)(2,1)}, u32[]{:S(2)}) copy-start(bf16[384,5120]{1,0:T(8,128)(2,1)} %get-tuple-element.88.x_ref) | copy-start | bytes 11796484
  121.2 8.1 %copy-start.5 = (bf16[48,5248]{1,0:T(8,128)(2,1)}, bf16[48,5248]{1,0:T(8,128)(2,1)S(1)}, u32[]{:S(2)}) copy-start(bf16[48,5248]{1,0:T(8,128)(2,1)S(1)} %get-tuple-element.77.refs_0_) | copy-start | bytes 1511428
  121.2 8.1 %copy-start.7 = (bf16[48,5248]{1,0:T(8,128)(2,1)}, bf16[48,5248]{1,0:T(8,128)(2,1)S(1)}, u32[]{:S(2)}) copy-start(bf16[48,5248]{1,0:T(8,128)(2,1)S(1)} %get-tuple-element.79.refs_0_) | copy-start | bytes 1511428
  121.2 10.2 %collective-permute-start.17 = (bf16[48,5248]{1,0:T(8,128)(2,1)S(1)}, bf16[48,5248]{1,0:T(8,128)(2,1)S(1)}, u32[]{:S(2)}, u32[]{:S(2)}) collective-permute-start(bf16[48,5248]{1,0:T(8,128)(2,1)S(1)} %get-tuple-element.80), channel_id=1, source_target_pairs={{0,128},{16,144},{32,160},{48,176},{64,192},{80,208},{96,224},{112... | collective-permute-start | bytes 1511432 | tf_op jit(solution)/shard_map/ppermute | solution.py:31
  122.1 10.0 %collective-permute-start.18 = (bf16[48,5248]{1,0:T(8,128)(2,1)S(1)}, bf16[48,5248]{1,0:T(8,128)(2,1)S(1)}, u32[]{:S(2)}, u32[]{:S(2)}) collective-permute-start(bf16[48,5248]{1,0:T(8,128)(2,1)S(1)} %get-tuple-element.81), channel_id=1, source_target_pairs={{0,96},{16,48},{32,0},{48,80},{64,32},{80,112},{96,64},{112,16},{1... | collective-permute-start | bytes 1511432 | tf_op jit(solution)/shard_map/ppermute | solution.py:31
  123.4 10.2 %collective-permute-start.19 = (bf16[48,5248]{1,0:T(8,128)(2,1)S(1)}, bf16[48,5248]{1,0:T(8,128)(2,1)S(1)}, u32[]{:S(2)}, u32[]{:S(2)}) collective-permute-start(bf16[48,5248]{1,0:T(8,128)(2,1)S(1)} %get-tuple-element.82), channel_id=1, source_target_pairs={{0,32},{16,112},{32,64},{48,16},{64,96},{80,48},{96,0},{112,80},{1... | collective-permute-start | bytes 1511432 | tf_op jit(solution)/shard_map/ppermute | solution.py:31
  124.2 2.1 %copy-start.2 = (bf16[384,5120]{1,0:T(8,128)(2,1)S(1)}, bf16[384,5120]{1,0:T(8,128)(2,1)}, u32[]{:S(2)}) copy-start(bf16[384,5120]{1,0:T(8,128)(2,1)} %get-tuple-element.87.py_ref) | copy-start | bytes 11796484
  126.3 7.3 %copy-start.10 = (bf16[48,5248]{1,0:T(8,128)(2,1)S(1)}, bf16[48,5248]{1,0:T(8,128)(2,1)}, u32[]{:S(2)}) copy-start(bf16[48,5248]{1,0:T(8,128)(2,1)} %copy-done.9) | copy-start | bytes 1511428
  131.4 29.8 %copy-start.6 = (bf16[48,5248]{1,0:T(8,128)(2,1)S(1)}, bf16[48,5248]{1,0:T(8,128)(2,1)}, u32[]{:S(2)}) copy-start(bf16[48,5248]{1,0:T(8,128)(2,1)} %copy-done.5) | copy-start | bytes 1511428
  133.5 28.9 %collective-permute-start.24 = (bf16[288,5120]{1,0:T(8,128)(2,1)S(1)}, bf16[288,5120]{1,0:T(8,128)(2,1)S(1)}, u32[]{:S(2)}, u32[]{:S(2)}) collective-permute-start(bf16[288,5120]{1,0:T(8,128)(2,1)S(1)} %wgrad_away.1), channel_id=1, source_target_pairs={{0,16},{16,0},{32,48},{48,32},{64,80},{80,64},{96,112},{112,96},{1... | collective-permute-start | bytes 8847368 | tf_op jit(solution)/shard_map/ppermute | solution.py:31
  134.0 14.0 %collective-permute-start.21 = (bf16[48,5248]{1,0:T(8,128)(2,1)S(1)}, bf16[48,5248]{1,0:T(8,128)(2,1)S(1)}, u32[]{:S(2)}, u32[]{:S(2)}) collective-permute-start(bf16[48,5248]{1,0:T(8,128)(2,1)S(1)} %join.4), channel_id=1, source_target_pairs={{0,128},{16,144},{32,160},{48,176},{64,192},{80,208},{96,224},{112... | collective-permute-start | bytes 1511432 | tf_op jit(solution)/shard_map/ppermute | solution.py:31
  135.2 1.0 copy-start.8
  136.6 14.1 %collective-permute-start.20 = (bf16[48,5248]{1,0:T(8,128)(2,1)S(1)}, bf16[48,5248]{1,0:T(8,128)(2,1)S(1)}, u32[]{:S(2)}, u32[]{:S(2)}) collective-permute-start(bf16[48,5248]{1,0:T(8,128)(2,1)S(1)} %join.3), channel_id=1, source_target_pairs={{0,96},{16,48},{32,0},{48,80},{64,32},{80,112},{96,64},{112,16},{1... | collective-permute-start | bytes 1511432 | tf_op jit(solution)/shard_map/ppermute | solution.py:31
  139.3 12.2 %collective-permute-start.22 = (bf16[48,5248]{1,0:T(8,128)(2,1)S(1)}, bf16[48,5248]{1,0:T(8,128)(2,1)S(1)}, u32[]{:S(2)}, u32[]{:S(2)}) collective-permute-start(bf16[48,5248]{1,0:T(8,128)(2,1)S(1)} %get-tuple-element.93), channel_id=1, source_target_pairs={{0,32},{16,112},{32,64},{48,16},{64,96},{80,48},{96,0},{112,80},{1... | collective-permute-start | bytes 1511432 | tf_op jit(solution)/shard_map/ppermute | solution.py:31
  151.7 9.5 %collective-permute-start.23 = (bf16[48,5248]{1,0:T(8,128)(2,1)S(1)}, bf16[48,5248]{1,0:T(8,128)(2,1)S(1)}, u32[]{:S(2)}, u32[]{:S(2)}) collective-permute-start(bf16[48,5248]{1,0:T(8,128)(2,1)S(1)} %join.5), channel_id=1, source_target_pairs={{0,96},{16,48},{32,0},{48,80},{64,32},{80,112},{96,64},{112,16},{1... | collective-permute-start | bytes 1511432 | tf_op jit(solution)/shard_map/ppermute | solution.py:31
  162.5 25.6 %all-to-all-start.2 = ((bf16[16,8,2048]{2,1,0:T(8,128)(2,1)}), bf16[16,8,2048]{2,1,0:T(8,128)(2,1)}, u32[]{:S(2)}, u32[]{:S(2)}) async-start(bf16[16,8,2048]{2,1,0:T(8,128)(2,1)} %bitcast.9), calls=%async_computation.2 | async-start | bytes 1048576 | tf_op jit(solution)/shard_map/all_to_all | solution.py:319
  172.1 2.1 %copy-start.1 = (bf16[384,5120]{1,0:T(8,128)(2,1)S(1)}, bf16[384,5120]{1,0:T(8,128)(2,1)}, u32[]{:S(2)}) copy-start(bf16[384,5120]{1,0:T(8,128)(2,1)} %get-tuple-element.88.x_ref) | copy-start | bytes 11796484
  174.3 2.1 %copy-start.3 = (bf16[384,5120]{1,0:T(8,128)(2,1)S(1)}, bf16[384,5120]{1,0:T(8,128)(2,1)}, u32[]{:S(2)}) copy-start(bf16[384,5120]{1,0:T(8,128)(2,1)} %get-tuple-element.87.py_ref) | copy-start | bytes 11796484
  (10 other events, 8.9 us)

commit v4 on v3

--- a/solution.py
+++ b/solution.py
@@ -168,8 +168,8 @@
 
 def main_kernel(*refs):
     ys, ds, ws, (gate_ref, up_ref) = refs[0:8], refs[8:10], refs[10:14], refs[14:16]
-    outs, (dg_ref, du_ref, hid_ref, py_ref) = refs[16:24], refs[24:28]
-    y_all, d_all, w_all, acc, y_sems, d_sems, w_sems = refs[28:]
+    outs, (dg_ref, du_ref, hid_ref, y_all) = refs[16:24], refs[24:28]
+    d_all, w_all, acc, y_sems, d_sems, w_sems = refs[28:]
     y_plan = [stacked(ys, y_all, y_sems, n) for n in range(BLOCKS)]
     d_plan = [stacked(ds, d_all, d_sems, n) for n in range(BLOCKS)]
     w_plan = [stacked(ws, w_all, w_sems, n) for n in range(BLOCKS)]
@@ -213,7 +213,6 @@
     tail = jnp.transpose(tail).astype(BF16)
     for k in range(8):
         outs[k][:, width:] = tail[k * rows : (k + 1) * rows, :]
-    prob_col = probs[:, 0:1]
     for n in range(BLOCKS):
         ready(w_plan[n])
         for m in range(2):
@@ -221,15 +220,15 @@
             got = dot(both, w_all[:, cols]).astype(BF16)
             for k in range(8):
                 outs[k][:, cols] = got[k * rows : (k + 1) * rows, :]
-            py_ref[:, cols] = (prob_col * y_all[:, cols].astype(F32)).astype(BF16)
-
-
-def wgrad_kernel(hid_ref, dg_ref, du_ref, py_ref, x_ref, *rest, away):
+
+
+def wgrad_kernel(hid_ref, dg_ref, du_ref, y_ref, prob_ref, x_ref, *rest, away):
     hid = hid_ref.shape[0] // 2
     first = hid if away else 0
-    sides = ((dg_ref, x_ref), (du_ref, x_ref), (hid_ref, py_ref))
+    scaled = (prob_ref[:, 0:1].astype(F32) * y_ref[...].astype(F32)).astype(BF16)
+    sides = ((dg_ref, x_ref[...]), (du_ref, x_ref[...]), (hid_ref, scaled))
     for i, (left, right) in enumerate(sides):
-        total = dot(left[first : first + hid, :], right[...])
+        total = dot(left[first : first + hid, :], right)
         if away:
             rest[0][i * hid : (i + 1) * hid, :] = total.astype(BF16)
         else:
@@ -337,24 +336,23 @@
     got_x, core_g, core_u, core_d = together((exchange(send_x), core_g, core_u, core_d))
     x = unpack(got_x, width, "unpack_x")
     xa, xb, oth = hop(x, X_A), hop(x, X_B), hop(x, Z_SWAP)
-    x_now, cot_now = together((x, cotangent))
     send_y = call(
         functools.partial(send_kernel, with_p=True),
         shape((LANES, CAP * group + LANES), BF16),
         "send_y",
         cost=(6 * 10**8, 2 * 10**6),
-    )(ids_t, probs_t, cot_now)
+    )(ids_t, probs_t, cotangent)
+    send_y, x_now = together((send_y, x))
     got_y = exchange(send_y)
     xa, xb, oth = together((xa, xb, oth))
-    far, oa, ob = hop(xa, X_A), hop(oth, X_A), hop(oth, X_B)
+    ob, oa, far = hop(oth, X_B), hop(xa, Z_SWAP), hop(xa, X_A)
+    o_far = hop(ob, X_B)
     far, oa, ob, got_y = together((far, oa, ob, got_y))
     y = unpack(got_y, wide, "unpack_y")
     ya, yb, y_oth = hop(y, X_A), hop(y, X_B), hop(y, Z_SWAP)
-    ya, yb, y_oth, far = together((ya, yb, y_oth, far))
-    y_far, yoa, yob = hop(ya, X_A), hop(y_oth, X_A), hop(y_oth, X_B)
-    o_far = hop(far, Z_SWAP)
-    y_far, o_far = together((y_far, o_far))
-    yo_far = hop(y_far, Z_SWAP)
+    ya, yb, y_oth, o_far = together((ya, yb, y_oth, o_far))
+    yob, yoa, y_far = hop(y_oth, X_B), hop(ya, Z_SWAP), hop(ya, X_A)
+    yo_far = hop(yob, X_B)
     gate, up, x_all = call(
         pre_kernel,
         [shape((2 * hid, total), F32)] * 2 + [shape((total, width), BF16)],
@@ -363,14 +361,13 @@
         specs=[any_spec] * 12,
         cost=(2 * work, 10 * 10**6),
     )(x, xa, far, xb, oth, oa, o_far, ob, g, core_g, u, core_u)
-    *parts, d_gate, d_up, hidden, py = call(
+    *parts, d_gate, d_up, hidden, y_all = call(
         main_kernel,
         [shape((rows, wide), BF16)] * 8
         + [shape((2 * hid, total), BF16)] * 3
-        + [shape((total, width), BF16)],
+        + [shape((total, wide), BF16)],
         "main",
         scratch=[
-            pltpu.VMEM((total, wide), BF16),
             pltpu.VMEM((2 * hid, width), BF16),
             pltpu.VMEM((4 * hid, width), BF16),
             pltpu.VMEM((2 * hid, total), F32),
@@ -393,20 +390,23 @@
         def part(height):
             return pl.BlockSpec((height, cols), lambda n: (0, n))
 
+        prob = pl.BlockSpec((total, LANES), lambda n: (0, width // LANES))
         left = pl.BlockSpec((2 * hid, total), lambda n: (0, 0))
         out = [shape((hid, width), BF16)] * 3 if came else shape((3 * hid, width), BF16)
         return pl.pallas_call(
             functools.partial(wgrad_kernel, away=not came),
             out_shape=out,
             grid=(blocks,),
-            in_specs=[left] * 3 + [part(total)] * 2 + [part(3 * hid)] * len(came),
+            in_specs=[left] * 3
+            + [part(total), prob, part(total)]
+            + [part(3 * hid)] * len(came),
             out_specs=[part(hid)] * 3 if came else part(3 * hid),
             compiler_params=pltpu.CompilerParams(vmem_limit_bytes=32 * 1024 * 1024),
             name="wgrad_mine" if came else "wgrad_away",
             cost_estimate=pl.CostEstimate(
                 flops=work * 3 // 2, bytes_accessed=12 * 10**6, transcendentals=0
             ),
-        )(hidden, d_gate, d_up, py, x_all, *came)
+        )(hidden, d_gate, d_up, y_all, y_all, x_all, *came)
 
     def join(*a):
         return call(
@@ -422,16 +422,16 @@
     of, oa, ob, pb, away = together((of, oa, ob, pb, away))
     f, oz = hop(join(far, of), X_B), hop(join(oth, oa, ob), Z_SWAP)
     pb = hop(pb, X_A)
+    f, oz, pb, away = together((f, oz, pb, away))
+    pa = hop(join(pa, f), X_B)
     came = hop(away, C_SWAP)
-    f, oz, pb = together((f, oz, pb))
-    pa = hop(join(pa, f), X_B)
     last = call(
         functools.partial(last_kernel, group=group),
         shape((LANES, CAP * group + LANES), BF16),
         "last",
         cost=(10**8, 3 * 10**6),
     )(own, pa, pb, oz)
-    last, came = together((last, came))
+    last, hidden = together((last, hidden))
     back = exchange(last)
     g_grad, u_grad, d_grad = wgrad(came)
     back, g_grad, u_grad, d_grad = together((back, g_grad, u_grad, d_grad))

time: 194 us -> 195 us (level)
  blocking collectives: 27.9 us -> 0 us
  waiting for transfers between devices: 67.9 us -> 95.6 us
  starting transfers between devices: 43.7 us -> 52.7 us
  local copies, waits for them, and re-layouts: 16.9 us -> 9.49 us
    all_to_all x1 -> x0, blocking collectives: 27.9 us -> none  [exchange(): a = lax.all_to_all(a, 'ep', split_axis=0, concat_axis=0, tiled=True)]
    all_to_all x2 -> x3, waiting for transfers between devices: 7.75 us -> 28.1 us  [exchange(): a = lax.all_to_all(a, 'ep', split_axis=0, concat_axis=0, tiled=True)]
    all_to_all x2 -> x3, starting transfers between devices: 14.7 us -> 22.6 us  [exchange(): a = lax.all_to_all(a, 'ep', split_axis=0, concat_axis=0, tiled=True)]
    ppermute x25, waiting for transfers between devices: 60.1 us -> 67.6 us  [hop(): return lax.ppermute(a, 'edp', perm)]
    unnamed x62 -> x32, local copies, waits for them, and re-layouts: 16.9 us -> 9.49 us
  transfers between devices with their start and end apart: 27 -> 28, of which waited for: 17 -> 15; matrix products, arithmetic and copies ran while one was open for 0% -> 0% of each run, Pallas kernels for 10% -> 11%
where the time goes in v4:
time: 195 us; the launch traced here: 194 us
  waiting for transfers between devices  95.6 us (49%)
  starting transfers between devices  52.7 us (27%)
  Pallas kernels  35.1 us (18%)
  local copies, waits for them, and re-layouts  9.49 us (5%)
    ppermute x25, waiting for transfers between devices, hop(): return lax.ppermute(a, 'edp', perm)  67.6 us
    ppermute x25, starting transfers between devices, hop(): return lax.ppermute(a, 'edp', perm)  30.2 us
    all_to_all x3, waiting for transfers between devices, exchange(): a = lax.all_to_all(a, 'ep', split_axis=0, concat_axis=0, tiled=True)  28.1 us
    pallas_call x11, Pallas kernels, run(): pl.pallas_call(kernel, out_shape=outs, in_specs=[one] * len(args) if spec...  26.5 us
    all_to_all x3, starting transfers between devices, exchange(): a = lax.all_to_all(a, 'ep', split_axis=0, concat_axis=0, tiled=True)  22.6 us
    unnamed x32, local copies, waits for them, and re-layouts  9.49 us
    pallas_call x2, Pallas kernels, wgrad(): pl.pallas_call(functools.partial(wgrad_kernel, away=not came), out_shape=...  8.68 us
  transfers between devices with their start and end apart: 28, of which 15 were waited for; matrix products, arithmetic and copies ran while one was open for 0% of the time, Pallas kernels for 11%

profile of v4, /device:TPU:32, one launch (start us, length us, event | category | flops | bytes accessed | tf_op | source)
XLA Modules:
  0.0 193.9 jit_solution(8914495680867769581)
XLA Ops:
  0.8 0.5 collective-permute-start.1
  1.4 1.3 copy-done.5
  2.7 0.7 copy-done.7
  3.4 2.1 %send_x.1 = bf16[128,1920]{1,0:T(8,128)(2,1)} custom-call(s32[6,128]{1,0:T(8,128)S(1)} %bitcast.20, bf16[128,5120]{1,0:T(8,128)(2,1)S(1)} %copy-done.5), custom_call_target="tpu_custom_call" | custom-call | flops 600000000 | bytes 2000000 | tf_op jit(solution)/shard_map/send_x/pallas_call | solution.py:51
  5.4 10.4 %all-to-all-start = ((bf16[16,8,1920]{2,1,0:T(8,128)(2,1)}), bf16[16,8,1920]{2,1,0:T(8,128)(2,1)S(1)}, u32[]{:S(2)}, u32[]{:S(2)}) async-start(bf16[16,8,1920]{2,1,0:T(8,128)(2,1)} %bitcast.1), calls=%async_computation | async-start | bytes 983040 | tf_op jit(solution)/shard_map/all_to_all | solution.py:318
  15.9 2.1 %send_y.1 = bf16[128,2048]{1,0:T(8,128)(2,1)} custom-call(s32[6,128]{1,0:T(8,128)S(1)} %bitcast.21, bf16[6,128]{1,0:T(8,128)(2,1)S(1)} %bitcast.23, bf16[128,5120]{1,0:T(8,128)(2,1)S(1)} %copy-done.6), custom_call_target="tpu_custom_call" | custom-call | flops 600000000 | bytes 2000000 | tf_op jit(solution)/shard_map/send_y/pallas_call | solution.py:51
  18.0 15.5 %all-to-all-done = bf16[16,8,1920]{2,1,0:T(8,128)(2,1)S(1)} async-done(((bf16[16,8,1920]{2,1,0:T(8,128)(2,1)}), bf16[16,8,1920]{2,1,0:T(8,128)(2,1)S(1)}, u32[]{:S(2)}, u32[]{:S(2)}) %all-to-all-start) | async-done | bytes 491552 | tf_op jit(solution)/shard_map/all_to_all | solution.py:318
  34.0 3.4 %collective-permute-start.4 = (bf16[48,5120]{1,0:T(8,128)(2,1)S(1)}, bf16[48,5120]{1,0:T(8,128)(2,1)S(1)}, u32[]{:S(2)}, u32[]{:S(2)}) collective-permute-start(bf16[48,5120]{1,0:T(8,128)(2,1)S(1)} %unpack_x.1.refs_0_), channel_id=1, source_target_pairs={{0,96},{16,48},{32,0},{48,80},{64,32},{80,112},{96,64},{112,16},{1... | collective-permute-start | bytes 1474568 | tf_op jit(solution)/shard_map/ppermute | solution.py:31
  37.4 4.9 %all-to-all-start.1 = ((bf16[16,8,2048]{2,1,0:T(8,128)(2,1)}), bf16[16,8,2048]{2,1,0:T(8,128)(2,1)S(1)}, u32[]{:S(2)}, u32[]{:S(2)}) async-start(bf16[16,8,2048]{2,1,0:T(8,128)(2,1)} %bitcast.7), calls=%async_computation.1 | async-start | bytes 1048576 | tf_op jit(solution)/shard_map/all_to_all | solution.py:318
  42.3 9.3 %collective-permute-done.5.refs_4_ = bf16[48,5120]{1,0:T(8,128)(2,1)S(1)} collective-permute-done((bf16[48,5120]{1,0:T(8,128)(2,1)S(1)}, bf16[48,5120]{1,0:T(8,128)(2,1)S(1)}, u32[]{:S(2)}, u32[]{:S(2)}) %collective-permute-start.5) | collective-permute-done | bytes 491552 | tf_op jit(solution)/shard_map/ppermute | solution.py:31
  51.6 2.1 %collective-permute-start.8 = (bf16[48,5120]{1,0:T(8,128)(2,1)S(1)}, bf16[48,5120]{1,0:T(8,128)(2,1)}, u32[]{:S(2)}, u32[]{:S(2)}) collective-permute-start(bf16[48,5120]{1,0:T(8,128)(2,1)S(1)} %collective-permute-done.5.refs_4_), channel_id=1, source_target_pairs={{0,96},{16,48},{32,0},{48,80},{64,32},{80,112},{96,64},{112,16},{1... | collective-permute-start | bytes 1474568 | tf_op jit(solution)/shard_map/ppermute | solution.py:31
  53.7 2.6 %collective-permute-start.7 = (bf16[48,5120]{1,0:T(8,128)(2,1)S(1)}, bf16[48,5120]{1,0:T(8,128)(2,1)}, u32[]{:S(2)}, u32[]{:S(2)}) collective-permute-start(bf16[48,5120]{1,0:T(8,128)(2,1)S(1)} %collective-permute-done.3.refs_1_), channel_id=1, source_target_pairs={{0,128},{16,144},{32,160},{48,176},{64,192},{80,208},{96,224},{112... | collective-permute-start | bytes 1474568 | tf_op jit(solution)/shard_map/ppermute | solution.py:31
  56.4 3.2 %all-to-all-done.1 = bf16[16,8,2048]{2,1,0:T(8,128)(2,1)S(1)} async-done(((bf16[16,8,2048]{2,1,0:T(8,128)(2,1)}), bf16[16,8,2048]{2,1,0:T(8,128)(2,1)S(1)}, u32[]{:S(2)}, u32[]{:S(2)}) %all-to-all-start.1) | async-done | bytes 524320 | tf_op jit(solution)/shard_map/all_to_all | solution.py:318
  59.6 3.6 %collective-permute-done.8.refs_7_ = bf16[48,5120]{1,0:T(8,128)(2,1)} collective-permute-done((bf16[48,5120]{1,0:T(8,128)(2,1)S(1)}, bf16[48,5120]{1,0:T(8,128)(2,1)}, u32[]{:S(2)}, u32[]{:S(2)}) %collective-permute-start.8) | collective-permute-done | bytes 491552 | tf_op jit(solution)/shard_map/ppermute | solution.py:31
  63.1 5.2 %collective-permute-done.7.refs_5_ = bf16[48,5120]{1,0:T(8,128)(2,1)} collective-permute-done((bf16[48,5120]{1,0:T(8,128)(2,1)S(1)}, bf16[48,5120]{1,0:T(8,128)(2,1)}, u32[]{:S(2)}, u32[]{:S(2)}) %collective-permute-start.7) | collective-permute-done | bytes 491552 | tf_op jit(solution)/shard_map/ppermute | solution.py:31
  68.3 0.3 unpack_y.1.refs_0_
  68.7 0.3 collective-permute-start.11
  69.0 1.9 collective-permute-start.10
  71.0 3.1 %collective-permute-start.12 = (bf16[48,5120]{1,0:T(8,128)(2,1)}, bf16[48,5120]{1,0:T(8,128)(2,1)S(1)}, u32[]{:S(2)}, u32[]{:S(2)}) collective-permute-start(bf16[48,5120]{1,0:T(8,128)(2,1)} %collective-permute-done.8.refs_7_), channel_id=1, source_target_pairs={{0,96},{16,48},{32,0},{48,80},{64,32},{80,112},{96,64},{112,16},{1... | collective-permute-start | bytes 1474568 | tf_op jit(solution)/shard_map/ppermute | solution.py:31
  74.1 13.2 %collective-permute-done.12.refs_6_ = bf16[48,5120]{1,0:T(8,128)(2,1)S(1)} collective-permute-done((bf16[48,5120]{1,0:T(8,128)(2,1)}, bf16[48,5120]{1,0:T(8,128)(2,1)S(1)}, u32[]{:S(2)}, u32[]{:S(2)}) %collective-permute-start.12) | collective-permute-done | bytes 491552 | tf_op jit(solution)/shard_map/ppermute | solution.py:31
  87.3 3.0 %collective-permute-start.15 = (bf16[48,5248]{1,0:T(8,128)(2,1)S(1)}, bf16[48,5248]{1,0:T(8,128)(2,1)S(1)}, u32[]{:S(2)}, u32[]{:S(2)}) collective-permute-start(bf16[48,5248]{1,0:T(8,128)(2,1)S(1)} %collective-permute-done.11.refs_4_), channel_id=1, source_target_pairs={{0,96},{16,48},{32,0},{48,80},{64,32},{80,112},{96,64},{112,16},{1... | collective-permute-start | bytes 1511432 | tf_op jit(solution)/shard_map/ppermute | solution.py:31
  90.4 1.7 collective-permute-start.14
  92.0 10.0 %collective-permute-done.15.refs_7_ = bf16[48,5248]{1,0:T(8,128)(2,1)S(1)} collective-permute-done((bf16[48,5248]{1,0:T(8,128)(2,1)S(1)}, bf16[48,5248]{1,0:T(8,128)(2,1)S(1)}, u32[]{:S(2)}, u32[]{:S(2)}) %collective-permute-start.15) | collective-permute-done | bytes 503840 | tf_op jit(solution)/shard_map/ppermute | solution.py:31
  102.0 3.7 %collective-permute-start.16 = (bf16[48,5248]{1,0:T(8,128)(2,1)S(1)}, bf16[48,5248]{1,0:T(8,128)(2,1)S(1)}, u32[]{:S(2)}, u32[]{:S(2)}) collective-permute-start(bf16[48,5248]{1,0:T(8,128)(2,1)S(1)} %collective-permute-done.15.refs_7_), channel_id=1, source_target_pairs={{0,96},{16,48},{32,0},{48,80},{64,32},{80,112},{96,64},{112,16},{1... | collective-permute-start | bytes 1511432 | tf_op jit(solution)/shard_map/ppermute | solution.py:31
  105.7 6.5 %pre.1 = (f32[192,384]{1,0:T(8,128)S(1)}, f32[192,384]{1,0:T(8,128)S(1)}, bf16[384,5120]{1,0:T(8,128)(2,1)}) custom-call(bf16[48,5120]{1,0:T(8,128)(2,1)S(1)} %unpack_x.1.refs_0_, bf16[48,5120]{1,0:T(8,128)(2,1)S(1)} %collective-permute-done.3.refs_1_, bf16[48,5120]{1,0:T(8,128)(2,1)} %collective-permute-done.6.refs_2_, ...), custom_call_target="tpu_custom_call" | custom-call | flops 1509949440 | bytes 10000000 | tf_op jit(solution)/shard_map/pre/pallas_call | solution.py:51
  112.4 0.9 copy-done.15
  113.4 9.3 %main.1 = (bf16[48,5248]{1,0:T(8,128)(2,1)S(1)}, bf16[48,5248]{1,0:T(8,128)(2,1)S(1)}, bf16[48,5248]{1,0:T(8,128)(2,1)S(1)}, bf16[48,5248]{1,0:T(8,128)(2,1)S(1)...) custom-call(bf16[48,5248]{1,0:T(8,128)(2,1)S(1)} %unpack_y.1.refs_0_, ...), custom_call_target="tpu_custom_call" | custom-call | flops 2264924160 | bytes 14000000 | tf_op jit(solution)/shard_map/main/pallas_call | solution.py:51
  122.7 0.9 collective-permute-start.17
  123.6 3.3 %collective-permute-start.18 = (bf16[48,5248]{1,0:T(8,128)(2,1)S(1)}, bf16[48,5248]{1,0:T(8,128)(2,1)S(1)}, u32[]{:S(2)}, u32[]{:S(2)}) collective-permute-start(bf16[48,5248]{1,0:T(8,128)(2,1)S(1)} %get-tuple-element.78), channel_id=1, source_target_pairs={{0,96},{16,48},{32,0},{48,80},{64,32},{80,112},{96,64},{112,16},{1... | collective-permute-start | bytes 1511432 | tf_op jit(solution)/shard_map/ppermute | solution.py:31
  126.9 2.1 %copy-done = bf16[384,5248]{1,0:T(8,128)(2,1)S(1)} copy-done((bf16[384,5248]{1,0:T(8,128)(2,1)S(1)}, bf16[384,5248]{1,0:T(8,128)(2,1)}, u32[]{:S(2)}) %copy-start) | copy-done | bytes 4030488
  129.1 3.3 %wgrad_away.1 = bf16[288,5120]{1,0:T(8,128)(2,1)S(1)} custom-call(bf16[192,384]{1,0:T(8,128)(2,1)S(1)} %get-tuple-element.96.hid_ref, bf16[192,384]{1,0:T(8,128)(2,1)S(1)} %get-tuple-element.82.dg_ref, bf16[192,384]{1,0:T(8,128)(2,1)S(1)} %get-tuple-element.83.du_ref, bf16[384,5248]{1,0:T(8,128)(2,1)S(1)} %copy-done, bf16[384,5248]{1,0:T(8,128)(2,1)S(1)} %copy-done, ...), custom_call_target="tpu_custom_call" | custom-call | flops 1132462080 | bytes 12000000 | tf_op jit(solution)/shard_map/wgrad_away/pallas_call | solution.py:396
  132.3 0.3 collective-permute-done.17.refs_1_
  132.7 1.9 collective-permute-done.18.refs_1_
  134.6 6.8 %collective-permute-done.19.refs_2_ = bf16[48,5248]{1,0:T(8,128)(2,1)S(1)} collective-permute-done((bf16[48,5248]{1,0:T(8,128)(2,1)S(1)}, bf16[48,5248]{1,0:T(8,128)(2,1)S(1)}, u32[]{:S(2)}, u32[]{:S(2)}) %collective-permute-start.19) | collective-permute-done | bytes 503840 | tf_op jit(solution)/shard_map/ppermute | solution.py:31
  141.4 0.5 join.4
  141.8 1.2 collective-permute-start.21
  143.3 2.0 %collective-permute-start.22 = (bf16[48,5248]{1,0:T(8,128)(2,1)S(1)}, bf16[48,5248]{1,0:T(8,128)(2,1)S(1)}, u32[]{:S(2)}, u32[]{:S(2)}) collective-permute-start(bf16[48,5248]{1,0:T(8,128)(2,1)S(1)} %get-tuple-element.90), channel_id=1, source_target_pairs={{0,32},{16,112},{32,64},{48,16},{64,96},{80,48},{96,0},{112,80},{1... | collective-permute-start | bytes 1511432 | tf_op jit(solution)/shard_map/ppermute | solution.py:31
  145.4 5.5 %collective-permute-done.21.refs_3_ = bf16[48,5248]{1,0:T(8,128)(2,1)S(1)} collective-permute-done((bf16[48,5248]{1,0:T(8,128)(2,1)S(1)}, bf16[48,5248]{1,0:T(8,128)(2,1)S(1)}, u32[]{:S(2)}, u32[]{:S(2)}) %collective-permute-start.21) | collective-permute-done | bytes 503840 | tf_op jit(solution)/shard_map/ppermute | solution.py:31
  150.9 1.4 collective-permute-done.20.refs_1_
  152.3 1.3 collective-permute-done.22.refs_2_
  154.0 8.9 %collective-permute-done.23.refs_1_ = bf16[48,5248]{1,0:T(8,128)(2,1)S(1)} collective-permute-done((bf16[48,5248]{1,0:T(8,128)(2,1)S(1)}, bf16[48,5248]{1,0:T(8,128)(2,1)S(1)}, u32[]{:S(2)}, u32[]{:S(2)}) %collective-permute-start.23) | collective-permute-done | bytes 503840 | tf_op jit(solution)/shard_map/ppermute | solution.py:31
  162.9 1.3 last.1
  164.2 7.2 %all-to-all-start.2 = ((bf16[16,8,2048]{2,1,0:T(8,128)(2,1)}), bf16[16,8,2048]{2,1,0:T(8,128)(2,1)}, u32[]{:S(2)}, u32[]{:S(2)}) async-start(bf16[16,8,2048]{2,1,0:T(8,128)(2,1)} %bitcast.9), calls=%async_computation.2 | async-start | bytes 1048576 | tf_op jit(solution)/shard_map/all_to_all | solution.py:318
  171.4 2.1 %copy-done.1 = bf16[384,5248]{1,0:T(8,128)(2,1)S(1)} copy-done((bf16[384,5248]{1,0:T(8,128)(2,1)S(1)}, bf16[384,5248]{1,0:T(8,128)(2,1)}, u32[]{:S(2)}) %copy-start.1) | copy-done | bytes 4030488
  173.5 2.1 %copy-done.3 = bf16[384,5120]{1,0:T(8,128)(2,1)S(1)} copy-done((bf16[384,5120]{1,0:T(8,128)(2,1)S(1)}, bf16[384,5120]{1,0:T(8,128)(2,1)}, u32[]{:S(2)}) %copy-start.3) | copy-done | bytes 3932184
  175.6 5.4 %wgrad_mine.1 = (bf16[96,5120]{1,0:T(8,128)(2,1)}, bf16[96,5120]{1,0:T(8,128)(2,1)}, bf16[96,5120]{1,0:T(8,128)(2,1)}) custom-call(bf16[192,384]{1,0:T(8,128)(2,1)S(1)} %get-tuple-element.96.hid_ref, bf16[192,384]{1,0:T(8,128)(2,1)S(1)} %get-tuple-element.82.dg_ref, bf16[192,384]{1,0:T(8,128)(2,1)S(1)} %get-tuple-element.83.du_ref, ...), custom_call_target="tpu_custom_call" | custom-call | flops 1132462080 | bytes 12000000 | tf_op jit(solution)/shard_map/wgrad_mine/pallas_call | solution.py:396
  181.1 9.4 %all-to-all-done.2 = bf16[16,8,2048]{2,1,0:T(8,128)(2,1)} async-done(((bf16[16,8,2048]{2,1,0:T(8,128)(2,1)}), bf16[16,8,2048]{2,1,0:T(8,128)(2,1)}, u32[]{:S(2)}, u32[]{:S(2)}) %all-to-all-start.2) | async-done | bytes 524320 | tf_op jit(solution)/shard_map/all_to_all | solution.py:318
  190.4 3.5 %final.1 = (bf16[128,5120]{1,0:T(8,128)(2,1)}, bf16[6,128]{1,0:T(8,128)(2,1)}) custom-call(s32[6,128]{1,0:T(8,128)S(1)} %bitcast.22, bf16[128,2048]{1,0:T(8,128)(2,1)} %bitcast.10.in_ref), custom_call_target="tpu_custom_call" | custom-call | flops 600000000 | bytes 2000000 | tf_op jit(solution)/shard_map/final/pallas_call | solution.py:51
  (53 shorter events, 1.7 us)
Async XLA Ops:
  0.6 15.3 %copy-start.8 = (s32[128,6]{0,1:T(8,128)S(1)}, s32[128,6]{0,1:T(8,128)}, u32[]{:S(2)}) copy-start(s32[128,6]{0,1:T(8,128)} %param.10) | copy-start | bytes 9220
  0.6 15.3 %copy-start.9 = (bf16[128,6]{0,1:T(8,128)(2,1)S(1)}, bf16[128,6]{0,1:T(8,128)(2,1)}, u32[]{:S(2)}) copy-start(bf16[128,6]{0,1:T(8,128)(2,1)} %param.9) | copy-start | bytes 4612
  0.7 32.9 %collective-permute-start = (bf16[96,5120]{1,0:T(8,128)(2,1)}, bf16[96,5120]{1,0:T(8,128)(2,1)}, u32[]{:S(2)}, u32[]{:S(2)}) collective-permute-start(bf16[96,5120]{1,0:T(8,128)(2,1)} %bitcast.15), channel_id=1, source_target_pairs={{0,16},{16,0},{32,48},{48,32},{64,80},{80,64},{96,112},{112,96},{1... | collective-permute-start | bytes 2949128 | tf_op jit(solution)/shard_map/ppermute | solution.py:31
  0.8 32.8 %collective-permute-start.1 = (bf16[96,5120]{1,0:T(8,128)(2,1)}, bf16[96,5120]{1,0:T(8,128)(2,1)}, u32[]{:S(2)}, u32[]{:S(2)}) collective-permute-start(bf16[96,5120]{1,0:T(8,128)(2,1)} %bitcast.24), channel_id=1, source_target_pairs={{0,16},{16,0},{32,48},{48,32},{64,80},{80,64},{96,112},{112,96},{1... | collective-permute-start | bytes 2949128 | tf_op jit(solution)/shard_map/ppermute | solution.py:31
  1.2 32.3 %collective-permute-start.2 = (bf16[96,5120]{1,0:T(8,128)(2,1)}, bf16[96,5120]{1,0:T(8,128)(2,1)}, u32[]{:S(2)}, u32[]{:S(2)}) collective-permute-start(bf16[96,5120]{1,0:T(8,128)(2,1)} %bitcast.27), channel_id=1, source_target_pairs={{0,16},{16,0},{32,48},{48,32},{64,80},{80,64},{96,112},{112,96},{1... | collective-permute-start | bytes 2949128 | tf_op jit(solution)/shard_map/ppermute | solution.py:31
  1.4 1.3 copy-start.5
  2.7 0.7 copy-start.7
  3.4 12.6 %copy-start.6 = (bf16[128,5120]{1,0:T(8,128)(2,1)S(1)}, bf16[128,5120]{1,0:T(8,128)(2,1)}, u32[]{:S(2)}) copy-start(bf16[128,5120]{1,0:T(8,128)(2,1)} %refs_2_.1) | copy-start | bytes 3932164
  5.4 100.3 %copy-start.4 = (bf16[1,96,5120]{2,1,0:T(8,128)(2,1)S(1)}, bf16[1,96,5120]{2,1,0:T(8,128)(2,1)}, u32[]{:S(2)}) copy-start(bf16[1,96,5120]{2,1,0:T(8,128)(2,1)} %param.11) | copy-start | bytes 2949124
  5.4 28.1 %all-to-all-start = ((bf16[16,8,1920]{2,1,0:T(8,128)(2,1)}), bf16[16,8,1920]{2,1,0:T(8,128)(2,1)S(1)}, u32[]{:S(2)}, u32[]{:S(2)}) async-start(bf16[16,8,1920]{2,1,0:T(8,128)(2,1)} %bitcast.1), calls=%async_computation | async-start | bytes 983040 | tf_op jit(solution)/shard_map/all_to_all | solution.py:318
  33.9 17.8 %collective-permute-start.5 = (bf16[48,5120]{1,0:T(8,128)(2,1)S(1)}, bf16[48,5120]{1,0:T(8,128)(2,1)S(1)}, u32[]{:S(2)}, u32[]{:S(2)}) collective-permute-start(bf16[48,5120]{1,0:T(8,128)(2,1)S(1)} %unpack_x.1.refs_0_), channel_id=1, source_target_pairs={{0,128},{16,144},{32,160},{48,176},{64,192},{80,208},{96,224},{112... | collective-permute-start | bytes 1474568 | tf_op jit(solution)/shard_map/ppermute | solution.py:31
  34.0 17.7 %collective-permute-start.4 = (bf16[48,5120]{1,0:T(8,128)(2,1)S(1)}, bf16[48,5120]{1,0:T(8,128)(2,1)S(1)}, u32[]{:S(2)}, u32[]{:S(2)}) collective-permute-start(bf16[48,5120]{1,0:T(8,128)(2,1)S(1)} %unpack_x.1.refs_0_), channel_id=1, source_target_pairs={{0,96},{16,48},{32,0},{48,80},{64,32},{80,112},{96,64},{112,16},{1... | collective-permute-start | bytes 1474568 | tf_op jit(solution)/shard_map/ppermute | solution.py:31
  37.4 14.3 %collective-permute-start.3 = (bf16[48,5120]{1,0:T(8,128)(2,1)S(1)}, bf16[48,5120]{1,0:T(8,128)(2,1)S(1)}, u32[]{:S(2)}, u32[]{:S(2)}) collective-permute-start(bf16[48,5120]{1,0:T(8,128)(2,1)S(1)} %unpack_x.1.refs_0_), channel_id=1, source_target_pairs={{0,32},{16,112},{32,64},{48,16},{64,96},{80,48},{96,0},{112,80},{1... | collective-permute-start | bytes 1474568 | tf_op jit(solution)/shard_map/ppermute | solution.py:31
  37.4 22.2 %all-to-all-start.1 = ((bf16[16,8,2048]{2,1,0:T(8,128)(2,1)}), bf16[16,8,2048]{2,1,0:T(8,128)(2,1)S(1)}, u32[]{:S(2)}, u32[]{:S(2)}) async-start(bf16[16,8,2048]{2,1,0:T(8,128)(2,1)} %bitcast.7), calls=%async_computation.1 | async-start | bytes 1048576 | tf_op jit(solution)/shard_map/all_to_all | solution.py:318
  51.6 11.5 %collective-permute-start.8 = (bf16[48,5120]{1,0:T(8,128)(2,1)S(1)}, bf16[48,5120]{1,0:T(8,128)(2,1)}, u32[]{:S(2)}, u32[]{:S(2)}) collective-permute-start(bf16[48,5120]{1,0:T(8,128)(2,1)S(1)} %collective-permute-done.5.refs_4_), channel_id=1, source_target_pairs={{0,96},{16,48},{32,0},{48,80},{64,32},{80,112},{96,64},{112,16},{1... | collective-permute-start | bytes 1474568 | tf_op jit(solution)/shard_map/ppermute | solution.py:31
  53.7 14.6 %collective-permute-start.7 = (bf16[48,5120]{1,0:T(8,128)(2,1)S(1)}, bf16[48,5120]{1,0:T(8,128)(2,1)}, u32[]{:S(2)}, u32[]{:S(2)}) collective-permute-start(bf16[48,5120]{1,0:T(8,128)(2,1)S(1)} %collective-permute-done.3.refs_1_), channel_id=1, source_target_pairs={{0,128},{16,144},{32,160},{48,176},{64,192},{80,208},{96,224},{112... | collective-permute-start | bytes 1474568 | tf_op jit(solution)/shard_map/ppermute | solution.py:31
  56.4 12.0 %collective-permute-start.6 = (bf16[48,5120]{1,0:T(8,128)(2,1)S(1)}, bf16[48,5120]{1,0:T(8,128)(2,1)}, u32[]{:S(2)}, u32[]{:S(2)}) collective-permute-start(bf16[48,5120]{1,0:T(8,128)(2,1)S(1)} %collective-permute-done.3.refs_1_), channel_id=1, source_target_pairs={{0,32},{16,112},{32,64},{48,16},{64,96},{80,48},{96,0},{112,80},{1... | collective-permute-start | bytes 1474568 | tf_op jit(solution)/shard_map/ppermute | solution.py:31
  68.7 18.6 %collective-permute-start.11 = (bf16[48,5248]{1,0:T(8,128)(2,1)S(1)}, bf16[48,5248]{1,0:T(8,128)(2,1)S(1)}, u32[]{:S(2)}, u32[]{:S(2)}) collective-permute-start(bf16[48,5248]{1,0:T(8,128)(2,1)S(1)} %unpack_y.1.refs_0_), channel_id=1, source_target_pairs={{0,128},{16,144},{32,160},{48,176},{64,192},{80,208},{96,224},{112... | collective-permute-start | bytes 1511432 | tf_op jit(solution)/shard_map/ppermute | solution.py:31
  69.0 18.3 %collective-permute-start.10 = (bf16[48,5248]{1,0:T(8,128)(2,1)S(1)}, bf16[48,5248]{1,0:T(8,128)(2,1)S(1)}, u32[]{:S(2)}, u32[]{:S(2)}) collective-permute-start(bf16[48,5248]{1,0:T(8,128)(2,1)S(1)} %unpack_y.1.refs_0_), channel_id=1, source_target_pairs={{0,96},{16,48},{32,0},{48,80},{64,32},{80,112},{96,64},{112,16},{1... | collective-permute-start | bytes 1511432 | tf_op jit(solution)/shard_map/ppermute | solution.py:31
  70.9 16.5 %collective-permute-start.9 = (bf16[48,5248]{1,0:T(8,128)(2,1)S(1)}, bf16[48,5248]{1,0:T(8,128)(2,1)S(1)}, u32[]{:S(2)}, u32[]{:S(2)}) collective-permute-start(bf16[48,5248]{1,0:T(8,128)(2,1)S(1)} %unpack_y.1.refs_0_), channel_id=1, source_target_pairs={{0,32},{16,112},{32,64},{48,16},{64,96},{80,48},{96,0},{112,80},{1... | collective-permute-start | bytes 1511432 | tf_op jit(solution)/shard_map/ppermute | solution.py:31
  71.0 16.3 %collective-permute-start.12 = (bf16[48,5120]{1,0:T(8,128)(2,1)}, bf16[48,5120]{1,0:T(8,128)(2,1)S(1)}, u32[]{:S(2)}, u32[]{:S(2)}) collective-permute-start(bf16[48,5120]{1,0:T(8,128)(2,1)} %collective-permute-done.8.refs_7_), channel_id=1, source_target_pairs={{0,96},{16,48},{32,0},{48,80},{64,32},{80,112},{96,64},{112,16},{1... | collective-permute-start | bytes 1474568 | tf_op jit(solution)/shard_map/ppermute | solution.py:31
  87.3 24.9 %copy-start.10 = (bf16[48,5248]{1,0:T(8,128)(2,1)}, bf16[48,5248]{1,0:T(8,128)(2,1)S(1)}, u32[]{:S(2)}) copy-start(bf16[48,5248]{1,0:T(8,128)(2,1)S(1)} %collective-permute-done.11.refs_4_) | copy-start | bytes 1511428
  87.3 24.9 %copy-start.11 = (bf16[48,5248]{1,0:T(8,128)(2,1)}, bf16[48,5248]{1,0:T(8,128)(2,1)S(1)}, u32[]{:S(2)}) copy-start(bf16[48,5248]{1,0:T(8,128)(2,1)S(1)} %collective-permute-done.10.refs_3_) | copy-start | bytes 1511428
  87.3 14.7 %collective-permute-start.15 = (bf16[48,5248]{1,0:T(8,128)(2,1)S(1)}, bf16[48,5248]{1,0:T(8,128)(2,1)S(1)}, u32[]{:S(2)}, u32[]{:S(2)}) collective-permute-start(bf16[48,5248]{1,0:T(8,128)(2,1)S(1)} %collective-permute-done.11.refs_4_), channel_id=1, source_target_pairs={{0,96},{16,48},{32,0},{48,80},{64,32},{80,112},{96,64},{112,16},{1... | collective-permute-start | bytes 1511432 | tf_op jit(solution)/shard_map/ppermute | solution.py:31
  90.4 21.9 %collective-permute-start.14 = (bf16[48,5248]{1,0:T(8,128)(2,1)S(1)}, bf16[48,5248]{1,0:T(8,128)(2,1)S(1)}, u32[]{:S(2)}, u32[]{:S(2)}) collective-permute-start(bf16[48,5248]{1,0:T(8,128)(2,1)S(1)} %collective-permute-done.9.refs_1_), channel_id=1, source_target_pairs={{0,128},{16,144},{32,160},{48,176},{64,192},{80,208},{96,224},{112... | collective-permute-start | bytes 1511432 | tf_op jit(solution)/shard_map/ppermute | solution.py:31
  92.0 20.3 %collective-permute-start.13 = (bf16[48,5248]{1,0:T(8,128)(2,1)S(1)}, bf16[48,5248]{1,0:T(8,128)(2,1)S(1)}, u32[]{:S(2)}, u32[]{:S(2)}) collective-permute-start(bf16[48,5248]{1,0:T(8,128)(2,1)S(1)} %collective-permute-done.9.refs_1_), channel_id=1, source_target_pairs={{0,32},{16,112},{32,64},{48,16},{64,96},{80,48},{96,0},{112,80},{1... | collective-permute-start | bytes 1511432 | tf_op jit(solution)/shard_map/ppermute | solution.py:31
  102.0 10.3 %copy-start.12 = (bf16[48,5248]{1,0:T(8,128)(2,1)}, bf16[48,5248]{1,0:T(8,128)(2,1)S(1)}, u32[]{:S(2)}) copy-start(bf16[48,5248]{1,0:T(8,128)(2,1)S(1)} %collective-permute-done.15.refs_7_) | copy-start | bytes 1511428
  102.0 10.3 %collective-permute-start.16 = (bf16[48,5248]{1,0:T(8,128)(2,1)S(1)}, bf16[48,5248]{1,0:T(8,128)(2,1)S(1)}, u32[]{:S(2)}, u32[]{:S(2)}) collective-permute-start(bf16[48,5248]{1,0:T(8,128)(2,1)S(1)} %collective-permute-done.15.refs_7_), channel_id=1, source_target_pairs={{0,96},{16,48},{32,0},{48,80},{64,32},{80,112},{96,64},{112,16},{1... | collective-permute-start | bytes 1511432 | tf_op jit(solution)/shard_map/ppermute | solution.py:31
  112.3 0.9 copy-start.13
  112.3 1.1 copy-start.14
  112.3 0.9 copy-start.15
  113.4 13.5 %copy-start.2 = (bf16[384,5120]{1,0:T(8,128)(2,1)S(1)}, bf16[384,5120]{1,0:T(8,128)(2,1)}, u32[]{:S(2)}) copy-start(bf16[384,5120]{1,0:T(8,128)(2,1)} %get-tuple-element.85.x_ref) | copy-start | bytes 11796484
  122.7 9.9 %collective-permute-start.17 = (bf16[48,5248]{1,0:T(8,128)(2,1)S(1)}, bf16[48,5248]{1,0:T(8,128)(2,1)S(1)}, u32[]{:S(2)}, u32[]{:S(2)}) collective-permute-start(bf16[48,5248]{1,0:T(8,128)(2,1)S(1)} %get-tuple-element.77), channel_id=1, source_target_pairs={{0,128},{16,144},{32,160},{48,176},{64,192},{80,208},{96,224},{112... | collective-permute-start | bytes 1511432 | tf_op jit(solution)/shard_map/ppermute | solution.py:31
  123.6 10.9 %collective-permute-start.18 = (bf16[48,5248]{1,0:T(8,128)(2,1)S(1)}, bf16[48,5248]{1,0:T(8,128)(2,1)S(1)}, u32[]{:S(2)}, u32[]{:S(2)}) collective-permute-start(bf16[48,5248]{1,0:T(8,128)(2,1)S(1)} %get-tuple-element.78), channel_id=1, source_target_pairs={{0,96},{16,48},{32,0},{48,80},{64,32},{80,112},{96,64},{112,16},{1... | collective-permute-start | bytes 1511432 | tf_op jit(solution)/shard_map/ppermute | solution.py:31
  126.9 14.4 %collective-permute-start.19 = (bf16[48,5248]{1,0:T(8,128)(2,1)S(1)}, bf16[48,5248]{1,0:T(8,128)(2,1)S(1)}, u32[]{:S(2)}, u32[]{:S(2)}) collective-permute-start(bf16[48,5248]{1,0:T(8,128)(2,1)S(1)} %get-tuple-element.79), channel_id=1, source_target_pairs={{0,32},{16,112},{32,64},{48,16},{64,96},{80,48},{96,0},{112,80},{1... | collective-permute-start | bytes 1511432 | tf_op jit(solution)/shard_map/ppermute | solution.py:31
  126.9 2.1 %copy-start = (bf16[384,5248]{1,0:T(8,128)(2,1)S(1)}, bf16[384,5248]{1,0:T(8,128)(2,1)}, u32[]{:S(2)}) copy-start(bf16[384,5248]{1,0:T(8,128)(2,1)} %get-tuple-element.84.y_ref.prob_ref) | copy-start | bytes 12091396
  141.8 9.0 %collective-permute-start.21 = (bf16[48,5248]{1,0:T(8,128)(2,1)S(1)}, bf16[48,5248]{1,0:T(8,128)(2,1)S(1)}, u32[]{:S(2)}, u32[]{:S(2)}) collective-permute-start(bf16[48,5248]{1,0:T(8,128)(2,1)S(1)} %join.4), channel_id=1, source_target_pairs={{0,128},{16,144},{32,160},{48,176},{64,192},{80,208},{96,224},{112... | collective-permute-start | bytes 1511432 | tf_op jit(solution)/shard_map/ppermute | solution.py:31
  143.3 9.0 %collective-permute-start.20 = (bf16[48,5248]{1,0:T(8,128)(2,1)S(1)}, bf16[48,5248]{1,0:T(8,128)(2,1)S(1)}, u32[]{:S(2)}, u32[]{:S(2)}) collective-permute-start(bf16[48,5248]{1,0:T(8,128)(2,1)S(1)} %join.3), channel_id=1, source_target_pairs={{0,96},{16,48},{32,0},{48,80},{64,32},{80,112},{96,64},{112,16},{1... | collective-permute-start | bytes 1511432 | tf_op jit(solution)/shard_map/ppermute | solution.py:31
  143.3 10.2 %collective-permute-start.22 = (bf16[48,5248]{1,0:T(8,128)(2,1)S(1)}, bf16[48,5248]{1,0:T(8,128)(2,1)S(1)}, u32[]{:S(2)}, u32[]{:S(2)}) collective-permute-start(bf16[48,5248]{1,0:T(8,128)(2,1)S(1)} %get-tuple-element.90), channel_id=1, source_target_pairs={{0,32},{16,112},{32,64},{48,16},{64,96},{80,48},{96,0},{112,80},{1... | collective-permute-start | bytes 1511432 | tf_op jit(solution)/shard_map/ppermute | solution.py:31
  153.6 17.8 %collective-permute-start.24 = (bf16[288,5120]{1,0:T(8,128)(2,1)S(1)}, bf16[288,5120]{1,0:T(8,128)(2,1)}, u32[]{:S(2)}, u32[]{:S(2)}) collective-permute-start(bf16[288,5120]{1,0:T(8,128)(2,1)S(1)} %wgrad_away.1), channel_id=1, source_target_pairs={{0,16},{16,0},{32,48},{48,32},{64,80},{80,64},{96,112},{112,96},{1... | collective-permute-start | bytes 8847368 | tf_op jit(solution)/shard_map/ppermute | solution.py:31
  153.9 9.0 %collective-permute-start.23 = (bf16[48,5248]{1,0:T(8,128)(2,1)S(1)}, bf16[48,5248]{1,0:T(8,128)(2,1)S(1)}, u32[]{:S(2)}, u32[]{:S(2)}) collective-permute-start(bf16[48,5248]{1,0:T(8,128)(2,1)S(1)} %join.5), channel_id=1, source_target_pairs={{0,96},{16,48},{32,0},{48,80},{64,32},{80,112},{96,64},{112,16},{1... | collective-permute-start | bytes 1511432 | tf_op jit(solution)/shard_map/ppermute | solution.py:31
  164.2 26.3 %all-to-all-start.2 = ((bf16[16,8,2048]{2,1,0:T(8,128)(2,1)}), bf16[16,8,2048]{2,1,0:T(8,128)(2,1)}, u32[]{:S(2)}, u32[]{:S(2)}) async-start(bf16[16,8,2048]{2,1,0:T(8,128)(2,1)} %bitcast.9), calls=%async_computation.2 | async-start | bytes 1048576 | tf_op jit(solution)/shard_map/all_to_all | solution.py:318
  171.4 2.1 %copy-start.1 = (bf16[384,5248]{1,0:T(8,128)(2,1)S(1)}, bf16[384,5248]{1,0:T(8,128)(2,1)}, u32[]{:S(2)}) copy-start(bf16[384,5248]{1,0:T(8,128)(2,1)} %get-tuple-element.84.y_ref.prob_ref) | copy-start | bytes 12091396
  173.5 2.1 %copy-start.3 = (bf16[384,5120]{1,0:T(8,128)(2,1)S(1)}, bf16[384,5120]{1,0:T(8,128)(2,1)}, u32[]{:S(2)}) copy-start(bf16[384,5120]{1,0:T(8,128)(2,1)} %get-tuple-element.85.x_ref) | copy-start | bytes 11796484

commit v5 on v4

--- a/solution.py
+++ b/solution.py
@@ -345,12 +345,12 @@
     send_y, x_now = together((send_y, x))
     got_y = exchange(send_y)
     xa, xb, oth = together((xa, xb, oth))
-    ob, oa, far = hop(oth, X_B), hop(xa, Z_SWAP), hop(xa, X_A)
+    ob, oa, far = hop(oth, X_B), hop(oth, X_A), hop(xa, X_A)
     o_far = hop(ob, X_B)
     far, oa, ob, got_y = together((far, oa, ob, got_y))
     y = unpack(got_y, wide, "unpack_y")
     ya, yb, y_oth = hop(y, X_A), hop(y, X_B), hop(y, Z_SWAP)
-    ya, yb, y_oth, o_far = together((ya, yb, y_oth, o_far))
+    ya, yb, y_oth = together((ya, yb, y_oth))
     yob, yoa, y_far = hop(y_oth, X_B), hop(ya, Z_SWAP), hop(ya, X_A)
     yo_far = hop(yob, X_B)
     gate, up, x_all = call(

time: 195 us -> 188 us (0.964)
  waiting for transfers between devices: 95.6 us -> 88.9 us
    ppermute x25, waiting for transfers between devices: 67.6 us -> 60.4 us  [hop(): return lax.ppermute(a, 'edp', perm)]
  transfers between devices with their start and end apart: 28 -> 28, of which waited for: 15 -> 18; matrix products, arithmetic and copies ran while one was open for 0% -> 0% of each run, Pallas kernels for 11% -> 11%
where the time goes in v5:
time: 188 us; the launch traced here: 187 us
  waiting for transfers between devices  88.9 us (47%)
  starting transfers between devices  52.4 us (28%)
  Pallas kernels  35.1 us (19%)
  local copies, waits for them, and re-layouts  9.49 us (5%)
    ppermute x25, waiting for transfers between devices, hop(): return lax.ppermute(a, 'edp', perm)  60.4 us
    all_to_all x3, waiting for transfers between devices, exchange(): a = lax.all_to_all(a, 'ep', split_axis=0, concat_axis=0, tiled=True)  28.6 us
    ppermute x25, starting transfers between devices, hop(): return lax.ppermute(a, 'edp', perm)  28.4 us
    pallas_call x11, Pallas kernels, run(): pl.pallas_call(kernel, out_shape=outs, in_specs=[one] * len(args) if spec...  26.5 us
    all_to_all x3, starting transfers between devices, exchange(): a = lax.all_to_all(a, 'ep', split_axis=0, concat_axis=0, tiled=True)  24 us
    unnamed x32, local copies, waits for them, and re-layouts  9.49 us
    pallas_call x2, Pallas kernels, wgrad(): pl.pallas_call(functools.partial(wgrad_kernel, away=not came), out_shape=...  8.68 us
  transfers between devices with their start and end apart: 28, of which 18 were waited for; matrix products, arithmetic and copies ran while one was open for 0% of the time, Pallas kernels for 11%

profile of v5, /device:TPU:32, one launch (start us, length us, event | category | flops | bytes accessed | tf_op | source)
XLA Modules:
  0.0 186.9 jit_solution(5862878424444325117)
XLA Ops:
  0.8 0.5 collective-permute-start.1
  1.4 1.3 copy-done.5
  2.7 0.7 copy-done.7
  3.4 2.1 %send_x.1 = bf16[128,1920]{1,0:T(8,128)(2,1)} custom-call(s32[6,128]{1,0:T(8,128)S(1)} %bitcast.20, bf16[128,5120]{1,0:T(8,128)(2,1)S(1)} %copy-done.5), custom_call_target="tpu_custom_call" | custom-call | flops 600000000 | bytes 2000000 | tf_op jit(solution)/shard_map/send_x/pallas_call | solution.py:51
  5.4 10.4 %all-to-all-start = ((bf16[16,8,1920]{2,1,0:T(8,128)(2,1)}), bf16[16,8,1920]{2,1,0:T(8,128)(2,1)S(1)}, u32[]{:S(2)}, u32[]{:S(2)}) async-start(bf16[16,8,1920]{2,1,0:T(8,128)(2,1)} %bitcast.1), calls=%async_computation | async-start | bytes 983040 | tf_op jit(solution)/shard_map/all_to_all | solution.py:318
  15.9 2.1 %send_y.1 = bf16[128,2048]{1,0:T(8,128)(2,1)} custom-call(s32[6,128]{1,0:T(8,128)S(1)} %bitcast.21, bf16[6,128]{1,0:T(8,128)(2,1)S(1)} %bitcast.23, bf16[128,5120]{1,0:T(8,128)(2,1)S(1)} %copy-done.6), custom_call_target="tpu_custom_call" | custom-call | flops 600000000 | bytes 2000000 | tf_op jit(solution)/shard_map/send_y/pallas_call | solution.py:51
  18.0 15.5 %all-to-all-done = bf16[16,8,1920]{2,1,0:T(8,128)(2,1)S(1)} async-done(((bf16[16,8,1920]{2,1,0:T(8,128)(2,1)}), bf16[16,8,1920]{2,1,0:T(8,128)(2,1)S(1)}, u32[]{:S(2)}, u32[]{:S(2)}) %all-to-all-start) | async-done | bytes 491552 | tf_op jit(solution)/shard_map/all_to_all | solution.py:318
  34.0 3.4 %collective-permute-start.4 = (bf16[48,5120]{1,0:T(8,128)(2,1)S(1)}, bf16[48,5120]{1,0:T(8,128)(2,1)S(1)}, u32[]{:S(2)}, u32[]{:S(2)}) collective-permute-start(bf16[48,5120]{1,0:T(8,128)(2,1)S(1)} %unpack_x.1.refs_0_), channel_id=1, source_target_pairs={{0,96},{16,48},{32,0},{48,80},{64,32},{80,112},{96,64},{112,16},{1... | collective-permute-start | bytes 1474568 | tf_op jit(solution)/shard_map/ppermute | solution.py:31
  37.4 4.9 %all-to-all-start.1 = ((bf16[16,8,2048]{2,1,0:T(8,128)(2,1)}), bf16[16,8,2048]{2,1,0:T(8,128)(2,1)S(1)}, u32[]{:S(2)}, u32[]{:S(2)}) async-start(bf16[16,8,2048]{2,1,0:T(8,128)(2,1)} %bitcast.7), calls=%async_computation.1 | async-start | bytes 1048576 | tf_op jit(solution)/shard_map/all_to_all | solution.py:318
  42.3 9.3 %collective-permute-done.5.refs_4_ = bf16[48,5120]{1,0:T(8,128)(2,1)S(1)} collective-permute-done((bf16[48,5120]{1,0:T(8,128)(2,1)S(1)}, bf16[48,5120]{1,0:T(8,128)(2,1)S(1)}, u32[]{:S(2)}, u32[]{:S(2)}) %collective-permute-start.5) | collective-permute-done | bytes 491552 | tf_op jit(solution)/shard_map/ppermute | solution.py:31
  51.6 1.5 collective-permute-start.6
  53.1 1.7 collective-permute-start.8
  55.2 3.7 %all-to-all-done.1 = bf16[16,8,2048]{2,1,0:T(8,128)(2,1)S(1)} async-done(((bf16[16,8,2048]{2,1,0:T(8,128)(2,1)}), bf16[16,8,2048]{2,1,0:T(8,128)(2,1)S(1)}, u32[]{:S(2)}, u32[]{:S(2)}) %all-to-all-start.1) | async-done | bytes 524320 | tf_op jit(solution)/shard_map/all_to_all | solution.py:318
  58.9 4.1 %collective-permute-done.6.refs_2_ = bf16[48,5120]{1,0:T(8,128)(2,1)} collective-permute-done((bf16[48,5120]{1,0:T(8,128)(2,1)S(1)}, bf16[48,5120]{1,0:T(8,128)(2,1)}, u32[]{:S(2)}, u32[]{:S(2)}) %collective-permute-start.6) | collective-permute-done | bytes 491552 | tf_op jit(solution)/shard_map/ppermute | solution.py:31
  63.0 3.1 %collective-permute-done.8.refs_7_ = bf16[48,5120]{1,0:T(8,128)(2,1)} collective-permute-done((bf16[48,5120]{1,0:T(8,128)(2,1)S(1)}, bf16[48,5120]{1,0:T(8,128)(2,1)}, u32[]{:S(2)}, u32[]{:S(2)}) %collective-permute-start.8) | collective-permute-done | bytes 491552 | tf_op jit(solution)/shard_map/ppermute | solution.py:31
  66.0 2.2 %collective-permute-done.7.refs_5_ = bf16[48,5120]{1,0:T(8,128)(2,1)} collective-permute-done((bf16[48,5120]{1,0:T(8,128)(2,1)S(1)}, bf16[48,5120]{1,0:T(8,128)(2,1)}, u32[]{:S(2)}, u32[]{:S(2)}) %collective-permute-start.7) | collective-permute-done | bytes 491552 | tf_op jit(solution)/shard_map/ppermute | solution.py:31
  68.6 2.1 %collective-permute-start.11 = (bf16[48,5248]{1,0:T(8,128)(2,1)S(1)}, bf16[48,5248]{1,0:T(8,128)(2,1)S(1)}, u32[]{:S(2)}, u32[]{:S(2)}) collective-permute-start(bf16[48,5248]{1,0:T(8,128)(2,1)S(1)} %unpack_y.1.refs_0_), channel_id=1, source_target_pairs={{0,128},{16,144},{32,160},{48,176},{64,192},{80,208},{96,224},{112... | collective-permute-start | bytes 1511432 | tf_op jit(solution)/shard_map/ppermute | solution.py:31
  71.0 1.7 collective-permute-start.9
  72.7 5.8 %collective-permute-done.11.refs_4_ = bf16[48,5248]{1,0:T(8,128)(2,1)S(1)} collective-permute-done((bf16[48,5248]{1,0:T(8,128)(2,1)S(1)}, bf16[48,5248]{1,0:T(8,128)(2,1)S(1)}, u32[]{:S(2)}, u32[]{:S(2)}) %collective-permute-start.11) | collective-permute-done | bytes 503840 | tf_op jit(solution)/shard_map/ppermute | solution.py:31
  78.6 1.8 collective-permute-done.10.refs_3_
  80.4 0.7 collective-permute-done.9.refs_1_
  81.2 3.0 %collective-permute-start.14 = (bf16[48,5248]{1,0:T(8,128)(2,1)S(1)}, bf16[48,5248]{1,0:T(8,128)(2,1)S(1)}, u32[]{:S(2)}, u32[]{:S(2)}) collective-permute-start(bf16[48,5248]{1,0:T(8,128)(2,1)S(1)} %collective-permute-done.11.refs_4_), channel_id=1, source_target_pairs={{0,96},{16,48},{32,0},{48,80},{64,32},{80,112},{96,64},{112,16},{1... | collective-permute-start | bytes 1511432 | tf_op jit(solution)/shard_map/ppermute | solution.py:31
  84.1 0.5 collective-permute-start.16
  85.0 1.6 collective-permute-start.12
  86.6 8.8 %collective-permute-done.14.refs_7_ = bf16[48,5248]{1,0:T(8,128)(2,1)S(1)} collective-permute-done((bf16[48,5248]{1,0:T(8,128)(2,1)S(1)}, bf16[48,5248]{1,0:T(8,128)(2,1)S(1)}, u32[]{:S(2)}, u32[]{:S(2)}) %collective-permute-start.14) | collective-permute-done | bytes 503840 | tf_op jit(solution)/shard_map/ppermute | solution.py:31
  95.4 2.4 %collective-permute-start.15 = (bf16[48,5248]{1,0:T(8,128)(2,1)S(1)}, bf16[48,5248]{1,0:T(8,128)(2,1)S(1)}, u32[]{:S(2)}, u32[]{:S(2)}) collective-permute-start(bf16[48,5248]{1,0:T(8,128)(2,1)S(1)} %collective-permute-done.14.refs_7_), channel_id=1, source_target_pairs={{0,96},{16,48},{32,0},{48,80},{64,32},{80,112},{96,64},{112,16},{1... | collective-permute-start | bytes 1511432 | tf_op jit(solution)/shard_map/ppermute | solution.py:31
  97.8 2.9 %collective-permute-done.16.refs_6_ = bf16[48,5120]{1,0:T(8,128)(2,1)S(1)} collective-permute-done((bf16[48,5120]{1,0:T(8,128)(2,1)}, bf16[48,5120]{1,0:T(8,128)(2,1)S(1)}, u32[]{:S(2)}, u32[]{:S(2)}) %collective-permute-start.16) | collective-permute-done | bytes 491552 | tf_op jit(solution)/shard_map/ppermute | solution.py:31
  100.7 6.5 %pre.1 = (f32[192,384]{1,0:T(8,128)S(1)}, f32[192,384]{1,0:T(8,128)S(1)}, bf16[384,5120]{1,0:T(8,128)(2,1)}) custom-call(bf16[48,5120]{1,0:T(8,128)(2,1)S(1)} %unpack_x.1.refs_0_, bf16[48,5120]{1,0:T(8,128)(2,1)S(1)} %collective-permute-done.3.refs_1_, bf16[48,5120]{1,0:T(8,128)(2,1)} %collective-permute-done.6.refs_2_, ...), custom_call_target="tpu_custom_call" | custom-call | flops 1509949440 | bytes 10000000 | tf_op jit(solution)/shard_map/pre/pallas_call | solution.py:51
  107.3 0.9 copy-done.15
  108.4 9.3 %main.1 = (bf16[48,5248]{1,0:T(8,128)(2,1)S(1)}, bf16[48,5248]{1,0:T(8,128)(2,1)S(1)}, bf16[48,5248]{1,0:T(8,128)(2,1)S(1)}, bf16[48,5248]{1,0:T(8,128)(2,1)S(1)...) custom-call(bf16[48,5248]{1,0:T(8,128)(2,1)S(1)} %unpack_y.1.refs_0_, ...), custom_call_target="tpu_custom_call" | custom-call | flops 2264924160 | bytes 14000000 | tf_op jit(solution)/shard_map/main/pallas_call | solution.py:51
  117.7 0.6 collective-permute-start.17
  118.3 3.6 %collective-permute-start.18 = (bf16[48,5248]{1,0:T(8,128)(2,1)S(1)}, bf16[48,5248]{1,0:T(8,128)(2,1)S(1)}, u32[]{:S(2)}, u32[]{:S(2)}) collective-permute-start(bf16[48,5248]{1,0:T(8,128)(2,1)S(1)} %get-tuple-element.76), channel_id=1, source_target_pairs={{0,96},{16,48},{32,0},{48,80},{64,32},{80,112},{96,64},{112,16},{1... | collective-permute-start | bytes 1511432 | tf_op jit(solution)/shard_map/ppermute | solution.py:31
  121.9 2.1 %copy-done = bf16[384,5248]{1,0:T(8,128)(2,1)S(1)} copy-done((bf16[384,5248]{1,0:T(8,128)(2,1)S(1)}, bf16[384,5248]{1,0:T(8,128)(2,1)}, u32[]{:S(2)}) %copy-start) | copy-done | bytes 4030488
  124.0 3.3 %wgrad_away.1 = bf16[288,5120]{1,0:T(8,128)(2,1)S(1)} custom-call(bf16[192,384]{1,0:T(8,128)(2,1)S(1)} %get-tuple-element.94.hid_ref, bf16[192,384]{1,0:T(8,128)(2,1)S(1)} %get-tuple-element.80.dg_ref, bf16[192,384]{1,0:T(8,128)(2,1)S(1)} %get-tuple-element.81.du_ref, bf16[384,5248]{1,0:T(8,128)(2,1)S(1)} %copy-done, bf16[384,5248]{1,0:T(8,128)(2,1)S(1)} %copy-done, ...), custom_call_target="tpu_custom_call" | custom-call | flops 1132462080 | bytes 12000000 | tf_op jit(solution)/shard_map/wgrad_away/pallas_call | solution.py:396
  127.4 2.5 %collective-permute-done.18.refs_1_ = bf16[48,5248]{1,0:T(8,128)(2,1)S(1)} collective-permute-done((bf16[48,5248]{1,0:T(8,128)(2,1)S(1)}, bf16[48,5248]{1,0:T(8,128)(2,1)S(1)}, u32[]{:S(2)}, u32[]{:S(2)}) %collective-permute-start.18) | collective-permute-done | bytes 503840 | tf_op jit(solution)/shard_map/ppermute | solution.py:31
  129.9 2.1 %collective-permute-done.19.refs_2_ = bf16[48,5248]{1,0:T(8,128)(2,1)S(1)} collective-permute-done((bf16[48,5248]{1,0:T(8,128)(2,1)S(1)}, bf16[48,5248]{1,0:T(8,128)(2,1)S(1)}, u32[]{:S(2)}, u32[]{:S(2)}) %collective-permute-start.19) | collective-permute-done | bytes 503840 | tf_op jit(solution)/shard_map/ppermute | solution.py:31
  133.2 1.6 collective-permute-start.20
  135.3 6.3 %collective-permute-done.21.refs_3_ = bf16[48,5248]{1,0:T(8,128)(2,1)S(1)} collective-permute-done((bf16[48,5248]{1,0:T(8,128)(2,1)S(1)}, bf16[48,5248]{1,0:T(8,128)(2,1)S(1)}, u32[]{:S(2)}, u32[]{:S(2)}) %collective-permute-start.21) | collective-permute-done | bytes 503840 | tf_op jit(solution)/shard_map/ppermute | solution.py:31
  141.5 3.6 %collective-permute-done.20.refs_1_ = bf16[48,5248]{1,0:T(8,128)(2,1)S(1)} collective-permute-done((bf16[48,5248]{1,0:T(8,128)(2,1)S(1)}, bf16[48,5248]{1,0:T(8,128)(2,1)S(1)}, u32[]{:S(2)}, u32[]{:S(2)}) %collective-permute-start.20) | collective-permute-done | bytes 503840 | tf_op jit(solution)/shard_map/ppermute | solution.py:31
  145.4 2.1 %collective-permute-start.23 = (bf16[48,5248]{1,0:T(8,128)(2,1)S(1)}, bf16[48,5248]{1,0:T(8,128)(2,1)S(1)}, u32[]{:S(2)}, u32[]{:S(2)}) collective-permute-start(bf16[48,5248]{1,0:T(8,128)(2,1)S(1)} %join.5), channel_id=1, source_target_pairs={{0,96},{16,48},{32,0},{48,80},{64,32},{80,112},{96,64},{112,16},{1... | collective-permute-start | bytes 1511432 | tf_op jit(solution)/shard_map/ppermute | solution.py:31
  147.5 6.9 %collective-permute-done.23.refs_1_ = bf16[48,5248]{1,0:T(8,128)(2,1)S(1)} collective-permute-done((bf16[48,5248]{1,0:T(8,128)(2,1)S(1)}, bf16[48,5248]{1,0:T(8,128)(2,1)S(1)}, u32[]{:S(2)}, u32[]{:S(2)}) %collective-permute-start.23) | collective-permute-done | bytes 503840 | tf_op jit(solution)/shard_map/ppermute | solution.py:31
  154.4 1.3 last.1
  155.7 8.7 %all-to-all-start.2 = ((bf16[16,8,2048]{2,1,0:T(8,128)(2,1)}), bf16[16,8,2048]{2,1,0:T(8,128)(2,1)}, u32[]{:S(2)}, u32[]{:S(2)}) async-start(bf16[16,8,2048]{2,1,0:T(8,128)(2,1)} %bitcast.9), calls=%async_computation.2 | async-start | bytes 1048576 | tf_op jit(solution)/shard_map/all_to_all | solution.py:318
  164.4 2.1 %copy-done.1 = bf16[384,5248]{1,0:T(8,128)(2,1)S(1)} copy-done((bf16[384,5248]{1,0:T(8,128)(2,1)S(1)}, bf16[384,5248]{1,0:T(8,128)(2,1)}, u32[]{:S(2)}) %copy-start.1) | copy-done | bytes 4030488
  166.5 2.1 %copy-done.3 = bf16[384,5120]{1,0:T(8,128)(2,1)S(1)} copy-done((bf16[384,5120]{1,0:T(8,128)(2,1)S(1)}, bf16[384,5120]{1,0:T(8,128)(2,1)}, u32[]{:S(2)}) %copy-start.3) | copy-done | bytes 3932184
  168.6 5.4 %wgrad_mine.1 = (bf16[96,5120]{1,0:T(8,128)(2,1)}, bf16[96,5120]{1,0:T(8,128)(2,1)}, bf16[96,5120]{1,0:T(8,128)(2,1)}) custom-call(bf16[192,384]{1,0:T(8,128)(2,1)S(1)} %get-tuple-element.94.hid_ref, bf16[192,384]{1,0:T(8,128)(2,1)S(1)} %get-tuple-element.80.dg_ref, bf16[192,384]{1,0:T(8,128)(2,1)S(1)} %get-tuple-element.81.du_ref, ...), custom_call_target="tpu_custom_call" | custom-call | flops 1132462080 | bytes 12000000 | tf_op jit(solution)/shard_map/wgrad_mine/pallas_call | solution.py:396
  174.1 9.4 %all-to-all-done.2 = bf16[16,8,2048]{2,1,0:T(8,128)(2,1)} async-done(((bf16[16,8,2048]{2,1,0:T(8,128)(2,1)}), bf16[16,8,2048]{2,1,0:T(8,128)(2,1)}, u32[]{:S(2)}, u32[]{:S(2)}) %all-to-all-start.2) | async-done | bytes 524320 | tf_op jit(solution)/shard_map/all_to_all | solution.py:318
  183.4 3.5 %final.1 = (bf16[128,5120]{1,0:T(8,128)(2,1)}, bf16[6,128]{1,0:T(8,128)(2,1)}) custom-call(s32[6,128]{1,0:T(8,128)S(1)} %bitcast.22, bf16[128,2048]{1,0:T(8,128)(2,1)} %bitcast.10.in_ref), custom_call_target="tpu_custom_call" | custom-call | flops 600000000 | bytes 2000000 | tf_op jit(solution)/shard_map/final/pallas_call | solution.py:51
  (53 shorter events, 4.2 us)
Async XLA Ops:
  0.6 15.3 %copy-start.8 = (s32[128,6]{0,1:T(8,128)S(1)}, s32[128,6]{0,1:T(8,128)}, u32[]{:S(2)}) copy-start(s32[128,6]{0,1:T(8,128)} %param.10) | copy-start | bytes 9220
  0.6 15.3 %copy-start.9 = (bf16[128,6]{0,1:T(8,128)(2,1)S(1)}, bf16[128,6]{0,1:T(8,128)(2,1)}, u32[]{:S(2)}) copy-start(bf16[128,6]{0,1:T(8,128)(2,1)} %param.9) | copy-start | bytes 4612
  0.7 32.9 %collective-permute-start = (bf16[96,5120]{1,0:T(8,128)(2,1)}, bf16[96,5120]{1,0:T(8,128)(2,1)}, u32[]{:S(2)}, u32[]{:S(2)}) collective-permute-start(bf16[96,5120]{1,0:T(8,128)(2,1)} %bitcast.15), channel_id=1, source_target_pairs={{0,16},{16,0},{32,48},{48,32},{64,80},{80,64},{96,112},{112,96},{1... | collective-permute-start | bytes 2949128 | tf_op jit(solution)/shard_map/ppermute | solution.py:31
  0.8 32.8 %collective-permute-start.1 = (bf16[96,5120]{1,0:T(8,128)(2,1)}, bf16[96,5120]{1,0:T(8,128)(2,1)}, u32[]{:S(2)}, u32[]{:S(2)}) collective-permute-start(bf16[96,5120]{1,0:T(8,128)(2,1)} %bitcast.24), channel_id=1, source_target_pairs={{0,16},{16,0},{32,48},{48,32},{64,80},{80,64},{96,112},{112,96},{1... | collective-permute-start | bytes 2949128 | tf_op jit(solution)/shard_map/ppermute | solution.py:31
  1.2 32.3 %collective-permute-start.2 = (bf16[96,5120]{1,0:T(8,128)(2,1)}, bf16[96,5120]{1,0:T(8,128)(2,1)}, u32[]{:S(2)}, u32[]{:S(2)}) collective-permute-start(bf16[96,5120]{1,0:T(8,128)(2,1)} %bitcast.27), channel_id=1, source_target_pairs={{0,16},{16,0},{32,48},{48,32},{64,80},{80,64},{96,112},{112,96},{1... | collective-permute-start | bytes 2949128 | tf_op jit(solution)/shard_map/ppermute | solution.py:31
  1.4 1.3 copy-start.5
  2.7 0.7 copy-start.7
  3.4 12.6 %copy-start.6 = (bf16[128,5120]{1,0:T(8,128)(2,1)S(1)}, bf16[128,5120]{1,0:T(8,128)(2,1)}, u32[]{:S(2)}) copy-start(bf16[128,5120]{1,0:T(8,128)(2,1)} %refs_2_.1) | copy-start | bytes 3932164
  5.4 95.2 %copy-start.4 = (bf16[1,96,5120]{2,1,0:T(8,128)(2,1)S(1)}, bf16[1,96,5120]{2,1,0:T(8,128)(2,1)}, u32[]{:S(2)}) copy-start(bf16[1,96,5120]{2,1,0:T(8,128)(2,1)} %param.11) | copy-start | bytes 2949124
  5.4 28.1 %all-to-all-start = ((bf16[16,8,1920]{2,1,0:T(8,128)(2,1)}), bf16[16,8,1920]{2,1,0:T(8,128)(2,1)S(1)}, u32[]{:S(2)}, u32[]{:S(2)}) async-start(bf16[16,8,1920]{2,1,0:T(8,128)(2,1)} %bitcast.1), calls=%async_computation | async-start | bytes 983040 | tf_op jit(solution)/shard_map/all_to_all | solution.py:318
  33.9 17.8 %collective-permute-start.5 = (bf16[48,5120]{1,0:T(8,128)(2,1)S(1)}, bf16[48,5120]{1,0:T(8,128)(2,1)S(1)}, u32[]{:S(2)}, u32[]{:S(2)}) collective-permute-start(bf16[48,5120]{1,0:T(8,128)(2,1)S(1)} %unpack_x.1.refs_0_), channel_id=1, source_target_pairs={{0,128},{16,144},{32,160},{48,176},{64,192},{80,208},{96,224},{112... | collective-permute-start | bytes 1474568 | tf_op jit(solution)/shard_map/ppermute | solution.py:31
  34.0 17.7 %collective-permute-start.4 = (bf16[48,5120]{1,0:T(8,128)(2,1)S(1)}, bf16[48,5120]{1,0:T(8,128)(2,1)S(1)}, u32[]{:S(2)}, u32[]{:S(2)}) collective-permute-start(bf16[48,5120]{1,0:T(8,128)(2,1)S(1)} %unpack_x.1.refs_0_), channel_id=1, source_target_pairs={{0,96},{16,48},{32,0},{48,80},{64,32},{80,112},{96,64},{112,16},{1... | collective-permute-start | bytes 1474568 | tf_op jit(solution)/shard_map/ppermute | solution.py:31
  37.4 14.3 %collective-permute-start.3 = (bf16[48,5120]{1,0:T(8,128)(2,1)S(1)}, bf16[48,5120]{1,0:T(8,128)(2,1)S(1)}, u32[]{:S(2)}, u32[]{:S(2)}) collective-permute-start(bf16[48,5120]{1,0:T(8,128)(2,1)S(1)} %unpack_x.1.refs_0_), channel_id=1, source_target_pairs={{0,32},{16,112},{32,64},{48,16},{64,96},{80,48},{96,0},{112,80},{1... | collective-permute-start | bytes 1474568 | tf_op jit(solution)/shard_map/ppermute | solution.py:31
  37.4 21.5 %all-to-all-start.1 = ((bf16[16,8,2048]{2,1,0:T(8,128)(2,1)}), bf16[16,8,2048]{2,1,0:T(8,128)(2,1)S(1)}, u32[]{:S(2)}, u32[]{:S(2)}) async-start(bf16[16,8,2048]{2,1,0:T(8,128)(2,1)} %bitcast.7), calls=%async_computation.1 | async-start | bytes 1048576 | tf_op jit(solution)/shard_map/all_to_all | solution.py:318
  51.6 11.3 %collective-permute-start.6 = (bf16[48,5120]{1,0:T(8,128)(2,1)S(1)}, bf16[48,5120]{1,0:T(8,128)(2,1)}, u32[]{:S(2)}, u32[]{:S(2)}) collective-permute-start(bf16[48,5120]{1,0:T(8,128)(2,1)S(1)} %collective-permute-done.3.refs_1_), channel_id=1, source_target_pairs={{0,32},{16,112},{32,64},{48,16},{64,96},{80,48},{96,0},{112,80},{1... | collective-permute-start | bytes 1474568 | tf_op jit(solution)/shard_map/ppermute | solution.py:31
  53.1 12.9 %collective-permute-start.8 = (bf16[48,5120]{1,0:T(8,128)(2,1)S(1)}, bf16[48,5120]{1,0:T(8,128)(2,1)}, u32[]{:S(2)}, u32[]{:S(2)}) collective-permute-start(bf16[48,5120]{1,0:T(8,128)(2,1)S(1)} %collective-permute-done.5.refs_4_), channel_id=1, source_target_pairs={{0,96},{16,48},{32,0},{48,80},{64,32},{80,112},{96,64},{112,16},{1... | collective-permute-start | bytes 1474568 | tf_op jit(solution)/shard_map/ppermute | solution.py:31
  54.9 13.3 %collective-permute-start.7 = (bf16[48,5120]{1,0:T(8,128)(2,1)S(1)}, bf16[48,5120]{1,0:T(8,128)(2,1)}, u32[]{:S(2)}, u32[]{:S(2)}) collective-permute-start(bf16[48,5120]{1,0:T(8,128)(2,1)S(1)} %collective-permute-done.5.refs_4_), channel_id=1, source_target_pairs={{0,32},{16,112},{32,64},{48,16},{64,96},{80,48},{96,0},{112,80},{1... | collective-permute-start | bytes 1474568 | tf_op jit(solution)/shard_map/ppermute | solution.py:31
  68.6 10.0 %collective-permute-start.11 = (bf16[48,5248]{1,0:T(8,128)(2,1)S(1)}, bf16[48,5248]{1,0:T(8,128)(2,1)S(1)}, u32[]{:S(2)}, u32[]{:S(2)}) collective-permute-start(bf16[48,5248]{1,0:T(8,128)(2,1)S(1)} %unpack_y.1.refs_0_), channel_id=1, source_target_pairs={{0,128},{16,144},{32,160},{48,176},{64,192},{80,208},{96,224},{112... | collective-permute-start | bytes 1511432 | tf_op jit(solution)/shard_map/ppermute | solution.py:31
  70.7 9.7 %collective-permute-start.10 = (bf16[48,5248]{1,0:T(8,128)(2,1)S(1)}, bf16[48,5248]{1,0:T(8,128)(2,1)S(1)}, u32[]{:S(2)}, u32[]{:S(2)}) collective-permute-start(bf16[48,5248]{1,0:T(8,128)(2,1)S(1)} %unpack_y.1.refs_0_), channel_id=1, source_target_pairs={{0,96},{16,48},{32,0},{48,80},{64,32},{80,112},{96,64},{112,16},{1... | collective-permute-start | bytes 1511432 | tf_op jit(solution)/shard_map/ppermute | solution.py:31
  71.0 10.2 %collective-permute-start.9 = (bf16[48,5248]{1,0:T(8,128)(2,1)S(1)}, bf16[48,5248]{1,0:T(8,128)(2,1)S(1)}, u32[]{:S(2)}, u32[]{:S(2)}) collective-permute-start(bf16[48,5248]{1,0:T(8,128)(2,1)S(1)} %unpack_y.1.refs_0_), channel_id=1, source_target_pairs={{0,32},{16,112},{32,64},{48,16},{64,96},{80,48},{96,0},{112,80},{1... | collective-permute-start | bytes 1511432 | tf_op jit(solution)/shard_map/ppermute | solution.py:31
  78.6 28.6 %copy-start.10 = (bf16[48,5248]{1,0:T(8,128)(2,1)}, bf16[48,5248]{1,0:T(8,128)(2,1)S(1)}, u32[]{:S(2)}) copy-start(bf16[48,5248]{1,0:T(8,128)(2,1)S(1)} %collective-permute-done.11.refs_4_) | copy-start | bytes 1511428
  80.4 26.8 %copy-start.11 = (bf16[48,5248]{1,0:T(8,128)(2,1)}, bf16[48,5248]{1,0:T(8,128)(2,1)S(1)}, u32[]{:S(2)}) copy-start(bf16[48,5248]{1,0:T(8,128)(2,1)S(1)} %collective-permute-done.10.refs_3_) | copy-start | bytes 1511428
  81.2 14.2 %collective-permute-start.14 = (bf16[48,5248]{1,0:T(8,128)(2,1)S(1)}, bf16[48,5248]{1,0:T(8,128)(2,1)S(1)}, u32[]{:S(2)}, u32[]{:S(2)}) collective-permute-start(bf16[48,5248]{1,0:T(8,128)(2,1)S(1)} %collective-permute-done.11.refs_4_), channel_id=1, source_target_pairs={{0,96},{16,48},{32,0},{48,80},{64,32},{80,112},{96,64},{112,16},{1... | collective-permute-start | bytes 1511432 | tf_op jit(solution)/shard_map/ppermute | solution.py:31
  84.1 16.6 %collective-permute-start.16 = (bf16[48,5120]{1,0:T(8,128)(2,1)}, bf16[48,5120]{1,0:T(8,128)(2,1)S(1)}, u32[]{:S(2)}, u32[]{:S(2)}) collective-permute-start(bf16[48,5120]{1,0:T(8,128)(2,1)} %collective-permute-done.8.refs_7_), channel_id=1, source_target_pairs={{0,96},{16,48},{32,0},{48,80},{64,32},{80,112},{96,64},{112,16},{1... | collective-permute-start | bytes 1474568 | tf_op jit(solution)/shard_map/ppermute | solution.py:31
  84.6 22.6 %collective-permute-start.13 = (bf16[48,5248]{1,0:T(8,128)(2,1)S(1)}, bf16[48,5248]{1,0:T(8,128)(2,1)S(1)}, u32[]{:S(2)}, u32[]{:S(2)}) collective-permute-start(bf16[48,5248]{1,0:T(8,128)(2,1)S(1)} %collective-permute-done.9.refs_1_), channel_id=1, source_target_pairs={{0,128},{16,144},{32,160},{48,176},{64,192},{80,208},{96,224},{112... | collective-permute-start | bytes 1511432 | tf_op jit(solution)/shard_map/ppermute | solution.py:31
  85.0 22.3 %collective-permute-start.12 = (bf16[48,5248]{1,0:T(8,128)(2,1)S(1)}, bf16[48,5248]{1,0:T(8,128)(2,1)S(1)}, u32[]{:S(2)}, u32[]{:S(2)}) collective-permute-start(bf16[48,5248]{1,0:T(8,128)(2,1)S(1)} %collective-permute-done.9.refs_1_), channel_id=1, source_target_pairs={{0,32},{16,112},{32,64},{48,16},{64,96},{80,48},{96,0},{112,80},{1... | collective-permute-start | bytes 1511432 | tf_op jit(solution)/shard_map/ppermute | solution.py:31
  95.4 11.8 %copy-start.12 = (bf16[48,5248]{1,0:T(8,128)(2,1)}, bf16[48,5248]{1,0:T(8,128)(2,1)S(1)}, u32[]{:S(2)}) copy-start(bf16[48,5248]{1,0:T(8,128)(2,1)S(1)} %collective-permute-done.14.refs_7_) | copy-start | bytes 1511428
  95.4 11.9 %collective-permute-start.15 = (bf16[48,5248]{1,0:T(8,128)(2,1)S(1)}, bf16[48,5248]{1,0:T(8,128)(2,1)S(1)}, u32[]{:S(2)}, u32[]{:S(2)}) collective-permute-start(bf16[48,5248]{1,0:T(8,128)(2,1)S(1)} %collective-permute-done.14.refs_7_), channel_id=1, source_target_pairs={{0,96},{16,48},{32,0},{48,80},{64,32},{80,112},{96,64},{112,16},{1... | collective-permute-start | bytes 1511432 | tf_op jit(solution)/shard_map/ppermute | solution.py:31
  107.3 0.9 copy-start.13
  107.3 1.1 copy-start.14
  107.3 0.9 copy-start.15
  108.4 13.5 %copy-start.2 = (bf16[384,5120]{1,0:T(8,128)(2,1)S(1)}, bf16[384,5120]{1,0:T(8,128)(2,1)}, u32[]{:S(2)}) copy-start(bf16[384,5120]{1,0:T(8,128)(2,1)} %get-tuple-element.83.x_ref) | copy-start | bytes 11796484
  117.7 9.7 %collective-permute-start.17 = (bf16[48,5248]{1,0:T(8,128)(2,1)S(1)}, bf16[48,5248]{1,0:T(8,128)(2,1)S(1)}, u32[]{:S(2)}, u32[]{:S(2)}) collective-permute-start(bf16[48,5248]{1,0:T(8,128)(2,1)S(1)} %get-tuple-element.75), channel_id=1, source_target_pairs={{0,128},{16,144},{32,160},{48,176},{64,192},{80,208},{96,224},{112... | collective-permute-start | bytes 1511432 | tf_op jit(solution)/shard_map/ppermute | solution.py:31
  118.3 11.6 %collective-permute-start.18 = (bf16[48,5248]{1,0:T(8,128)(2,1)S(1)}, bf16[48,5248]{1,0:T(8,128)(2,1)S(1)}, u32[]{:S(2)}, u32[]{:S(2)}) collective-permute-start(bf16[48,5248]{1,0:T(8,128)(2,1)S(1)} %get-tuple-element.76), channel_id=1, source_target_pairs={{0,96},{16,48},{32,0},{48,80},{64,32},{80,112},{96,64},{112,16},{1... | collective-permute-start | bytes 1511432 | tf_op jit(solution)/shard_map/ppermute | solution.py:31
  121.9 10.2 %collective-permute-start.19 = (bf16[48,5248]{1,0:T(8,128)(2,1)S(1)}, bf16[48,5248]{1,0:T(8,128)(2,1)S(1)}, u32[]{:S(2)}, u32[]{:S(2)}) collective-permute-start(bf16[48,5248]{1,0:T(8,128)(2,1)S(1)} %get-tuple-element.77), channel_id=1, source_target_pairs={{0,32},{16,112},{32,64},{48,16},{64,96},{80,48},{96,0},{112,80},{1... | collective-permute-start | bytes 1511432 | tf_op jit(solution)/shard_map/ppermute | solution.py:31
  121.9 2.1 %copy-start = (bf16[384,5248]{1,0:T(8,128)(2,1)S(1)}, bf16[384,5248]{1,0:T(8,128)(2,1)}, u32[]{:S(2)}) copy-start(bf16[384,5248]{1,0:T(8,128)(2,1)} %get-tuple-element.82.y_ref.prob_ref) | copy-start | bytes 12091396
  132.5 9.0 %collective-permute-start.21 = (bf16[48,5248]{1,0:T(8,128)(2,1)S(1)}, bf16[48,5248]{1,0:T(8,128)(2,1)S(1)}, u32[]{:S(2)}, u32[]{:S(2)}) collective-permute-start(bf16[48,5248]{1,0:T(8,128)(2,1)S(1)} %join.4), channel_id=1, source_target_pairs={{0,128},{16,144},{32,160},{48,176},{64,192},{80,208},{96,224},{112... | collective-permute-start | bytes 1511432 | tf_op jit(solution)/shard_map/ppermute | solution.py:31
  133.2 11.9 %collective-permute-start.20 = (bf16[48,5248]{1,0:T(8,128)(2,1)S(1)}, bf16[48,5248]{1,0:T(8,128)(2,1)S(1)}, u32[]{:S(2)}, u32[]{:S(2)}) collective-permute-start(bf16[48,5248]{1,0:T(8,128)(2,1)S(1)} %join.3), channel_id=1, source_target_pairs={{0,96},{16,48},{32,0},{48,80},{64,32},{80,112},{96,64},{112,16},{1... | collective-permute-start | bytes 1511432 | tf_op jit(solution)/shard_map/ppermute | solution.py:31
  134.8 10.3 %collective-permute-start.22 = (bf16[48,5248]{1,0:T(8,128)(2,1)S(1)}, bf16[48,5248]{1,0:T(8,128)(2,1)S(1)}, u32[]{:S(2)}, u32[]{:S(2)}) collective-permute-start(bf16[48,5248]{1,0:T(8,128)(2,1)S(1)} %get-tuple-element.88), channel_id=1, source_target_pairs={{0,32},{16,112},{32,64},{48,16},{64,96},{80,48},{96,0},{112,80},{1... | collective-permute-start | bytes 1511432 | tf_op jit(solution)/shard_map/ppermute | solution.py:31
  145.1 19.3 %collective-permute-start.24 = (bf16[288,5120]{1,0:T(8,128)(2,1)S(1)}, bf16[288,5120]{1,0:T(8,128)(2,1)}, u32[]{:S(2)}, u32[]{:S(2)}) collective-permute-start(bf16[288,5120]{1,0:T(8,128)(2,1)S(1)} %wgrad_away.1), channel_id=1, source_target_pairs={{0,16},{16,0},{32,48},{48,32},{64,80},{80,64},{96,112},{112,96},{1... | collective-permute-start | bytes 8847368 | tf_op jit(solution)/shard_map/ppermute | solution.py:31
  145.4 9.0 %collective-permute-start.23 = (bf16[48,5248]{1,0:T(8,128)(2,1)S(1)}, bf16[48,5248]{1,0:T(8,128)(2,1)S(1)}, u32[]{:S(2)}, u32[]{:S(2)}) collective-permute-start(bf16[48,5248]{1,0:T(8,128)(2,1)S(1)} %join.5), channel_id=1, source_target_pairs={{0,96},{16,48},{32,0},{48,80},{64,32},{80,112},{96,64},{112,16},{1... | collective-permute-start | bytes 1511432 | tf_op jit(solution)/shard_map/ppermute | solution.py:31
  155.7 27.7 %all-to-all-start.2 = ((bf16[16,8,2048]{2,1,0:T(8,128)(2,1)}), bf16[16,8,2048]{2,1,0:T(8,128)(2,1)}, u32[]{:S(2)}, u32[]{:S(2)}) async-start(bf16[16,8,2048]{2,1,0:T(8,128)(2,1)} %bitcast.9), calls=%async_computation.2 | async-start | bytes 1048576 | tf_op jit(solution)/shard_map/all_to_all | solution.py:318
  164.4 2.1 %copy-start.1 = (bf16[384,5248]{1,0:T(8,128)(2,1)S(1)}, bf16[384,5248]{1,0:T(8,128)(2,1)}, u32[]{:S(2)}) copy-start(bf16[384,5248]{1,0:T(8,128)(2,1)} %get-tuple-element.82.y_ref.prob_ref) | copy-start | bytes 12091396
  166.5 2.1 %copy-start.3 = (bf16[384,5120]{1,0:T(8,128)(2,1)S(1)}, bf16[384,5120]{1,0:T(8,128)(2,1)}, u32[]{:S(2)}) copy-start(bf16[384,5120]{1,0:T(8,128)(2,1)} %get-tuple-element.83.x_ref) | copy-start | bytes 11796484

commit v6 on v5

--- a/solution.py
+++ b/solution.py
@@ -424,14 +424,14 @@
     pb = hop(pb, X_A)
     f, oz, pb, away = together((f, oz, pb, away))
     pa = hop(join(pa, f), X_B)
-    came = hop(away, C_SWAP)
     last = call(
         functools.partial(last_kernel, group=group),
         shape((LANES, CAP * group + LANES), BF16),
         "last",
         cost=(10**8, 3 * 10**6),
     )(own, pa, pb, oz)
-    last, hidden = together((last, hidden))
+    last, hidden, away = together((last, hidden, away))
+    came = hop(away, C_SWAP)
     back = exchange(last)
     g_grad, u_grad, d_grad = wgrad(came)
     back, g_grad, u_grad, d_grad = together((back, g_grad, u_grad, d_grad))

time: 188 us -> 187 us (level)
  no operation moved by 1% of the time
where the time goes in v6:
time: 187 us
  waiting for transfers between devices  88.8 us (47%)
  starting transfers between devices  52.4 us (28%)
  Pallas kernels  35.1 us (19%)
  local copies, waits for them, and re-layouts  9.49 us (5%)
    ppermute x25, waiting for transfers between devices, hop(): return lax.ppermute(a, 'edp', perm)  60.4 us
    all_to_all x3, waiting for transfers between devices, exchange(): a = lax.all_to_all(a, 'ep', split_axis=0, concat_axis=0, tiled=True)  28.5 us
    ppermute x25, starting transfers between devices, hop(): return lax.ppermute(a, 'edp', perm)  28.4 us
    pallas_call x11, Pallas kernels, run(): pl.pallas_call(kernel, out_shape=outs, in_specs=[one] * len(args) if spec...  26.5 us
    all_to_all x3, starting transfers between devices, exchange(): a = lax.all_to_all(a, 'ep', split_axis=0, concat_axis=0, tiled=True)  24 us
    unnamed x32, local copies, waits for them, and re-layouts  9.49 us
    pallas_call x2, Pallas kernels, wgrad(): pl.pallas_call(functools.partial(wgrad_kernel, away=not came), out_shape=...  8.68 us
  transfers between devices with their start and end apart: 28, of which 18 were waited for; matrix products, arithmetic and copies ran while one was open for 0% of the time, Pallas kernels for 11%

profile of v6, /device:TPU:32, one launch (start us, length us, event | category | flops | bytes accessed | tf_op | source)
XLA Modules:
  0.0 186.8 jit_solution(5430305427038628097)
XLA Ops:
  0.8 0.5 collective-permute-start.1
  1.4 1.3 copy-done.5
  2.7 0.7 copy-done.7
  3.4 2.1 %send_x.1 = bf16[128,1920]{1,0:T(8,128)(2,1)} custom-call(s32[6,128]{1,0:T(8,128)S(1)} %bitcast.20, bf16[128,5120]{1,0:T(8,128)(2,1)S(1)} %copy-done.5), custom_call_target="tpu_custom_call" | custom-call | flops 600000000 | bytes 2000000 | tf_op jit(solution)/shard_map/send_x/pallas_call | solution.py:51
  5.4 10.4 %all-to-all-start = ((bf16[16,8,1920]{2,1,0:T(8,128)(2,1)}), bf16[16,8,1920]{2,1,0:T(8,128)(2,1)S(1)}, u32[]{:S(2)}, u32[]{:S(2)}) async-start(bf16[16,8,1920]{2,1,0:T(8,128)(2,1)} %bitcast.1), calls=%async_computation | async-start | bytes 983040 | tf_op jit(solution)/shard_map/all_to_all | solution.py:318
  15.9 2.1 %send_y.1 = bf16[128,2048]{1,0:T(8,128)(2,1)} custom-call(s32[6,128]{1,0:T(8,128)S(1)} %bitcast.21, bf16[6,128]{1,0:T(8,128)(2,1)S(1)} %bitcast.23, bf16[128,5120]{1,0:T(8,128)(2,1)S(1)} %copy-done.6), custom_call_target="tpu_custom_call" | custom-call | flops 600000000 | bytes 2000000 | tf_op jit(solution)/shard_map/send_y/pallas_call | solution.py:51
  18.0 15.5 %all-to-all-done = bf16[16,8,1920]{2,1,0:T(8,128)(2,1)S(1)} async-done(((bf16[16,8,1920]{2,1,0:T(8,128)(2,1)}), bf16[16,8,1920]{2,1,0:T(8,128)(2,1)S(1)}, u32[]{:S(2)}, u32[]{:S(2)}) %all-to-all-start) | async-done | bytes 491552 | tf_op jit(solution)/shard_map/all_to_all | solution.py:318
  34.0 3.4 %collective-permute-start.4 = (bf16[48,5120]{1,0:T(8,128)(2,1)S(1)}, bf16[48,5120]{1,0:T(8,128)(2,1)S(1)}, u32[]{:S(2)}, u32[]{:S(2)}) collective-permute-start(bf16[48,5120]{1,0:T(8,128)(2,1)S(1)} %unpack_x.1.refs_0_), channel_id=1, source_target_pairs={{0,96},{16,48},{32,0},{48,80},{64,32},{80,112},{96,64},{112,16},{1... | collective-permute-start | bytes 1474568 | tf_op jit(solution)/shard_map/ppermute | solution.py:31
  37.4 4.9 %all-to-all-start.1 = ((bf16[16,8,2048]{2,1,0:T(8,128)(2,1)}), bf16[16,8,2048]{2,1,0:T(8,128)(2,1)S(1)}, u32[]{:S(2)}, u32[]{:S(2)}) async-start(bf16[16,8,2048]{2,1,0:T(8,128)(2,1)} %bitcast.7), calls=%async_computation.1 | async-start | bytes 1048576 | tf_op jit(solution)/shard_map/all_to_all | solution.py:318
  42.3 9.3 %collective-permute-done.5.refs_4_ = bf16[48,5120]{1,0:T(8,128)(2,1)S(1)} collective-permute-done((bf16[48,5120]{1,0:T(8,128)(2,1)S(1)}, bf16[48,5120]{1,0:T(8,128)(2,1)S(1)}, u32[]{:S(2)}, u32[]{:S(2)}) %collective-permute-start.5) | collective-permute-done | bytes 491552 | tf_op jit(solution)/shard_map/ppermute | solution.py:31
  51.6 1.5 collective-permute-start.6
  53.1 1.7 collective-permute-start.8
  55.2 3.7 %all-to-all-done.1 = bf16[16,8,2048]{2,1,0:T(8,128)(2,1)S(1)} async-done(((bf16[16,8,2048]{2,1,0:T(8,128)(2,1)}), bf16[16,8,2048]{2,1,0:T(8,128)(2,1)S(1)}, u32[]{:S(2)}, u32[]{:S(2)}) %all-to-all-start.1) | async-done | bytes 524320 | tf_op jit(solution)/shard_map/all_to_all | solution.py:318
  58.9 4.1 %collective-permute-done.6.refs_2_ = bf16[48,5120]{1,0:T(8,128)(2,1)} collective-permute-done((bf16[48,5120]{1,0:T(8,128)(2,1)S(1)}, bf16[48,5120]{1,0:T(8,128)(2,1)}, u32[]{:S(2)}, u32[]{:S(2)}) %collective-permute-start.6) | collective-permute-done | bytes 491552 | tf_op jit(solution)/shard_map/ppermute | solution.py:31
  63.0 3.1 %collective-permute-done.8.refs_7_ = bf16[48,5120]{1,0:T(8,128)(2,1)} collective-permute-done((bf16[48,5120]{1,0:T(8,128)(2,1)S(1)}, bf16[48,5120]{1,0:T(8,128)(2,1)}, u32[]{:S(2)}, u32[]{:S(2)}) %collective-permute-start.8) | collective-permute-done | bytes 491552 | tf_op jit(solution)/shard_map/ppermute | solution.py:31
  66.0 2.2 %collective-permute-done.7.refs_5_ = bf16[48,5120]{1,0:T(8,128)(2,1)} collective-permute-done((bf16[48,5120]{1,0:T(8,128)(2,1)S(1)}, bf16[48,5120]{1,0:T(8,128)(2,1)}, u32[]{:S(2)}, u32[]{:S(2)}) %collective-permute-start.7) | collective-permute-done | bytes 491552 | tf_op jit(solution)/shard_map/ppermute | solution.py:31
  68.6 2.1 %collective-permute-start.11 = (bf16[48,5248]{1,0:T(8,128)(2,1)S(1)}, bf16[48,5248]{1,0:T(8,128)(2,1)S(1)}, u32[]{:S(2)}, u32[]{:S(2)}) collective-permute-start(bf16[48,5248]{1,0:T(8,128)(2,1)S(1)} %unpack_y.1.refs_0_), channel_id=1, source_target_pairs={{0,128},{16,144},{32,160},{48,176},{64,192},{80,208},{96,224},{112... | collective-permute-start | bytes 1511432 | tf_op jit(solution)/shard_map/ppermute | solution.py:31
  71.0 1.7 collective-permute-start.9
  72.7 5.8 %collective-permute-done.11.refs_4_ = bf16[48,5248]{1,0:T(8,128)(2,1)S(1)} collective-permute-done((bf16[48,5248]{1,0:T(8,128)(2,1)S(1)}, bf16[48,5248]{1,0:T(8,128)(2,1)S(1)}, u32[]{:S(2)}, u32[]{:S(2)}) %collective-permute-start.11) | collective-permute-done | bytes 503840 | tf_op jit(solution)/shard_map/ppermute | solution.py:31
  78.6 1.8 collective-permute-done.10.refs_3_
  80.4 0.7 collective-permute-done.9.refs_1_
  81.2 3.0 %collective-permute-start.14 = (bf16[48,5248]{1,0:T(8,128)(2,1)S(1)}, bf16[48,5248]{1,0:T(8,128)(2,1)S(1)}, u32[]{:S(2)}, u32[]{:S(2)}) collective-permute-start(bf16[48,5248]{1,0:T(8,128)(2,1)S(1)} %collective-permute-done.11.refs_4_), channel_id=1, source_target_pairs={{0,96},{16,48},{32,0},{48,80},{64,32},{80,112},{96,64},{112,16},{1... | collective-permute-start | bytes 1511432 | tf_op jit(solution)/shard_map/ppermute | solution.py:31
  84.1 0.5 collective-permute-start.16
  85.0 1.6 collective-permute-start.12
  86.6 8.8 %collective-permute-done.14.refs_7_ = bf16[48,5248]{1,0:T(8,128)(2,1)S(1)} collective-permute-done((bf16[48,5248]{1,0:T(8,128)(2,1)S(1)}, bf16[48,5248]{1,0:T(8,128)(2,1)S(1)}, u32[]{:S(2)}, u32[]{:S(2)}) %collective-permute-start.14) | collective-permute-done | bytes 503840 | tf_op jit(solution)/shard_map/ppermute | solution.py:31
  95.4 2.4 %collective-permute-start.15 = (bf16[48,5248]{1,0:T(8,128)(2,1)S(1)}, bf16[48,5248]{1,0:T(8,128)(2,1)S(1)}, u32[]{:S(2)}, u32[]{:S(2)}) collective-permute-start(bf16[48,5248]{1,0:T(8,128)(2,1)S(1)} %collective-permute-done.14.refs_7_), channel_id=1, source_target_pairs={{0,96},{16,48},{32,0},{48,80},{64,32},{80,112},{96,64},{112,16},{1... | collective-permute-start | bytes 1511432 | tf_op jit(solution)/shard_map/ppermute | solution.py:31
  97.8 2.9 %collective-permute-done.16.refs_6_ = bf16[48,5120]{1,0:T(8,128)(2,1)S(1)} collective-permute-done((bf16[48,5120]{1,0:T(8,128)(2,1)}, bf16[48,5120]{1,0:T(8,128)(2,1)S(1)}, u32[]{:S(2)}, u32[]{:S(2)}) %collective-permute-start.16) | collective-permute-done | bytes 491552 | tf_op jit(solution)/shard_map/ppermute | solution.py:31
  100.7 6.5 %pre.1 = (f32[192,384]{1,0:T(8,128)S(1)}, f32[192,384]{1,0:T(8,128)S(1)}, bf16[384,5120]{1,0:T(8,128)(2,1)}) custom-call(bf16[48,5120]{1,0:T(8,128)(2,1)S(1)} %unpack_x.1.refs_0_, bf16[48,5120]{1,0:T(8,128)(2,1)S(1)} %collective-permute-done.3.refs_1_, bf16[48,5120]{1,0:T(8,128)(2,1)} %collective-permute-done.6.refs_2_, ...), custom_call_target="tpu_custom_call" | custom-call | flops 1509949440 | bytes 10000000 | tf_op jit(solution)/shard_map/pre/pallas_call | solution.py:51
  107.3 0.9 copy-done.15
  108.4 9.3 %main.1 = (bf16[48,5248]{1,0:T(8,128)(2,1)S(1)}, bf16[48,5248]{1,0:T(8,128)(2,1)S(1)}, bf16[48,5248]{1,0:T(8,128)(2,1)S(1)}, bf16[48,5248]{1,0:T(8,128)(2,1)S(1)...) custom-call(bf16[48,5248]{1,0:T(8,128)(2,1)S(1)} %unpack_y.1.refs_0_, ...), custom_call_target="tpu_custom_call" | custom-call | flops 2264924160 | bytes 14000000 | tf_op jit(solution)/shard_map/main/pallas_call | solution.py:51
  117.7 0.6 collective-permute-start.17
  118.3 3.6 %collective-permute-start.18 = (bf16[48,5248]{1,0:T(8,128)(2,1)S(1)}, bf16[48,5248]{1,0:T(8,128)(2,1)S(1)}, u32[]{:S(2)}, u32[]{:S(2)}) collective-permute-start(bf16[48,5248]{1,0:T(8,128)(2,1)S(1)} %get-tuple-element.77), channel_id=1, source_target_pairs={{0,96},{16,48},{32,0},{48,80},{64,32},{80,112},{96,64},{112,16},{1... | collective-permute-start | bytes 1511432 | tf_op jit(solution)/shard_map/ppermute | solution.py:31
  121.9 2.1 %copy-done = bf16[384,5248]{1,0:T(8,128)(2,1)S(1)} copy-done((bf16[384,5248]{1,0:T(8,128)(2,1)S(1)}, bf16[384,5248]{1,0:T(8,128)(2,1)}, u32[]{:S(2)}) %copy-start) | copy-done | bytes 4030488
  124.0 3.3 %wgrad_away.1 = bf16[288,5120]{1,0:T(8,128)(2,1)S(1)} custom-call(bf16[192,384]{1,0:T(8,128)(2,1)S(1)} %get-tuple-element.96.hid_ref, bf16[192,384]{1,0:T(8,128)(2,1)S(1)} %get-tuple-element.81.dg_ref, bf16[192,384]{1,0:T(8,128)(2,1)S(1)} %get-tuple-element.82.du_ref, bf16[384,5248]{1,0:T(8,128)(2,1)S(1)} %copy-done, bf16[384,5248]{1,0:T(8,128)(2,1)S(1)} %copy-done, ...), custom_call_target="tpu_custom_call" | custom-call | flops 1132462080 | bytes 12000000 | tf_op jit(solution)/shard_map/wgrad_away/pallas_call | solution.py:396
  127.4 2.5 %collective-permute-done.18.refs_1_ = bf16[48,5248]{1,0:T(8,128)(2,1)S(1)} collective-permute-done((bf16[48,5248]{1,0:T(8,128)(2,1)S(1)}, bf16[48,5248]{1,0:T(8,128)(2,1)S(1)}, u32[]{:S(2)}, u32[]{:S(2)}) %collective-permute-start.18) | collective-permute-done | bytes 503840 | tf_op jit(solution)/shard_map/ppermute | solution.py:31
  129.9 2.1 %collective-permute-done.19.refs_2_ = bf16[48,5248]{1,0:T(8,128)(2,1)S(1)} collective-permute-done((bf16[48,5248]{1,0:T(8,128)(2,1)S(1)}, bf16[48,5248]{1,0:T(8,128)(2,1)S(1)}, u32[]{:S(2)}, u32[]{:S(2)}) %collective-permute-start.19) | collective-permute-done | bytes 503840 | tf_op jit(solution)/shard_map/ppermute | solution.py:31
  133.2 1.6 collective-permute-start.20
  135.3 6.3 %collective-permute-done.21.refs_3_ = bf16[48,5248]{1,0:T(8,128)(2,1)S(1)} collective-permute-done((bf16[48,5248]{1,0:T(8,128)(2,1)S(1)}, bf16[48,5248]{1,0:T(8,128)(2,1)S(1)}, u32[]{:S(2)}, u32[]{:S(2)}) %collective-permute-start.21) | collective-permute-done | bytes 503840 | tf_op jit(solution)/shard_map/ppermute | solution.py:31
  141.5 3.6 %collective-permute-done.20.refs_1_ = bf16[48,5248]{1,0:T(8,128)(2,1)S(1)} collective-permute-done((bf16[48,5248]{1,0:T(8,128)(2,1)S(1)}, bf16[48,5248]{1,0:T(8,128)(2,1)S(1)}, u32[]{:S(2)}, u32[]{:S(2)}) %collective-permute-start.20) | collective-permute-done | bytes 503840 | tf_op jit(solution)/shard_map/ppermute | solution.py:31
  145.4 2.1 %collective-permute-start.23 = (bf16[48,5248]{1,0:T(8,128)(2,1)S(1)}, bf16[48,5248]{1,0:T(8,128)(2,1)S(1)}, u32[]{:S(2)}, u32[]{:S(2)}) collective-permute-start(bf16[48,5248]{1,0:T(8,128)(2,1)S(1)} %join.5), channel_id=1, source_target_pairs={{0,96},{16,48},{32,0},{48,80},{64,32},{80,112},{96,64},{112,16},{1... | collective-permute-start | bytes 1511432 | tf_op jit(solution)/shard_map/ppermute | solution.py:31
  147.5 6.9 %collective-permute-done.23.refs_1_ = bf16[48,5248]{1,0:T(8,128)(2,1)S(1)} collective-permute-done((bf16[48,5248]{1,0:T(8,128)(2,1)S(1)}, bf16[48,5248]{1,0:T(8,128)(2,1)S(1)}, u32[]{:S(2)}, u32[]{:S(2)}) %collective-permute-start.23) | collective-permute-done | bytes 503840 | tf_op jit(solution)/shard_map/ppermute | solution.py:31
  154.4 1.3 last.1
  155.7 8.7 %all-to-all-start.2 = ((bf16[16,8,2048]{2,1,0:T(8,128)(2,1)}), bf16[16,8,2048]{2,1,0:T(8,128)(2,1)}, u32[]{:S(2)}, u32[]{:S(2)}) async-start(bf16[16,8,2048]{2,1,0:T(8,128)(2,1)} %bitcast.9), calls=%async_computation.2 | async-start | bytes 1048576 | tf_op jit(solution)/shard_map/all_to_all | solution.py:318
  164.4 2.1 %copy-done.1 = bf16[384,5248]{1,0:T(8,128)(2,1)S(1)} copy-done((bf16[384,5248]{1,0:T(8,128)(2,1)S(1)}, bf16[384,5248]{1,0:T(8,128)(2,1)}, u32[]{:S(2)}) %copy-start.1) | copy-done | bytes 4030488
  166.5 2.1 %copy-done.3 = bf16[384,5120]{1,0:T(8,128)(2,1)S(1)} copy-done((bf16[384,5120]{1,0:T(8,128)(2,1)S(1)}, bf16[384,5120]{1,0:T(8,128)(2,1)}, u32[]{:S(2)}) %copy-start.3) | copy-done | bytes 3932184
  168.6 5.4 %wgrad_mine.1 = (bf16[96,5120]{1,0:T(8,128)(2,1)}, bf16[96,5120]{1,0:T(8,128)(2,1)}, bf16[96,5120]{1,0:T(8,128)(2,1)}) custom-call(bf16[192,384]{1,0:T(8,128)(2,1)S(1)} %get-tuple-element.96.hid_ref, bf16[192,384]{1,0:T(8,128)(2,1)S(1)} %get-tuple-element.81.dg_ref, bf16[192,384]{1,0:T(8,128)(2,1)S(1)} %get-tuple-element.82.du_ref, ...), custom_call_target="tpu_custom_call" | custom-call | flops 1132462080 | bytes 12000000 | tf_op jit(solution)/shard_map/wgrad_mine/pallas_call | solution.py:396
  174.1 9.2 %all-to-all-done.2 = bf16[16,8,2048]{2,1,0:T(8,128)(2,1)} async-done(((bf16[16,8,2048]{2,1,0:T(8,128)(2,1)}), bf16[16,8,2048]{2,1,0:T(8,128)(2,1)}, u32[]{:S(2)}, u32[]{:S(2)}) %all-to-all-start.2) | async-done | bytes 524320 | tf_op jit(solution)/shard_map/all_to_all | solution.py:318
  183.3 3.5 %final.1 = (bf16[128,5120]{1,0:T(8,128)(2,1)}, bf16[6,128]{1,0:T(8,128)(2,1)}) custom-call(s32[6,128]{1,0:T(8,128)S(1)} %bitcast.22, bf16[128,2048]{1,0:T(8,128)(2,1)} %bitcast.10.in_ref), custom_call_target="tpu_custom_call" | custom-call | flops 600000000 | bytes 2000000 | tf_op jit(solution)/shard_map/final/pallas_call | solution.py:51
  (53 shorter events, 4.2 us)
Async XLA Ops:
  0.6 15.3 %copy-start.8 = (s32[128,6]{0,1:T(8,128)S(1)}, s32[128,6]{0,1:T(8,128)}, u32[]{:S(2)}) copy-start(s32[128,6]{0,1:T(8,128)} %param.10) | copy-start | bytes 9220
  0.6 15.3 %copy-start.9 = (bf16[128,6]{0,1:T(8,128)(2,1)S(1)}, bf16[128,6]{0,1:T(8,128)(2,1)}, u32[]{:S(2)}) copy-start(bf16[128,6]{0,1:T(8,128)(2,1)} %param.9) | copy-start | bytes 4612
  0.7 32.9 %collective-permute-start = (bf16[96,5120]{1,0:T(8,128)(2,1)}, bf16[96,5120]{1,0:T(8,128)(2,1)}, u32[]{:S(2)}, u32[]{:S(2)}) collective-permute-start(bf16[96,5120]{1,0:T(8,128)(2,1)} %bitcast.15), channel_id=1, source_target_pairs={{0,16},{16,0},{32,48},{48,32},{64,80},{80,64},{96,112},{112,96},{1... | collective-permute-start | bytes 2949128 | tf_op jit(solution)/shard_map/ppermute | solution.py:31
  0.8 32.8 %collective-permute-start.1 = (bf16[96,5120]{1,0:T(8,128)(2,1)}, bf16[96,5120]{1,0:T(8,128)(2,1)}, u32[]{:S(2)}, u32[]{:S(2)}) collective-permute-start(bf16[96,5120]{1,0:T(8,128)(2,1)} %bitcast.24), channel_id=1, source_target_pairs={{0,16},{16,0},{32,48},{48,32},{64,80},{80,64},{96,112},{112,96},{1... | collective-permute-start | bytes 2949128 | tf_op jit(solution)/shard_map/ppermute | solution.py:31
  1.2 32.3 %collective-permute-start.2 = (bf16[96,5120]{1,0:T(8,128)(2,1)}, bf16[96,5120]{1,0:T(8,128)(2,1)}, u32[]{:S(2)}, u32[]{:S(2)}) collective-permute-start(bf16[96,5120]{1,0:T(8,128)(2,1)} %bitcast.27), channel_id=1, source_target_pairs={{0,16},{16,0},{32,48},{48,32},{64,80},{80,64},{96,112},{112,96},{1... | collective-permute-start | bytes 2949128 | tf_op jit(solution)/shard_map/ppermute | solution.py:31
  1.4 1.3 copy-start.5
  2.7 0.7 copy-start.7
  3.4 12.6 %copy-start.6 = (bf16[128,5120]{1,0:T(8,128)(2,1)S(1)}, bf16[128,5120]{1,0:T(8,128)(2,1)}, u32[]{:S(2)}) copy-start(bf16[128,5120]{1,0:T(8,128)(2,1)} %refs_2_.1) | copy-start | bytes 3932164
  5.4 95.2 %copy-start.4 = (bf16[1,96,5120]{2,1,0:T(8,128)(2,1)S(1)}, bf16[1,96,5120]{2,1,0:T(8,128)(2,1)}, u32[]{:S(2)}) copy-start(bf16[1,96,5120]{2,1,0:T(8,128)(2,1)} %param.11) | copy-start | bytes 2949124
  5.4 28.1 %all-to-all-start = ((bf16[16,8,1920]{2,1,0:T(8,128)(2,1)}), bf16[16,8,1920]{2,1,0:T(8,128)(2,1)S(1)}, u32[]{:S(2)}, u32[]{:S(2)}) async-start(bf16[16,8,1920]{2,1,0:T(8,128)(2,1)} %bitcast.1), calls=%async_computation | async-start | bytes 983040 | tf_op jit(solution)/shard_map/all_to_all | solution.py:318
  33.9 17.8 %collective-permute-start.5 = (bf16[48,5120]{1,0:T(8,128)(2,1)S(1)}, bf16[48,5120]{1,0:T(8,128)(2,1)S(1)}, u32[]{:S(2)}, u32[]{:S(2)}) collective-permute-start(bf16[48,5120]{1,0:T(8,128)(2,1)S(1)} %unpack_x.1.refs_0_), channel_id=1, source_target_pairs={{0,128},{16,144},{32,160},{48,176},{64,192},{80,208},{96,224},{112... | collective-permute-start | bytes 1474568 | tf_op jit(solution)/shard_map/ppermute | solution.py:31
  34.0 17.7 %collective-permute-start.4 = (bf16[48,5120]{1,0:T(8,128)(2,1)S(1)}, bf16[48,5120]{1,0:T(8,128)(2,1)S(1)}, u32[]{:S(2)}, u32[]{:S(2)}) collective-permute-start(bf16[48,5120]{1,0:T(8,128)(2,1)S(1)} %unpack_x.1.refs_0_), channel_id=1, source_target_pairs={{0,96},{16,48},{32,0},{48,80},{64,32},{80,112},{96,64},{112,16},{1... | collective-permute-start | bytes 1474568 | tf_op jit(solution)/shard_map/ppermute | solution.py:31
  37.4 14.3 %collective-permute-start.3 = (bf16[48,5120]{1,0:T(8,128)(2,1)S(1)}, bf16[48,5120]{1,0:T(8,128)(2,1)S(1)}, u32[]{:S(2)}, u32[]{:S(2)}) collective-permute-start(bf16[48,5120]{1,0:T(8,128)(2,1)S(1)} %unpack_x.1.refs_0_), channel_id=1, source_target_pairs={{0,32},{16,112},{32,64},{48,16},{64,96},{80,48},{96,0},{112,80},{1... | collective-permute-start | bytes 1474568 | tf_op jit(solution)/shard_map/ppermute | solution.py:31
  37.4 21.5 %all-to-all-start.1 = ((bf16[16,8,2048]{2,1,0:T(8,128)(2,1)}), bf16[16,8,2048]{2,1,0:T(8,128)(2,1)S(1)}, u32[]{:S(2)}, u32[]{:S(2)}) async-start(bf16[16,8,2048]{2,1,0:T(8,128)(2,1)} %bitcast.7), calls=%async_computation.1 | async-start | bytes 1048576 | tf_op jit(solution)/shard_map/all_to_all | solution.py:318
  51.6 11.3 %collective-permute-start.6 = (bf16[48,5120]{1,0:T(8,128)(2,1)S(1)}, bf16[48,5120]{1,0:T(8,128)(2,1)}, u32[]{:S(2)}, u32[]{:S(2)}) collective-permute-start(bf16[48,5120]{1,0:T(8,128)(2,1)S(1)} %collective-permute-done.3.refs_1_), channel_id=1, source_target_pairs={{0,32},{16,112},{32,64},{48,16},{64,96},{80,48},{96,0},{112,80},{1... | collective-permute-start | bytes 1474568 | tf_op jit(solution)/shard_map/ppermute | solution.py:31
  53.1 12.9 %collective-permute-start.8 = (bf16[48,5120]{1,0:T(8,128)(2,1)S(1)}, bf16[48,5120]{1,0:T(8,128)(2,1)}, u32[]{:S(2)}, u32[]{:S(2)}) collective-permute-start(bf16[48,5120]{1,0:T(8,128)(2,1)S(1)} %collective-permute-done.5.refs_4_), channel_id=1, source_target_pairs={{0,96},{16,48},{32,0},{48,80},{64,32},{80,112},{96,64},{112,16},{1... | collective-permute-start | bytes 1474568 | tf_op jit(solution)/shard_map/ppermute | solution.py:31
  54.9 13.3 %collective-permute-start.7 = (bf16[48,5120]{1,0:T(8,128)(2,1)S(1)}, bf16[48,5120]{1,0:T(8,128)(2,1)}, u32[]{:S(2)}, u32[]{:S(2)}) collective-permute-start(bf16[48,5120]{1,0:T(8,128)(2,1)S(1)} %collective-permute-done.5.refs_4_), channel_id=1, source_target_pairs={{0,32},{16,112},{32,64},{48,16},{64,96},{80,48},{96,0},{112,80},{1... | collective-permute-start | bytes 1474568 | tf_op jit(solution)/shard_map/ppermute | solution.py:31
  68.6 10.0 %collective-permute-start.11 = (bf16[48,5248]{1,0:T(8,128)(2,1)S(1)}, bf16[48,5248]{1,0:T(8,128)(2,1)S(1)}, u32[]{:S(2)}, u32[]{:S(2)}) collective-permute-start(bf16[48,5248]{1,0:T(8,128)(2,1)S(1)} %unpack_y.1.refs_0_), channel_id=1, source_target_pairs={{0,128},{16,144},{32,160},{48,176},{64,192},{80,208},{96,224},{112... | collective-permute-start | bytes 1511432 | tf_op jit(solution)/shard_map/ppermute | solution.py:31
  70.7 9.7 %collective-permute-start.10 = (bf16[48,5248]{1,0:T(8,128)(2,1)S(1)}, bf16[48,5248]{1,0:T(8,128)(2,1)S(1)}, u32[]{:S(2)}, u32[]{:S(2)}) collective-permute-start(bf16[48,5248]{1,0:T(8,128)(2,1)S(1)} %unpack_y.1.refs_0_), channel_id=1, source_target_pairs={{0,96},{16,48},{32,0},{48,80},{64,32},{80,112},{96,64},{112,16},{1... | collective-permute-start | bytes 1511432 | tf_op jit(solution)/shard_map/ppermute | solution.py:31
  71.0 10.2 %collective-permute-start.9 = (bf16[48,5248]{1,0:T(8,128)(2,1)S(1)}, bf16[48,5248]{1,0:T(8,128)(2,1)S(1)}, u32[]{:S(2)}, u32[]{:S(2)}) collective-permute-start(bf16[48,5248]{1,0:T(8,128)(2,1)S(1)} %unpack_y.1.refs_0_), channel_id=1, source_target_pairs={{0,32},{16,112},{32,64},{48,16},{64,96},{80,48},{96,0},{112,80},{1... | collective-permute-start | bytes 1511432 | tf_op jit(solution)/shard_map/ppermute | solution.py:31
  78.6 28.6 %copy-start.10 = (bf16[48,5248]{1,0:T(8,128)(2,1)}, bf16[48,5248]{1,0:T(8,128)(2,1)S(1)}, u32[]{:S(2)}) copy-start(bf16[48,5248]{1,0:T(8,128)(2,1)S(1)} %collective-permute-done.11.refs_4_) | copy-start | bytes 1511428
  80.4 26.8 %copy-start.11 = (bf16[48,5248]{1,0:T(8,128)(2,1)}, bf16[48,5248]{1,0:T(8,128)(2,1)S(1)}, u32[]{:S(2)}) copy-start(bf16[48,5248]{1,0:T(8,128)(2,1)S(1)} %collective-permute-done.10.refs_3_) | copy-start | bytes 1511428
  81.2 14.2 %collective-permute-start.14 = (bf16[48,5248]{1,0:T(8,128)(2,1)S(1)}, bf16[48,5248]{1,0:T(8,128)(2,1)S(1)}, u32[]{:S(2)}, u32[]{:S(2)}) collective-permute-start(bf16[48,5248]{1,0:T(8,128)(2,1)S(1)} %collective-permute-done.11.refs_4_), channel_id=1, source_target_pairs={{0,96},{16,48},{32,0},{48,80},{64,32},{80,112},{96,64},{112,16},{1... | collective-permute-start | bytes 1511432 | tf_op jit(solution)/shard_map/ppermute | solution.py:31
  84.1 16.6 %collective-permute-start.16 = (bf16[48,5120]{1,0:T(8,128)(2,1)}, bf16[48,5120]{1,0:T(8,128)(2,1)S(1)}, u32[]{:S(2)}, u32[]{:S(2)}) collective-permute-start(bf16[48,5120]{1,0:T(8,128)(2,1)} %collective-permute-done.8.refs_7_), channel_id=1, source_target_pairs={{0,96},{16,48},{32,0},{48,80},{64,32},{80,112},{96,64},{112,16},{1... | collective-permute-start | bytes 1474568 | tf_op jit(solution)/shard_map/ppermute | solution.py:31
  84.6 22.6 %collective-permute-start.13 = (bf16[48,5248]{1,0:T(8,128)(2,1)S(1)}, bf16[48,5248]{1,0:T(8,128)(2,1)S(1)}, u32[]{:S(2)}, u32[]{:S(2)}) collective-permute-start(bf16[48,5248]{1,0:T(8,128)(2,1)S(1)} %collective-permute-done.9.refs_1_), channel_id=1, source_target_pairs={{0,128},{16,144},{32,160},{48,176},{64,192},{80,208},{96,224},{112... | collective-permute-start | bytes 1511432 | tf_op jit(solution)/shard_map/ppermute | solution.py:31
  85.0 22.3 %collective-permute-start.12 = (bf16[48,5248]{1,0:T(8,128)(2,1)S(1)}, bf16[48,5248]{1,0:T(8,128)(2,1)S(1)}, u32[]{:S(2)}, u32[]{:S(2)}) collective-permute-start(bf16[48,5248]{1,0:T(8,128)(2,1)S(1)} %collective-permute-done.9.refs_1_), channel_id=1, source_target_pairs={{0,32},{16,112},{32,64},{48,16},{64,96},{80,48},{96,0},{112,80},{1... | collective-permute-start | bytes 1511432 | tf_op jit(solution)/shard_map/ppermute | solution.py:31
  95.4 11.8 %copy-start.12 = (bf16[48,5248]{1,0:T(8,128)(2,1)}, bf16[48,5248]{1,0:T(8,128)(2,1)S(1)}, u32[]{:S(2)}) copy-start(bf16[48,5248]{1,0:T(8,128)(2,1)S(1)} %collective-permute-done.14.refs_7_) | copy-start | bytes 1511428
  95.4 11.9 %collective-permute-start.15 = (bf16[48,5248]{1,0:T(8,128)(2,1)S(1)}, bf16[48,5248]{1,0:T(8,128)(2,1)S(1)}, u32[]{:S(2)}, u32[]{:S(2)}) collective-permute-start(bf16[48,5248]{1,0:T(8,128)(2,1)S(1)} %collective-permute-done.14.refs_7_), channel_id=1, source_target_pairs={{0,96},{16,48},{32,0},{48,80},{64,32},{80,112},{96,64},{112,16},{1... | collective-permute-start | bytes 1511432 | tf_op jit(solution)/shard_map/ppermute | solution.py:31
  107.3 0.9 copy-start.13
  107.3 1.1 copy-start.14
  107.3 0.9 copy-start.15
  108.4 13.5 %copy-start.2 = (bf16[384,5120]{1,0:T(8,128)(2,1)S(1)}, bf16[384,5120]{1,0:T(8,128)(2,1)}, u32[]{:S(2)}) copy-start(bf16[384,5120]{1,0:T(8,128)(2,1)} %get-tuple-element.84.x_ref) | copy-start | bytes 11796484
  117.7 9.7 %collective-permute-start.17 = (bf16[48,5248]{1,0:T(8,128)(2,1)S(1)}, bf16[48,5248]{1,0:T(8,128)(2,1)S(1)}, u32[]{:S(2)}, u32[]{:S(2)}) collective-permute-start(bf16[48,5248]{1,0:T(8,128)(2,1)S(1)} %get-tuple-element.76), channel_id=1, source_target_pairs={{0,128},{16,144},{32,160},{48,176},{64,192},{80,208},{96,224},{112... | collective-permute-start | bytes 1511432 | tf_op jit(solution)/shard_map/ppermute | solution.py:31
  118.3 11.6 %collective-permute-start.18 = (bf16[48,5248]{1,0:T(8,128)(2,1)S(1)}, bf16[48,5248]{1,0:T(8,128)(2,1)S(1)}, u32[]{:S(2)}, u32[]{:S(2)}) collective-permute-start(bf16[48,5248]{1,0:T(8,128)(2,1)S(1)} %get-tuple-element.77), channel_id=1, source_target_pairs={{0,96},{16,48},{32,0},{48,80},{64,32},{80,112},{96,64},{112,16},{1... | collective-permute-start | bytes 1511432 | tf_op jit(solution)/shard_map/ppermute | solution.py:31
  121.9 10.2 %collective-permute-start.19 = (bf16[48,5248]{1,0:T(8,128)(2,1)S(1)}, bf16[48,5248]{1,0:T(8,128)(2,1)S(1)}, u32[]{:S(2)}, u32[]{:S(2)}) collective-permute-start(bf16[48,5248]{1,0:T(8,128)(2,1)S(1)} %get-tuple-element.78), channel_id=1, source_target_pairs={{0,32},{16,112},{32,64},{48,16},{64,96},{80,48},{96,0},{112,80},{1... | collective-permute-start | bytes 1511432 | tf_op jit(solution)/shard_map/ppermute | solution.py:31
  121.9 2.1 %copy-start = (bf16[384,5248]{1,0:T(8,128)(2,1)S(1)}, bf16[384,5248]{1,0:T(8,128)(2,1)}, u32[]{:S(2)}) copy-start(bf16[384,5248]{1,0:T(8,128)(2,1)} %get-tuple-element.83.y_ref.prob_ref) | copy-start | bytes 12091396
  132.5 9.0 %collective-permute-start.21 = (bf16[48,5248]{1,0:T(8,128)(2,1)S(1)}, bf16[48,5248]{1,0:T(8,128)(2,1)S(1)}, u32[]{:S(2)}, u32[]{:S(2)}) collective-permute-start(bf16[48,5248]{1,0:T(8,128)(2,1)S(1)} %join.4), channel_id=1, source_target_pairs={{0,128},{16,144},{32,160},{48,176},{64,192},{80,208},{96,224},{112... | collective-permute-start | bytes 1511432 | tf_op jit(solution)/shard_map/ppermute | solution.py:31
  133.2 11.9 %collective-permute-start.20 = (bf16[48,5248]{1,0:T(8,128)(2,1)S(1)}, bf16[48,5248]{1,0:T(8,128)(2,1)S(1)}, u32[]{:S(2)}, u32[]{:S(2)}) collective-permute-start(bf16[48,5248]{1,0:T(8,128)(2,1)S(1)} %join.3), channel_id=1, source_target_pairs={{0,96},{16,48},{32,0},{48,80},{64,32},{80,112},{96,64},{112,16},{1... | collective-permute-start | bytes 1511432 | tf_op jit(solution)/shard_map/ppermute | solution.py:31
  134.8 10.3 %collective-permute-start.22 = (bf16[48,5248]{1,0:T(8,128)(2,1)S(1)}, bf16[48,5248]{1,0:T(8,128)(2,1)S(1)}, u32[]{:S(2)}, u32[]{:S(2)}) collective-permute-start(bf16[48,5248]{1,0:T(8,128)(2,1)S(1)} %get-tuple-element.89), channel_id=1, source_target_pairs={{0,32},{16,112},{32,64},{48,16},{64,96},{80,48},{96,0},{112,80},{1... | collective-permute-start | bytes 1511432 | tf_op jit(solution)/shard_map/ppermute | solution.py:31
  145.4 9.0 %collective-permute-start.23 = (bf16[48,5248]{1,0:T(8,128)(2,1)S(1)}, bf16[48,5248]{1,0:T(8,128)(2,1)S(1)}, u32[]{:S(2)}, u32[]{:S(2)}) collective-permute-start(bf16[48,5248]{1,0:T(8,128)(2,1)S(1)} %join.5), channel_id=1, source_target_pairs={{0,96},{16,48},{32,0},{48,80},{64,32},{80,112},{96,64},{112,16},{1... | collective-permute-start | bytes 1511432 | tf_op jit(solution)/shard_map/ppermute | solution.py:31
  155.7 8.7 %collective-permute-start.24 = (bf16[288,5120]{1,0:T(8,128)(2,1)S(1)}, bf16[288,5120]{1,0:T(8,128)(2,1)}, u32[]{:S(2)}, u32[]{:S(2)}) collective-permute-start(bf16[288,5120]{1,0:T(8,128)(2,1)S(1)} %wgrad_away.1), channel_id=1, source_target_pairs={{0,16},{16,0},{32,48},{48,32},{64,80},{80,64},{96,112},{112,96},{1... | collective-permute-start | bytes 8847368 | tf_op jit(solution)/shard_map/ppermute | solution.py:31
  155.7 27.6 %all-to-all-start.2 = ((bf16[16,8,2048]{2,1,0:T(8,128)(2,1)}), bf16[16,8,2048]{2,1,0:T(8,128)(2,1)}, u32[]{:S(2)}, u32[]{:S(2)}) async-start(bf16[16,8,2048]{2,1,0:T(8,128)(2,1)} %bitcast.9), calls=%async_computation.2 | async-start | bytes 1048576 | tf_op jit(solution)/shard_map/all_to_all | solution.py:318
  164.4 2.1 %copy-start.1 = (bf16[384,5248]{1,0:T(8,128)(2,1)S(1)}, bf16[384,5248]{1,0:T(8,128)(2,1)}, u32[]{:S(2)}) copy-start(bf16[384,5248]{1,0:T(8,128)(2,1)} %get-tuple-element.83.y_ref.prob_ref) | copy-start | bytes 12091396
  166.5 2.1 %copy-start.3 = (bf16[384,5120]{1,0:T(8,128)(2,1)S(1)}, bf16[384,5120]{1,0:T(8,128)(2,1)}, u32[]{:S(2)}) copy-start(bf16[384,5120]{1,0:T(8,128)(2,1)} %get-tuple-element.84.x_ref) | copy-start | bytes 11796484
